TPU v7x, 32 devices: a whole 2x2x4 slice. The times are simulated.
32 devices in a mesh: ctx: 8 (over y, x, core), fsdp: 4 (over z).
Axes of the slice: x: 2, y: 2, z: 4, core: 2. Of those that a mesh axis runs over, the one named last changes fastest.
Arguments:
- tokens: bfloat16 [4, 1024, 2304], P('fsdp', 'ctx'), may hold values from -6 to 6
- cotangent: bfloat16 [4, 1024, 2304], P('fsdp', 'ctx'), may hold values from -6 to 6
- block_order: int32 [16], replicated, may hold values from 0 to 15, each once
- w_qkv: float32 [2304, 4096], P(('ctx', 'fsdp')), may hold values from -0.125 to 0.125
- w_out: float32 [2304, 2048], P(('ctx', 'fsdp')), may hold values from -0.125 to 0.125
- w_gate_up: float32 [2304, 18432], P(('ctx', 'fsdp')), may hold values from -0.125 to 0.125
- w_down: float32 [2304, 9216], P(('ctx', 'fsdp')), may hold values from -0.0625 to 0.0625
- norm_gains: float32 [4, 2304], P(None, ('ctx', 'fsdp')), may hold values from 0.5 to 1.5
- first_qkv: float32 [2304, 4096], P(('ctx', 'fsdp')), may hold values from -20 to 20
- first_out: float32 [2304, 2048], P(('ctx', 'fsdp')), may hold values from -40 to 40
- first_gate_up: float32 [2304, 18432], P(('ctx', 'fsdp')), may hold values from -20 to 20
- first_down: float32 [2304, 9216], P(('ctx', 'fsdp')), may hold values from -40 to 40
- first_gains: float32 [4, 2304], P(None, ('ctx', 'fsdp')), may hold values from -40 to 40
- second_qkv: float32 [2304, 4096], P(('ctx', 'fsdp')), may hold values from 27.0336 to 430.08
- second_out: float32 [2304, 2048], P(('ctx', 'fsdp')), may hold values from 106.496 to 1720.32
- second_gate_up: float32 [2304, 18432], P(('ctx', 'fsdp')), may hold values from 27.0336 to 430.08
- second_down: float32 [2304, 9216], P(('ctx', 'fsdp')), may hold values from 106.496 to 1720.32
- second_gains: float32 [4, 2304], P(None, ('ctx', 'fsdp')), may hold values from 106.496 to 1720.32
Outputs:
- output: bfloat16 [4, 1024, 2304], P('fsdp', 'ctx')
- token_grad: bfloat16 [4, 1024, 2304], P('fsdp', 'ctx')
- moment_qkv: float32 [2304, 4096], P(('ctx', 'fsdp'))
- moment_out: float32 [2304, 2048], P(('ctx', 'fsdp'))
- moment_gate_up: float32 [2304, 18432], P(('ctx', 'fsdp'))
- moment_down: float32 [2304, 9216], P(('ctx', 'fsdp'))
- moment_gains: float32 [4, 2304], P(None, ('ctx', 'fsdp'))
- square_qkv: float32 [2304, 4096], P(('ctx', 'fsdp'))
- square_out: float32 [2304, 2048], P(('ctx', 'fsdp'))
- square_gate_up: float32 [2304, 18432], P(('ctx', 'fsdp'))
- square_down: float32 [2304, 9216], P(('ctx', 'fsdp'))
- square_gains: float32 [4, 2304], P(None, ('ctx', 'fsdp'))
- new_qkv: float32 [2304, 4096], P(('ctx', 'fsdp'))
- new_out: float32 [2304, 2048], P(('ctx', 'fsdp'))
- new_gate_up: float32 [2304, 18432], P(('ctx', 'fsdp'))
- new_down: float32 [2304, 9216], P(('ctx', 'fsdp'))
- new_gains: float32 [4, 2304], P(None, ('ctx', 'fsdp'))
Inputs may be any that keep to these rules, and one draw needn't show every extreme that they name: Slot s of every sequence holds that sequence's block number block_order[s]; each block number appears once.
All inputs are finite; a program needn't handle non-finite values.
Results may differ from a plain program's by a relative error of at most 0.025.
Values may be sent and summed in bfloat16 or wider, within the bound.
No kernel may reach another device: no remote copies, remote signals or barrier semaphores. Data moves between devices by JAX's collectives and lax.ppermute only.
A program may use at most 512 MiB of HBM per device.

v0:
```python
import jax
import jax.numpy as jnp
from jax import lax
from jax.sharding import PartitionSpec as P

HEADS = 8
KV_HEADS = 4
HEAD_DIM = 256
STEP = 5


SOFT_CAP = 3.0
NORM_EPS = 1e-06
BETA_ONE = 0.9
BETA_TWO = 0.95
ADAM_EPS = 1e-08
MATRIX_RATE = 0.02
GAIN_RATE = 0.3
WEIGHT_DECAY = 0.1


def rms_norm(values, gain_row):
    return values * lax.rsqrt(jnp.mean(values * values, -1, keepdims=True) + NORM_EPS) * gain_row


def norm_back(values, gain_row, grad_out):
    _, pull_back = jax.vjp(rms_norm, values, gain_row)
    grad_values, grad_gain = pull_back(grad_out)
    return (grad_values, jnp.sum(grad_gain.reshape(-1, grad_gain.shape[-1]), 0))


def gelu_tanh(values):
    return (
        0.5
        * values
        * (1.0 + jnp.tanh(0.7978845608028654 * (values + 0.044715 * values * values * values)))
    )


def gated_unit(gate_part, up_part):
    return gelu_tanh(gate_part) * up_part


def rotate(values, cos_table, sin_table):
    half_dim = values.shape[-1] // 2
    front_half = values[..., :half_dim]
    back_half = values[..., half_dim:]
    return jnp.concatenate(
        [
            front_half * cos_table - back_half * sin_table,
            back_half * cos_table + front_half * sin_table,
        ],
        -1,
    )


def rope_tables(positions, head_size):
    frequency = 10000.0 ** (-(jnp.arange(head_size // 2, dtype=jnp.float32) * 2.0) / head_size)
    turned = positions.astype(jnp.float32)[:, None] * frequency[None, :]
    return (jnp.cos(turned)[:, None, :], jnp.sin(turned)[:, None, :])


def positions_of(slot_table, row_total, block_size):
    row_ids = jnp.arange(row_total, dtype=jnp.int32)
    slot_ids = row_ids // block_size
    picked = jnp.sum(
        jnp.where(
            slot_ids[:, None] == jnp.arange(slot_table.shape[0], dtype=jnp.int32)[None, :],
            slot_table[None, :],
            0,
        ),
        1,
    )
    return picked * block_size + row_ids % block_size


def adamw(weight, moment_one, moment_two, gradient, rate, decay):
    first_new = BETA_ONE * moment_one + (1.0 - BETA_ONE) * gradient
    second_new = BETA_TWO * moment_two + (1.0 - BETA_TWO) * gradient * gradient
    step_size = (
        first_new
        / (1.0 - BETA_ONE**STEP)
        / (jnp.sqrt(second_new / (1.0 - BETA_TWO**STEP)) + ADAM_EPS)
    )
    return (first_new, second_new, weight - rate * (step_size + decay * weight))


def per_device(
    tokens,
    cotangent,
    block_order,
    w_qkv,
    w_out,
    w_gate_up,
    w_down,
    norm_gains,
    first_qkv,
    first_out,
    first_gate_up,
    first_down,
    first_gains,
    second_qkv,
    second_out,
    second_gate_up,
    second_down,
    second_gains,
):
    row_count = tokens.shape[1]
    block_size = row_count // 2
    ctx_count = lax.axis_size("ctx")
    seq_length = row_count * ctx_count
    head_size = HEAD_DIM
    group_size = HEADS // KV_HEADS
    q_width = HEADS * HEAD_DIM
    kv_width = KV_HEADS * HEAD_DIM
    ff_width = w_down.shape[1]
    scale = HEAD_DIM ** (-0.5)
    key_positions = positions_of(block_order, seq_length, block_size)
    query_positions = lax.dynamic_slice_in_dim(
        key_positions, lax.axis_index("ctx") * row_count, row_count
    )
    cos_table, sin_table = rope_tables(query_positions, head_size)
    allowed = key_positions[None, :] <= query_positions[:, None]
    sent_qkv = w_qkv.astype(jnp.bfloat16)
    sent_out = w_out.astype(jnp.bfloat16)
    sent_gate_up = w_gate_up.astype(jnp.bfloat16)
    sent_down = w_down.astype(jnp.bfloat16)
    full_qkv, full_out, full_gate_up, full_down, full_gains = (
        lax.all_gather(sent_qkv, ("ctx", "fsdp"), axis=0, tiled=True),
        lax.all_gather(sent_out, ("ctx", "fsdp"), axis=0, tiled=True),
        lax.all_gather(sent_gate_up, ("ctx", "fsdp"), axis=0, tiled=True),
        lax.all_gather(sent_down, ("ctx", "fsdp"), axis=0, tiled=True),
        lax.all_gather(norm_gains.astype(jnp.bfloat16), ("ctx", "fsdp"), axis=1, tiled=True),
    )
    gains = full_gains.astype(jnp.float32)
    inputs = tokens[0].astype(jnp.float32)
    normed_one = rms_norm(inputs, gains[0]).astype(jnp.bfloat16)
    projected = jnp.dot(normed_one, full_qkv, preferred_element_type=jnp.float32)
    queries = rotate(
        projected[:, :q_width].reshape(row_count, HEADS, head_size), cos_table, sin_table
    ).astype(jnp.bfloat16)
    keys_local = rotate(
        projected[:, q_width : q_width + kv_width].reshape(row_count, KV_HEADS, head_size),
        cos_table,
        sin_table,
    ).astype(jnp.bfloat16)
    values_local = projected[:, q_width + kv_width :].astype(jnp.bfloat16)
    all_keys, all_values = (
        lax.all_gather(keys_local.reshape(row_count, kv_width), "ctx", axis=0, tiled=True),
        lax.all_gather(values_local, "ctx", axis=0, tiled=True),
    )
    all_keys = all_keys.reshape(seq_length, KV_HEADS, head_size)
    all_values = all_values.reshape(seq_length, KV_HEADS, head_size)
    grouped = queries.reshape(row_count, KV_HEADS, group_size, head_size)

    def capped_scores():
        raw_scores = (
            jnp.einsum("qkgd,pkd->kgqp", grouped, all_keys, preferred_element_type=jnp.float32)
            * scale
        )
        tanh_part = jnp.tanh(raw_scores / SOFT_CAP)
        return (jnp.where(allowed, SOFT_CAP * tanh_part, -1e30), tanh_part)

    capped, tanh_part = capped_scores()
    top_score = jnp.max(capped, -1, keepdims=True)
    exp_scores = jnp.exp(capped - top_score)
    exp_total = jnp.sum(exp_scores, -1, keepdims=True)
    log_total = top_score + jnp.log(exp_total)
    attn_low = (exp_scores / exp_total).astype(jnp.bfloat16)
    attended = jnp.einsum(
        "kgqp,pkd->qkgd", attn_low, all_values, preferred_element_type=jnp.float32
    )
    attended_low = attended.reshape(row_count, q_width).astype(jnp.bfloat16)
    branch = jnp.einsum("th,dh->td", attended_low, full_out, preferred_element_type=jnp.float32)
    hidden_in = inputs + rms_norm(branch, gains[1])
    normed_two = rms_norm(hidden_in, gains[2]).astype(jnp.bfloat16)
    gate_up = jnp.dot(normed_two, full_gate_up, preferred_element_type=jnp.float32)
    gate_part = gate_up[:, :ff_width]
    up_part = gate_up[:, ff_width:]
    activated = gated_unit(gate_part, up_part).astype(jnp.bfloat16)
    lowered = jnp.einsum("tf,df->td", activated, full_down, preferred_element_type=jnp.float32)
    result = hidden_in + rms_norm(lowered, gains[3])
    output = result.astype(jnp.bfloat16)[None]
    back_qkv, back_out, back_gate_up, back_down = (
        lax.all_gather(sent_qkv, ("ctx", "fsdp"), axis=0, tiled=True),
        lax.all_gather(sent_out, ("ctx", "fsdp"), axis=0, tiled=True),
        lax.all_gather(sent_gate_up, ("ctx", "fsdp"), axis=0, tiled=True),
        lax.all_gather(sent_down, ("ctx", "fsdp"), axis=0, tiled=True),
    )
    upstream = cotangent[0].astype(jnp.float32)
    grad_lowered, gain_three = norm_back(lowered, gains[3], upstream)
    grad_lowered_low = grad_lowered.astype(jnp.bfloat16)
    grad_activated = jnp.einsum(
        "td,df->tf", grad_lowered_low, back_down, preferred_element_type=jnp.float32
    )
    _, pull_back = jax.vjp(gated_unit, gate_part, up_part)
    grad_gate, grad_up = pull_back(grad_activated)
    grad_gate_up = jnp.concatenate([grad_gate, grad_up], 1).astype(jnp.bfloat16)
    grad_normed_two = jnp.einsum(
        "tf,df->td", grad_gate_up, back_gate_up, preferred_element_type=jnp.float32
    )
    grad_hidden_part, gain_two = norm_back(hidden_in, gains[2], grad_normed_two)
    grad_hidden = upstream + grad_hidden_part
    grad_branch, gain_one = norm_back(branch, gains[1], grad_hidden)
    grad_branch_low = grad_branch.astype(jnp.bfloat16)
    grad_attended = jnp.dot(grad_branch_low, back_out, preferred_element_type=jnp.float32).astype(
        jnp.bfloat16
    )
    grad_grouped = grad_attended.reshape(row_count, KV_HEADS, group_size, head_size)
    capped, tanh_part = capped_scores()
    attn_probs = jnp.exp(capped - log_total)
    attn_low = attn_probs.astype(jnp.bfloat16)
    grad_probs = jnp.einsum(
        "qkgd,pkd->kgqp", grad_grouped, all_values, preferred_element_type=jnp.float32
    )
    inner_sum = jnp.sum(attn_probs * grad_probs, -1, keepdims=True)
    grad_raw = (attn_probs * (grad_probs - inner_sum) * (1.0 - tanh_part * tanh_part)).astype(
        jnp.bfloat16
    )
    grad_queries = (
        jnp.einsum("kgqp,pkd->qkgd", grad_raw, all_keys, preferred_element_type=jnp.float32) * scale
    )
    key_terms = (
        jnp.einsum("kgqp,qkgd->pkd", grad_raw, grouped, preferred_element_type=jnp.float32) * scale
    )
    value_terms = jnp.einsum(
        "kgqp,qkgd->pkd", attn_low, grad_grouped, preferred_element_type=jnp.float32
    )
    grad_keys, grad_values = (
        lax.psum_scatter(
            key_terms.reshape(seq_length, kv_width).astype(jnp.bfloat16),
            "ctx",
            scatter_dimension=0,
            tiled=True,
        ).astype(jnp.float32),
        lax.psum_scatter(
            value_terms.reshape(seq_length, kv_width).astype(jnp.bfloat16),
            "ctx",
            scatter_dimension=0,
            tiled=True,
        ).astype(jnp.float32),
    )
    queries_back = rotate(
        grad_queries.reshape(row_count, HEADS, head_size), cos_table, -sin_table
    ).reshape(row_count, q_width)
    keys_back = rotate(
        grad_keys.reshape(row_count, KV_HEADS, head_size), cos_table, -sin_table
    ).reshape(row_count, kv_width)
    grad_projected = jnp.concatenate([queries_back, keys_back, grad_values], 1).astype(jnp.bfloat16)
    grad_normed_one = jnp.einsum(
        "tc,dc->td", grad_projected, back_qkv, preferred_element_type=jnp.float32
    )
    grad_input_part, gain_zero = norm_back(inputs, gains[0], grad_normed_one)
    token_grad = (grad_hidden + grad_input_part).astype(jnp.bfloat16)[None]
    model_width = normed_one.shape[1]
    ctx_rows = model_width // ctx_count
    first_column = lax.axis_index("ctx") * ctx_rows

    def row_term(left_piece, right_piece):
        picked = lax.dynamic_slice_in_dim(left_piece, first_column, ctx_rows, 1)
        return jnp.einsum("tr,tc->rc", picked, right_piece, preferred_element_type=jnp.float32)

    grad_qkv, grad_out, grad_gate_up_w, grad_down = (
        lax.psum_scatter(
            row_term(
                lax.all_gather(normed_one, "ctx", axis=0, tiled=True),
                lax.all_gather(grad_projected, "ctx", axis=0, tiled=True),
            ).astype(jnp.bfloat16),
            "fsdp",
            scatter_dimension=0,
            tiled=True,
        ).astype(jnp.float32),
        lax.psum_scatter(
            row_term(
                lax.all_gather(grad_branch_low, "ctx", axis=0, tiled=True),
                lax.all_gather(attended_low, "ctx", axis=0, tiled=True),
            ).astype(jnp.bfloat16),
            "fsdp",
            scatter_dimension=0,
            tiled=True,
        ).astype(jnp.float32),
        lax.psum_scatter(
            row_term(
                lax.all_gather(normed_two, "ctx", axis=0, tiled=True),
                lax.all_gather(grad_gate_up, "ctx", axis=0, tiled=True),
            ).astype(jnp.bfloat16),
            "fsdp",
            scatter_dimension=0,
            tiled=True,
        ).astype(jnp.float32),
        lax.psum_scatter(
            row_term(
                lax.all_gather(grad_lowered_low, "ctx", axis=0, tiled=True),
                lax.all_gather(activated, "ctx", axis=0, tiled=True),
            ).astype(jnp.bfloat16),
            "fsdp",
            scatter_dimension=0,
            tiled=True,
        ).astype(jnp.float32),
    )
    grad_gains = lax.psum_scatter(
        jnp.stack([gain_zero, gain_one, gain_two, gain_three], 0),
        ("ctx", "fsdp"),
        scatter_dimension=1,
        tiled=True,
    )
    moment_qkv, square_qkv, new_qkv = adamw(
        w_qkv, first_qkv, second_qkv, grad_qkv, MATRIX_RATE, WEIGHT_DECAY
    )
    moment_out, square_out, new_out = adamw(
        w_out, first_out, second_out, grad_out, MATRIX_RATE, WEIGHT_DECAY
    )
    moment_gate_up, square_gate_up, new_gate_up = adamw(
        w_gate_up, first_gate_up, second_gate_up, grad_gate_up_w, MATRIX_RATE, WEIGHT_DECAY
    )
    moment_down, square_down, new_down = adamw(
        w_down, first_down, second_down, grad_down, MATRIX_RATE, WEIGHT_DECAY
    )
    moment_gains, square_gains, new_gains = adamw(
        norm_gains, first_gains, second_gains, grad_gains, GAIN_RATE, 0.0
    )
    return (
        output,
        token_grad,
        moment_qkv,
        moment_out,
        moment_gate_up,
        moment_down,
        moment_gains,
        square_qkv,
        square_out,
        square_gate_up,
        square_down,
        square_gains,
        new_qkv,
        new_out,
        new_gate_up,
        new_down,
        new_gains,
    )


def solution(mesh):
    return jax.shard_map(
        per_device,
        mesh=mesh,
        in_specs=(
            P("fsdp", "ctx", None),
            P("fsdp", "ctx", None),
            P(),
            P(("ctx", "fsdp"), None),
            P(("ctx", "fsdp"), None),
            P(("ctx", "fsdp"), None),
            P(("ctx", "fsdp"), None),
            P(None, ("ctx", "fsdp")),
            P(("ctx", "fsdp"), None),
            P(("ctx", "fsdp"), None),
            P(("ctx", "fsdp"), None),
            P(("ctx", "fsdp"), None),
            P(None, ("ctx", "fsdp")),
            P(("ctx", "fsdp"), None),
            P(("ctx", "fsdp"), None),
            P(("ctx", "fsdp"), None),
            P(("ctx", "fsdp"), None),
            P(None, ("ctx", "fsdp")),
        ),
        out_specs=(
            P("fsdp", "ctx", None),
            P("fsdp", "ctx", None),
            P(("ctx", "fsdp"), None),
            P(("ctx", "fsdp"), None),
            P(("ctx", "fsdp"), None),
            P(("ctx", "fsdp"), None),
            P(None, ("ctx", "fsdp")),
            P(("ctx", "fsdp"), None),
            P(("ctx", "fsdp"), None),
            P(("ctx", "fsdp"), None),
            P(("ctx", "fsdp"), None),
            P(None, ("ctx", "fsdp")),
            P(("ctx", "fsdp"), None),
            P(("ctx", "fsdp"), None),
            P(("ctx", "fsdp"), None),
            P(("ctx", "fsdp"), None),
            P(None, ("ctx", "fsdp")),
        ),
        check_vma=False,
    )
```

profile of v0, /device:TPU:0, one launch (start us, length us, event | category | flops | bytes accessed | tf_op | source)
XLA Modules:
  0.0 2100.4 jit_solution(12809113531678536751)
XLA Ops:
  10.1 70.3 %all-gather = bf16[32,72,4]{1,2,0:T(4,128)(2,1)S(1)} all-gather(bf16[1,72,4]{1,2,0:T(4,128)(2,1)S(1)} %convert_bitcast_fusion), channel_id=1, replica_groups=mesh['ctx'=8,'fsdp'=4] {'ctx','fsdp'}, dimensions={0}, use_global_device_ids=true | all-gather | bytes 19008 | tf_op jit(solution)/shard_map/all_gather | solution.py:133
  84.0 54.8 %all-gather.16.cloned.1.call-done = bf16[2304,4096]{1,0:T(8,128)(2,1)} async-done(((bf16[72,4096]{1,0:T(8,128)(2,1)}), bf16[2304,4096]{1,0:T(8,128)(2,1)}) %all-gather.16.cloned.1.call-update) | async-done | bytes 18874384 | tf_op jit(solution)/shard_map/all_gather | solution.py:129
  138.8 7.8 fusion.109
  152.8 4.5 convert_element_type.143
  160.5 13.1 all-gather.18.cloned.1.call-done
  173.6 3.5 reshape.293
  177.2 27.1 %all-gather.20.cloned.1.call-done = bf16[1024,1024]{0,1:T(8,128)(2,1)} async-done(((bf16[128,1024]{0,1:T(8,128)(2,1)}), bf16[1024,1024]{0,1:T(8,128)(2,1)}) %all-gather.20.cloned.1.call-update) | async-done | bytes 2097168 | tf_op jit(solution)/shard_map/all_gather | solution.py:149
  204.3 2.9 fusion.24
  211.2 78.4 %all-gather.22.cloned.1.call-done = bf16[2304,2048]{1,0:T(8,128)(2,1)} async-done(((bf16[72,2048]{1,0:T(8,128)(2,1)}), bf16[2304,2048]{1,0:T(8,128)(2,1)}) %all-gather.22.cloned.1.call-update) | async-done | bytes 9437200 | tf_op jit(solution)/shard_map/all_gather | solution.py:130
  289.6 7.0 multiply_reduce_fusion.6
  298.9 434.3 %all-gather.24.cloned.1.call-done = bf16[2304,18432]{1,0:T(8,128)(2,1)} async-done(((bf16[72,18432]{1,0:T(8,128)(2,1)}), bf16[2304,18432]{1,0:T(8,128)(2,1)}) %all-gather.24.cloned.1.call-update) | async-done | bytes 84934672 | tf_op jit(solution)/shard_map/all_gather | solution.py:131
  733.2 34.3 %fusion.110 = f32[128,18432]{1,0:T(8,128)} fusion(bf16[128,2304]{1,0:T(8,128)(2,1)S(1)} %multiply_convert_fusion.2, bf16[2304,18432]{1,0:T(8,128)(2,1)} %all-gather.24.cloned.1.call-done), kind=kOutput, calls=%fused_computation.193 | convolution fusion | flops 10871635968 | bytes 94961664 | tf_op jit(solution)/shard_map/dot_general | solution.py:177
  767.5 5.0 multiply_convert_fusion.1
  772.5 199.8 %all-gather.26.cloned.1.call-done = bf16[2304,9216]{1,0:T(8,128)(2,1)} async-done(((bf16[72,9216]{1,0:T(8,128)(2,1)}), bf16[2304,9216]{1,0:T(8,128)(2,1)}) %all-gather.26.cloned.1.call-update) | async-done | bytes 42467344 | tf_op jit(solution)/shard_map/all_gather | solution.py:132
  972.3 21.3 %multiply_reduce_fusion.4 = (f32[128]{0:T(128)}, f32[128,2304]{1,0:T(8,128)}) fusion(bf16[128,9216]{1,0:T(8,128)(2,1)S(1)} %multiply_convert_fusion.1, bf16[2304,9216]{1,0:T(8,128)(2,1)} %all-gather.26.cloned.1.call-done), kind=kOutput, calls=%fused_computation.91 | convolution fusion | flops 5436407808 | bytes 46006784 | tf_op jit(solution)/shard_map/tf,df->td/dot_general | solution.py:181
  997.5 2.7 fusion.37
  1000.2 22.1 %fusion.6 = (bf16[128,9216]{1,0:T(8,128)(2,1)}, bf16[128,9216]{1,0:T(8,128)(2,1)}) fusion(f32[128,18432]{1,0:T(8,128)} %fusion.110, bf16[128,2304]{1,0:T(8,128)(2,1)S(1)} %get-tuple-element.51, bf16[2304,9216]{1,0:T(8,128)(2,1)} %all-gather.26.cloned.1.call-done), kind=kOutput, calls=%fused_computation.16 | convolution fusion | flops 5468848128 | bytes 57212928 | tf_op jit(solution)/shard_map/td,df->tf/dot_general | solution.py:193
  1022.4 37.6 %multiply_reduce_fusion = (f32[2304]{0:T(1024)}, f32[128]{0:T(128)S(1)}, f32[128,2304]{1,0:T(8,128)}) fusion(f32[128,2304]{1,0:T(8,128)S(1)} %get-tuple-element.46, f32[128]{0:T(128)S(1)} %copy-done.37, f32[2304]{0:T(1024)S(1)} %copy-done.29, bf16[2304,18432]{1,0:T(8,128)(2,1)} %all-gather.24.cloned.1.call-done, bf16[128,9216]{1,0:T(8,128)(2,1)} %get-tuple-element.50, ...), kind=kOutput, calls=%fused_computation.86 | convolution fusion | flops 10882840576 | bytes 92032000 | tf_op jit(solution)/shard_map/tf,df->td/dot_general | solution.py:199
  1059.9 2.7 multiply_reduce_fusion.1
  1063.8 6.2 convolution_convert_fusion.4
  1072.0 3.8 fusion.21
  1075.8 10.1 fusion.9
  1088.9 4.0 bitcast_convert_fusion
  1093.0 2.6 copy.145
  1097.7 11.2 fusion.29
  1111.9 16.1 reduce-scatter.20.cloned.1.call-done
  1134.7 38.2 %reduce-scatter.22.cloned.1.call-done = bf16[128,1024]{1,0:T(8,128)(2,1)} async-done(((bf16[1024,1024]{1,0:T(8,128)(2,1)}), bf16[128,1024]{1,0:T(8,128)(2,1)}) %reduce-scatter.22.cloned.1.call-update) | async-done | bytes 262160 | tf_op jit(solution)/shard_map/reduce_scatter | solution.py:236
  1176.6 4.2 pad_maximum_fusion
  1180.9 32.0 %all-gather.34.cloned.1.call-done = bf16[1024,2048]{0,1:T(8,128)(2,1)} async-done(((bf16[128,2048]{0,1:T(8,128)(2,1)}), bf16[1024,2048]{0,1:T(8,128)(2,1)}) %all-gather.34.cloned.1.call-update) | async-done | bytes 4194320 | tf_op jit(solution)/shard_map/all_gather | solution.py:276
  1212.8 41.3 %all-gather.32.cloned.1.call-done = bf16[1024,2304]{1,0:T(8,128)(2,1)} async-done(((bf16[128,2304]{1,0:T(8,128)(2,1)}), bf16[1024,2304]{1,0:T(8,128)(2,1)}) %all-gather.32.cloned.1.call-update) | async-done | bytes 4718608 | tf_op jit(solution)/shard_map/all_gather | solution.py:275
  1254.1 5.7 convolution_convert_fusion.3
  1260.0 35.5 %all-gather.28.cloned.1.call-done = bf16[1024,2304]{1,0:T(8,128)(2,1)} async-done(((bf16[128,2304]{1,0:T(8,128)(2,1)}), bf16[1024,2304]{1,0:T(8,128)(2,1)}) %all-gather.28.cloned.1.call-update) | async-done | bytes 4718608 | tf_op jit(solution)/shard_map/all_gather | solution.py:266
  1295.5 56.7 %all-gather.30.cloned.1.call-done = bf16[1024,4096]{1,0:T(8,128)(2,1)} async-done(((bf16[128,4096]{1,0:T(8,128)(2,1)}), bf16[1024,4096]{1,0:T(8,128)(2,1)}) %all-gather.30.cloned.1.call-update) | async-done | bytes 8388624 | tf_op jit(solution)/shard_map/all_gather | solution.py:267
  1352.3 7.9 convolution_convert_fusion.2
  1360.2 33.4 %all-gather.40.cloned.1.call-done = bf16[1024,2304]{1,0:T(8,128)(2,1)} async-done(((bf16[128,2304]{1,0:T(8,128)(2,1)}), bf16[1024,2304]{1,0:T(8,128)(2,1)}) %all-gather.40.cloned.1.call-update) | async-done | bytes 4718608 | tf_op jit(solution)/shard_map/all_gather | solution.py:293
  1393.7 101.1 %all-gather.42.cloned.1.call-done = bf16[1024,9216]{1,0:T(8,128)(2,1)} async-done(((bf16[128,9216]{1,0:T(8,128)(2,1)}), bf16[1024,9216]{1,0:T(8,128)(2,1)}) %all-gather.42.cloned.1.call-update) | async-done | bytes 18874384 | tf_op jit(solution)/shard_map/all_gather | solution.py:294
  1494.7 11.6 convolution_convert_fusion.1
  1506.4 29.6 %all-gather.36.cloned.1.call-done = bf16[1024,2304]{1,0:T(8,128)(2,1)} async-done(((bf16[128,2304]{1,0:T(8,128)(2,1)}), bf16[1024,2304]{1,0:T(8,128)(2,1)}) %all-gather.36.cloned.1.call-update) | async-done | bytes 4718608 | tf_op jit(solution)/shard_map/all_gather | solution.py:284
  1536.0 182.0 %all-gather.38.cloned.1.call-done = bf16[1024,18432]{1,0:T(8,128)(2,1)} async-done(((bf16[128,18432]{1,0:T(8,128)(2,1)}), bf16[1024,18432]{1,0:T(8,128)(2,1)}) %all-gather.38.cloned.1.call-update) | async-done | bytes 37748752 | tf_op jit(solution)/shard_map/all_gather | solution.py:285
  1718.0 21.8 %convolution_convert_fusion = bf16[288,18432]{1,0:T(8,128)(2,1)} fusion(bf16[1024,18432]{1,0:T(8,128)(2,1)} %all-gather.38.cloned.1.call-done, bf16[1024,2304]{1,0:T(8,128)(2,1)} %all-gather.36.cloned.1.call-done, s32[]{:T(128)S(6)} %select_n.43), kind=kOutput, calls=%fused_computation.1 | convolution fusion | flops 10876944384 | bytes 49152004 | tf_op jit(solution)/shard_map/tr,tc->rc/dot_general | solution.py:261
  1741.3 13.9 fusion.34
  1755.3 44.3 %all-reduce = f32[4,2304]{1,0:T(4,128)S(1)} all-reduce(f32[4,2304]{1,0:T(4,128)S(1)} %pad_maximum_fusion.7), channel_id=8, replica_groups=mesh['ctx'=8,'fsdp'=4] {'ctx','fsdp'}, use_global_device_ids=true, to_apply=%region_22.23.clone | all-reduce | flops 9216 | bytes 73728
  1802.8 2.8 multiply_subtract_fusion.3
  1805.7 4.7 multiply_subtract_fusion.2
  1810.4 87.2 %reduce-scatter.18.cloned.1.call-done = bf16[72,9216]{1,0:T(8,128)(2,1)} async-done(((bf16[288,9216]{1,0:T(8,128)(2,1)}), bf16[72,9216]{1,0:T(8,128)(2,1)}) %reduce-scatter.18.cloned.1.call-update) | async-done | bytes 1327120 | tf_op jit(solution)/shard_map/reduce_scatter | solution.py:291
  1897.5 7.6 multiply_subtract_fusion.1
  1905.1 175.5 %reduce-scatter.16.cloned.1.call-done = bf16[72,18432]{1,0:T(8,128)(2,1)} async-done(((bf16[288,18432]{1,0:T(8,128)(2,1)}), bf16[72,18432]{1,0:T(8,128)(2,1)}) %reduce-scatter.16.cloned.1.call-update) | async-done | bytes 2654224 | tf_op jit(solution)/shard_map/reduce_scatter | solution.py:282
  2080.6 12.8 multiply_subtract_fusion
  (206 shorter events, 52.1 us)
Async XLA Ops:
  7.2 131.6 %all-gather.16.cloned.1.call-start = ((), (), s32[]{:S(2)}) async-start(), calls=%async_computation.6 | async-start | bytes 19464192 | tf_op jit(solution)/shard_map/all_gather | solution.py:129
  9.4 164.2 %all-gather.18.cloned.1.call-start = ((), (), s32[]{:S(2)}) async-start(), calls=%async_computation.7 | async-start | bytes 2359296 | tf_op jit(solution)/shard_map/all_gather | solution.py:150
  81.2 217.5 %copy-start.28 = (f32[2304]{0:T(1024)}, f32[2304]{0:T(1024)S(1)}, u32[]{:S(2)}) copy-start(f32[2304]{0:T(1024)S(1)} %get-tuple-element.26) | copy-start | bytes 27652
  82.6 63.9 %copy-start.44 = (f32[128]{0:T(128)}, f32[128]{0:T(128)S(1)}, u32[]{:S(2)}) copy-start(f32[128]{0:T(128)S(1)} %fusion.43) | copy-start | bytes 1540
  82.7 63.9 %copy-start.34 = (f32[128]{0:T(128)}, f32[128]{0:T(128)S(1)}, u32[]{:S(2)}) copy-start(f32[128]{0:T(128)S(1)} %fusion.70) | copy-start | bytes 1540
  84.0 62.7 %copy-start.12 = (bf16[128,2304]{1,0:T(8,128)(2,1)}, bf16[128,2304]{1,0:T(8,128)(2,1)S(1)}, u32[]{:S(2)}) copy-start(bf16[128,2304]{1,0:T(8,128)(2,1)S(1)} %fusion.33) | copy-start | bytes 1769476
  84.0 63.5 %copy-start.43 = (s32[16]{0:T(128)S(1)}, s32[16]{0:T(128)}, u32[]{:S(2)}) copy-start(s32[16]{0:T(128)} %param.20) | copy-start | bytes 196
  147.4 56.9 %all-gather.20.cloned.1.call-start = ((), (), s32[]{:S(2)}) async-start(), calls=%async_computation.8 | async-start | bytes 2359296 | tf_op jit(solution)/shard_map/all_gather | solution.py:149
  148.6 11.6 copy-start.19
  151.9 137.7 %all-gather.22.cloned.1.call-start = ((), (), s32[]{:S(2)}) async-start(), calls=%async_computation.9 | async-start | bytes 9732096 | tf_op jit(solution)/shard_map/all_gather | solution.py:130
  152.8 580.3 %all-gather.24.cloned.1.call-start = ((), (), s32[]{:S(2)}) async-start(), calls=%async_computation.10 | async-start | bytes 87588864 | tf_op jit(solution)/shard_map/all_gather | solution.py:131
  157.4 814.9 %all-gather.26.cloned.1.call-start = ((), (), s32[]{:S(2)}) async-start(), calls=%async_computation.11 | async-start | bytes 43794432 | tf_op jit(solution)/shard_map/all_gather | solution.py:132
  158.7 969.3 %reduce-scatter.20.cloned.1.call-start = ((), (), s32[]{:S(2)}) async-start(), calls=%async_computation.24 | async-start | bytes 2359296
  158.9 49.6 %copy-start.22 = (pred[128,1024]{0,1:T(8,128)(4,1)}, pred[128,1024]{0,1:T(8,128)(4,1)S(1)}, u32[]{:S(2)}) copy-start(pred[128,1024]{0,1:T(8,128)(4,1)S(1)} %broadcast_compare_fusion) | copy-start | bytes 393220
  160.4 46.8 %copy-start.24 = (bf16[128,8,128]{2,0,1:T(8,128)(2,1)}, bf16[128,8,128]{2,0,1:T(8,128)(2,1)S(1)}, u32[]{:S(2)}) copy-start(bf16[128,8,128]{2,0,1:T(8,128)(2,1)S(1)} %copy.110) | copy-start | bytes 786436
  160.5 46.8 %copy-start.25 = (bf16[128,8,128]{2,0,1:T(8,128)(2,1)}, bf16[128,8,128]{2,0,1:T(8,128)(2,1)S(1)}, u32[]{:S(2)}) copy-start(bf16[128,8,128]{2,0,1:T(8,128)(2,1)S(1)} %copy.109) | copy-start | bytes 786436
  177.2 31.4 %copy-start.8 = (bf16[1024,4,256]{2,1,0:T(4,128)(2,1)}, bf16[1024,4,256]{2,1,0:T(4,128)(2,1)S(1)}, u32[]{:S(2)}) copy-start(bf16[1024,4,256]{2,1,0:T(4,128)(2,1)S(1)} %reshape.293) | copy-start | bytes 6291460
  211.2 85.4 %copy-start.18 = (bf16[4,256,2,128]{3,1,2,0:T(8,128)(2,1)}, bf16[4,256,2,128]{3,1,2,0:T(8,128)(2,1)S(1)}, u32[]{:S(2)}) copy-start(bf16[4,256,2,128]{3,1,2,0:T(8,128)(2,1)S(1)} %fusion.30) | copy-start | bytes 1572868
  298.0 435.1 %copy-start.46 = (f32[128]{0:T(128)}, f32[128]{0:T(128)S(1)}, u32[]{:S(2)}) copy-start(f32[128]{0:T(128)S(1)} %get-tuple-element.45) | copy-start | bytes 1540
  298.1 435.1 %copy-start.36 = (f32[128]{0:T(128)}, f32[128]{0:T(128)S(1)}, u32[]{:S(2)}) copy-start(f32[128]{0:T(128)S(1)} %fusion.72) | copy-start | bytes 1540
  298.9 434.3 %copy-start.13 = (bf16[128,2304]{1,0:T(8,128)(2,1)}, bf16[128,2304]{1,0:T(8,128)(2,1)S(1)}, u32[]{:S(2)}) copy-start(bf16[128,2304]{1,0:T(8,128)(2,1)S(1)} %multiply_convert_fusion.2) | copy-start | bytes 1769476
  772.5 221.2 %copy-start = (bf16[128,9216]{1,0:T(8,128)(2,1)}, bf16[128,9216]{1,0:T(8,128)(2,1)S(1)}, u32[]{:S(2)}) copy-start(bf16[128,9216]{1,0:T(8,128)(2,1)S(1)} %multiply_convert_fusion.1) | copy-start | bytes 7077892
  1000.2 22.1 %copy-start.15 = (bf16[128,2304]{1,0:T(8,128)(2,1)}, bf16[128,2304]{1,0:T(8,128)(2,1)S(1)}, u32[]{:S(2)}) copy-start(bf16[128,2304]{1,0:T(8,128)(2,1)S(1)} %get-tuple-element.51) | copy-start | bytes 1769476
  1000.2 22.1 %copy-start.29 = (f32[2304]{0:T(1024)S(1)}, f32[2304]{0:T(1024)}, u32[]{:S(2)}) copy-start(f32[2304]{0:T(1024)} %copy-done.28) | copy-start | bytes 27652
  1000.2 22.1 %copy-start.37 = (f32[128]{0:T(128)S(1)}, f32[128]{0:T(128)}, u32[]{:S(2)}) copy-start(f32[128]{0:T(128)} %copy-done.36) | copy-start | bytes 1540
  1022.3 37.6 %copy-start.47 = (f32[128]{0:T(128)S(1)}, f32[128]{0:T(128)}, u32[]{:S(2)}) copy-start(f32[128]{0:T(128)} %copy-done.46) | copy-start | bytes 1540
  1022.3 37.6 %copy-start.2 = (f32[128,2304]{1,0:T(8,128)S(1)}, f32[128,2304]{1,0:T(8,128)}, u32[]{:S(2)}) copy-start(f32[128,2304]{1,0:T(8,128)} %copy-done.1) | copy-start | bytes 3538948
  1063.8 8.3 copy-start.9
  1088.5 84.4 %reduce-scatter.22.cloned.1.call-start = ((), (), s32[]{:S(2)}) async-start(), calls=%async_computation.25 | async-start | bytes 2359296 | tf_op jit(solution)/shard_map/reduce_scatter | solution.py:236
  1095.6 117.2 %all-gather.34.cloned.1.call-start = ((), (), s32[]{:S(2)}) async-start(), calls=%async_computation.16 | async-start | bytes 4718592 | tf_op jit(solution)/shard_map/all_gather | solution.py:276
  1096.4 157.7 %all-gather.32.cloned.1.call-start = ((), (), s32[]{:S(2)}) async-start(), calls=%async_computation.15 | async-start | bytes 5308416 | tf_op jit(solution)/shard_map/all_gather | solution.py:275
  1097.0 198.6 %all-gather.28.cloned.1.call-start = ((), (), s32[]{:S(2)}) async-start(), calls=%async_computation.12 | async-start | bytes 5308416 | tf_op jit(solution)/shard_map/all_gather | solution.py:266
  1097.7 254.6 %all-gather.30.cloned.1.call-start = ((), (), s32[]{:S(2)}) async-start(), calls=%async_computation.13 | async-start | bytes 9437184 | tf_op jit(solution)/shard_map/all_gather | solution.py:267
  1130.7 45.8 %copy-start.7 = (bf16[128,9216]{1,0:T(8,128)(2,1)S(1)}, bf16[128,9216]{1,0:T(8,128)(2,1)}, u32[]{:S(2)}) copy-start(bf16[128,9216]{1,0:T(8,128)(2,1)} %get-tuple-element.49) | copy-start | bytes 7077892
  1174.6 219.1 %all-gather.40.cloned.1.call-start = ((), (), s32[]{:S(2)}) async-start(), calls=%async_computation.21 | async-start | bytes 5308416 | tf_op jit(solution)/shard_map/all_gather | solution.py:293
  1175.3 319.4 %all-gather.42.cloned.1.call-start = ((), (), s32[]{:S(2)}) async-start(), calls=%async_computation.22 | async-start | bytes 21233664 | tf_op jit(solution)/shard_map/all_gather | solution.py:294
  1175.9 360.1 %all-gather.36.cloned.1.call-start = ((), (), s32[]{:S(2)}) async-start(), calls=%async_computation.18 | async-start | bytes 5308416 | tf_op jit(solution)/shard_map/all_gather | solution.py:284
  1176.5 541.4 %all-gather.38.cloned.1.call-start = ((), (), s32[]{:S(2)}) async-start(), calls=%async_computation.19 | async-start | bytes 42467328 | tf_op jit(solution)/shard_map/all_gather | solution.py:285
  1180.8 622.0 %reduce-scatter.14.cloned.1.call-start = ((), (), s32[]{:S(2)}) async-start(), calls=%async_computation.17 | async-start | bytes 1474560 | tf_op jit(solution)/shard_map/reduce_scatter | solution.py:273
  1259.8 545.9 %reduce-scatter.12.cloned.1.call-start = ((), (), s32[]{:S(2)}) async-start(), calls=%async_computation.14 | async-start | bytes 2949120 | tf_op jit(solution)/shard_map/reduce_scatter | solution.py:264
  1360.2 537.4 %reduce-scatter.18.cloned.1.call-start = ((), (), s32[]{:S(2)}) async-start(), calls=%async_computation.23 | async-start | bytes 6635520 | tf_op jit(solution)/shard_map/reduce_scatter | solution.py:291
  1506.3 574.2 %reduce-scatter.16.cloned.1.call-start = ((), (), s32[]{:S(2)}) async-start(), calls=%async_computation.20 | async-start | bytes 13271040 | tf_op jit(solution)/shard_map/reduce_scatter | solution.py:282
  1741.3 58.3 %copy-start.45 = (f32[128]{0:T(128)S(1)}, f32[128]{0:T(128)}, u32[]{:S(2)}) copy-start(f32[128]{0:T(128)} %copy-done.44) | copy-start | bytes 1540
  1741.3 58.4 %copy-start.33 = (f32[4,72]{1,0:T(4,128)S(1)}, f32[4,72]{1,0:T(4,128)}, u32[]{:S(2)}) copy-start(f32[4,72]{1,0:T(4,128)} %param.25) | copy-start | bytes 3460
  1741.3 58.4 %copy-start.39 = (f32[4,72]{1,0:T(4,128)S(1)}, f32[4,72]{1,0:T(4,128)}, u32[]{:S(2)}) copy-start(f32[4,72]{1,0:T(4,128)} %param.35) | copy-start | bytes 3460
  1741.3 58.4 %copy-start.40 = (f32[4,72]{1,0:T(4,128)S(1)}, f32[4,72]{1,0:T(4,128)}, u32[]{:S(2)}) copy-start(f32[4,72]{1,0:T(4,128)} %param.30) | copy-start | bytes 3460
  1741.3 61.5 %copy-start.17 = (f32[72,2048]{1,0:T(8,128)S(1)}, f32[72,2048]{1,0:T(8,128)}, u32[]{:S(2)}) copy-start(f32[72,2048]{1,0:T(8,128)} %param.22) | copy-start | bytes 1769476
  1805.7 91.9 %copy-start.6 = (f32[72,9216]{1,0:T(8,128)S(1)}, f32[72,9216]{1,0:T(8,128)}, u32[]{:S(2)}) copy-start(f32[72,9216]{1,0:T(8,128)} %param.24) | copy-start | bytes 7962628
  (21 other events, 57.0 us)
Sparse Core Ops, SparseCore 0:
  11.4 127.3 all-gather.15
  147.5 26.0 all-gather.17
  176.1 28.1 all-gather.19
  207.5 82.0 all-gather.21
  292.8 440.2 all-gather.23
  736.4 235.8 all-gather.25
  1088.6 39.3 reduce-scatter.19
  1131.6 41.2 reduce-scatter.21
  1175.4 37.4 all-gather.33
  1215.1 38.9 all-gather.31
  1256.6 38.9 all-gather.27
  1297.8 54.3 all-gather.29
  1354.7 38.9 all-gather.39
  1396.0 98.7 all-gather.41
  1497.0 38.9 all-gather.35
  1538.3 179.5 all-gather.37
  1720.7 29.1 reduce-scatter.13
  1752.6 47.6 reduce-scatter.11
  1803.2 94.3 reduce-scatter.17
  1899.9 180.6 reduce-scatter.15
where the time goes:
time: 2110 us; the launch traced here: 2100 us
  waiting for transfers between devices  1640 us (78%)
  matrix products  231 us (11%)
  blocking collectives  115 us (5%)
  other arithmetic  68.3 us (3%)
  local copies, waits for them, and re-layouts  29.7 us (1%)
    all_gather x1, waiting for transfers between devices, per_device(): lax.all_gather(sent_gate_up, ('ctx', 'fsdp'), axis=0, tiled=True)  434 us
    all_gather x1, waiting for transfers between devices, per_device(): lax.all_gather(sent_down, ('ctx', 'fsdp'), axis=0, tiled=True)  200 us
    all_gather x1, waiting for transfers between devices, per_device(): lax.all_gather(grad_gate_up, 'ctx', axis=0, tiled=True)  182 us
    reduce_scatter x1, waiting for transfers between devices, per_device(): lax.psum_scatter(row_term(lax.all_gather(normed_two, 'ctx', axis=0, tiled...  175 us
    all_gather x1, waiting for transfers between devices, per_device(): lax.all_gather(activated, 'ctx', axis=0, tiled=True)  101 us
    reduce_scatter x1, waiting for transfers between devices, per_device(): lax.psum_scatter(row_term(lax.all_gather(grad_lowered_low, 'ctx', axis=0,...  87.2 us
    all_gather x1, waiting for transfers between devices, per_device(): lax.all_gather(sent_out, ('ctx', 'fsdp'), axis=0, tiled=True)  78.4 us
    all_gather x1, blocking collectives, per_device(): lax.all_gather(norm_gains.astype(jnp.bfloat16), ('ctx', 'fsdp'), axis=1,...  70.3 us
  transfers between devices with their start and end apart: 20, of which 18 were waited for; matrix products, arithmetic and copies ran while one was open for 9% of the time, Pallas kernels for 0%

commit v1 on v0

v1 whole, which is shorter than its diff:
```python
import jax
import jax.numpy as jnp
from jax import lax
from jax.sharding import Mesh
from jax.sharding import PartitionSpec as P

HEADS = 8
KV_HEADS = 4
HEAD_DIM = 256
STEP = 5


SOFT_CAP = 3.0
NORM_EPS = 1e-06
BETA_ONE = 0.9
BETA_TWO = 0.95
ADAM_EPS = 1e-08
MATRIX_RATE = 0.02
GAIN_RATE = 0.3
WEIGHT_DECAY = 0.1

PLANE = ("y", "x")
HEAD_AXES = ("y", "x", "core")
CTX = ("row", "y", "x", "core")
TENSOR = ("core", "fsdp")
EVERY = ("row", "y", "x", "core", "fsdp")


def rms_norm(values, gain_row):
    return values * lax.rsqrt(jnp.mean(values * values, -1, keepdims=True) + NORM_EPS) * gain_row


def norm_back(values, gain_row, grad_out):
    _, pull_back = jax.vjp(rms_norm, values, gain_row)
    grad_values, grad_gain = pull_back(grad_out)
    return (grad_values, jnp.sum(grad_gain.reshape(-1, grad_gain.shape[-1]), 0))


def gelu_tanh(values):
    return (
        0.5
        * values
        * (1.0 + jnp.tanh(0.7978845608028654 * (values + 0.044715 * values * values * values)))
    )


def gated_unit(gate_part, up_part):
    return gelu_tanh(gate_part) * up_part


def rotate(values, cos_table, sin_table):
    half_dim = values.shape[-1] // 2
    front_half = values[..., :half_dim]
    back_half = values[..., half_dim:]
    return jnp.concatenate(
        [
            front_half * cos_table - back_half * sin_table,
            back_half * cos_table + front_half * sin_table,
        ],
        -1,
    )


def rope_tables(positions, head_size):
    frequency = 10000.0 ** (-(jnp.arange(head_size // 2, dtype=jnp.float32) * 2.0) / head_size)
    turned = positions.astype(jnp.float32)[:, None] * frequency[None, :]
    return (jnp.cos(turned), jnp.sin(turned))


def positions_of(slot_table, row_total, block_size):
    row_ids = jnp.arange(row_total, dtype=jnp.int32)
    slot_ids = row_ids // block_size
    picked = jnp.sum(
        jnp.where(
            slot_ids[:, None] == jnp.arange(slot_table.shape[0], dtype=jnp.int32)[None, :],
            slot_table[None, :],
            0,
        ),
        1,
    )
    return picked * block_size + row_ids % block_size


def adamw(weight, moment_one, moment_two, gradient, rate, decay):
    first_new = BETA_ONE * moment_one + (1.0 - BETA_ONE) * gradient
    second_new = BETA_TWO * moment_two + (1.0 - BETA_TWO) * gradient * gradient
    step_size = (
        first_new
        / (1.0 - BETA_ONE**STEP)
        / (jnp.sqrt(second_new / (1.0 - BETA_TWO**STEP)) + ADAM_EPS)
    )
    return (first_new, second_new, weight - rate * (step_size + decay * weight))


def low(values):
    return values.astype(jnp.bfloat16)


def dot(left, right):
    return jnp.dot(left, right, preferred_element_type=jnp.float32)


def dot_t(left, right):
    return lax.dot_general(left, right, (((1,), (1,)), ((), ())), preferred_element_type=jnp.float32)


def t_dot(left, right):
    return lax.dot_general(left, right, (((0,), (0,)), ((), ())), preferred_element_type=jnp.float32)


def gather_rows(piece, axes):
    return lax.all_gather(piece, axes, axis=0, tiled=True)


def scatter_rows(terms, axes):
    return lax.psum_scatter(terms, axes, scatter_dimension=0, tiled=True)


def exchange(piece, axis):
    return lax.ppermute(piece, axis, [(0, 1), (1, 0)])


def columns_out(weight_piece, axes, parts):
    rows = weight_piece.shape[0]
    blocks = weight_piece.reshape(rows, parts, -1)
    return lax.all_to_all(blocks, axes, split_axis=1, concat_axis=0, tiled=True).reshape(
        parts * rows, -1
    )


def columns_back(grad_piece, axes, parts):
    rows = grad_piece.shape[0] // parts
    blocks = grad_piece.reshape(parts, rows, -1)
    return jnp.transpose(
        lax.all_to_all(blocks, axes, split_axis=0, concat_axis=0, tiled=True), (1, 0, 2)
    )


def per_device(
    tokens,
    cotangent,
    block_order,
    w_qkv,
    w_out,
    w_gate_up,
    w_down,
    norm_gains,
    first_qkv,
    first_out,
    first_gate_up,
    first_down,
    first_gains,
    second_qkv,
    second_out,
    second_gate_up,
    second_down,
    second_gains,
):
    row_count = tokens.shape[1]
    block_size = row_count // 2
    row_parts = lax.axis_size("row")
    fsdp_count = lax.axis_size("fsdp")
    core_id = lax.axis_index("core")
    row_id = lax.axis_index("row")
    seq_length = row_count * row_parts * HEADS
    query_rows = row_count * HEADS
    own_rows = w_qkv.shape[0]
    width = tokens.shape[2]
    q_width = HEADS * HEAD_DIM
    kv_width = KV_HEADS * HEAD_DIM
    ff_width = w_down.shape[1]
    tensor_parts = 2 * fsdp_count
    ff_own = ff_width // tensor_parts
    scale = HEAD_DIM ** (-0.5)

    q_cols = low(w_qkv[:, :q_width]).reshape(own_rows, HEADS, HEAD_DIM)
    k_cols = low(w_qkv[:, q_width : q_width + kv_width]).reshape(own_rows, KV_HEADS, 1, HEAD_DIM)
    v_cols = low(w_qkv[:, q_width + kv_width :]).reshape(own_rows, KV_HEADS, 1, HEAD_DIM)
    kv_cols = jnp.concatenate([k_cols, v_cols], 2).reshape(own_rows, HEADS, HEAD_DIM)

    def head_weight(cols):
        mine = columns_out(cols, HEAD_AXES, HEADS).reshape(HEADS, own_rows, -1)
        every = lax.all_gather(mine, "fsdp", axis=1, tiled=False)
        if row_parts > 1:
            every = lax.all_gather(every, "row", axis=0, tiled=True)
        return every.reshape(width, -1)

    head_qkv = head_weight(jnp.concatenate([q_cols, kv_cols], 2))
    head_out = head_weight(low(w_out).reshape(own_rows, HEADS, HEAD_DIM))

    gate_up_cols = jnp.concatenate(
        [
            low(w_gate_up[:, :ff_width]).reshape(own_rows, tensor_parts, ff_own),
            low(w_gate_up[:, ff_width:]).reshape(own_rows, tensor_parts, ff_own),
        ],
        2,
    )
    own_gate_up = gather_rows(
        columns_out(gate_up_cols, TENSOR, tensor_parts), ("row",) + PLANE
    )
    own_down = gather_rows(
        columns_out(low(w_down), TENSOR, tensor_parts), ("row",) + PLANE
    )

    gains = lax.all_gather(low(norm_gains), EVERY, axis=1, tiled=True).astype(jnp.float32)

    key_positions = positions_of(block_order, seq_length, block_size)
    cos_table, sin_table = rope_tables(key_positions, HEAD_DIM)
    first_row = row_id * query_rows

    def query_part(array):
        if row_parts == 1:
            return array
        return lax.dynamic_slice_in_dim(array, first_row, query_rows, 0)

    query_cos, query_sin = query_part(cos_table), query_part(sin_table)
    allowed = key_positions[None, :] <= query_part(key_positions)[:, None]

    inputs = tokens[0].astype(jnp.float32)
    seq_tokens = gather_rows(tokens[0], CTX)
    normed_one = low(rms_norm(seq_tokens.astype(jnp.float32), gains[0]))
    normed_query = query_part(normed_one)
    queries = low(rotate(dot(normed_query, head_qkv[:, :HEAD_DIM]), query_cos, query_sin))
    kv_raw = dot(normed_one, head_qkv[:, HEAD_DIM:])
    kv_mine = low(jnp.where(core_id == 0, rotate(kv_raw, cos_table, sin_table), kv_raw))
    kv_other = exchange(kv_mine, "core")
    keys = jnp.where(core_id == 0, kv_mine, kv_other)
    values = jnp.where(core_id == 0, kv_other, kv_mine)
    tanh_part = jnp.tanh(dot_t(queries, keys) * (scale / SOFT_CAP))
    capped = jnp.where(allowed, SOFT_CAP * tanh_part, -1e30)
    top_score = jnp.max(capped, -1, keepdims=True)
    exp_scores = jnp.exp(capped - top_score)
    exp_total = jnp.sum(exp_scores, -1, keepdims=True)
    probs = exp_scores / exp_total
    probs_low = low(probs)
    attended = low(dot(probs_low, values))
    branch = scatter_rows(low(dot_t(attended, head_out)), HEAD_AXES).astype(jnp.float32)
    hidden_in = inputs + rms_norm(branch, gains[1])

    normed_two = gather_rows(low(rms_norm(hidden_in, gains[2])), TENSOR)
    gate_up = dot(normed_two, own_gate_up)
    gate_part, up_part = gate_up[:, :ff_own], gate_up[:, ff_own:]
    activated = low(gated_unit(gate_part, up_part))
    lowered = scatter_rows(low(dot_t(activated, own_down)), TENSOR).astype(jnp.float32)
    output = low(hidden_in + rms_norm(lowered, gains[3]))[None]

    upstream = cotangent[0].astype(jnp.float32)
    grad_lowered, gain_three = norm_back(lowered, gains[3], upstream)
    grad_lowered = gather_rows(low(grad_lowered), TENSOR)
    grad_activated = dot(grad_lowered, own_down)
    _, pull_back = jax.vjp(gated_unit, gate_part, up_part)
    grad_gate_up = low(jnp.concatenate(pull_back(grad_activated), 1))
    grad_normed_two = scatter_rows(low(dot_t(grad_gate_up, own_gate_up)), TENSOR).astype(
        jnp.float32
    )
    term_gate_up = low(t_dot(normed_two, grad_gate_up))
    term_down = low(t_dot(grad_lowered, activated))

    def ff_grad(term):
        return columns_back(
            scatter_rows(term, ("row",) + PLANE), TENSOR, tensor_parts
        ).astype(jnp.float32)

    sum_gate_up = ff_grad(term_gate_up)
    grad_gate_up_w = jnp.concatenate(
        [
            sum_gate_up[:, :, :ff_own].reshape(own_rows, ff_width),
            sum_gate_up[:, :, ff_own:].reshape(own_rows, ff_width),
        ],
        1,
    )
    grad_down = ff_grad(term_down).reshape(own_rows, ff_width)

    grad_hidden_part, gain_two = norm_back(hidden_in, gains[2], grad_normed_two)
    grad_hidden = upstream + grad_hidden_part
    grad_branch, gain_one = norm_back(branch, gains[1], grad_hidden)
    grad_branch = gather_rows(low(grad_branch), HEAD_AXES)

    grad_attended = low(dot(grad_branch, head_out))
    grad_probs = dot_t(grad_attended, values)
    inner_sum = jnp.sum(probs * grad_probs, -1, keepdims=True)
    grad_raw = low(probs * (grad_probs - inner_sum) * (1.0 - tanh_part * tanh_part))
    grad_queries = dot(grad_raw, keys) * scale
    key_terms = t_dot(grad_raw, queries) * scale
    value_terms = t_dot(probs_low, grad_attended)
    kv_terms = jnp.where(core_id == 0, key_terms, value_terms) + exchange(
        jnp.where(core_id == 0, value_terms, key_terms), "core"
    )
    if row_parts > 1:
        kv_terms = scatter_rows(kv_terms, "row")
    kv_back = jnp.where(core_id == 0, rotate(kv_terms, query_cos, -query_sin), kv_terms)
    grad_projected = low(
        jnp.concatenate([rotate(grad_queries, query_cos, -query_sin), kv_back], 1)
    )
    grad_normed_one = scatter_rows(low(dot_t(grad_projected, head_qkv)), HEAD_AXES).astype(
        jnp.float32
    )
    grad_input_part, gain_zero = norm_back(inputs, gains[0], grad_normed_one)
    token_grad = low(grad_hidden + grad_input_part)[None]

    def head_grad(term):
        term = low(term)
        if row_parts > 1:
            term = scatter_rows(term, "row")
        by_owner = jnp.transpose(
            term.reshape(HEADS, fsdp_count, own_rows, -1), (1, 0, 2, 3)
        ).reshape(term.shape)
        return columns_back(scatter_rows(by_owner, "fsdp"), HEAD_AXES, HEADS).astype(jnp.float32)

    grad_out = head_grad(t_dot(grad_branch, attended)).reshape(own_rows, q_width)
    sum_qkv = head_grad(t_dot(normed_query, grad_projected))
    kv_sum = sum_qkv[:, :, HEAD_DIM:].reshape(own_rows, KV_HEADS, 2, HEAD_DIM)
    grad_qkv = jnp.concatenate(
        [
            sum_qkv[:, :, :HEAD_DIM].reshape(own_rows, q_width),
            kv_sum[:, :, 0].reshape(own_rows, kv_width),
            kv_sum[:, :, 1].reshape(own_rows, kv_width),
        ],
        1,
    )
    gain_terms = jnp.stack([gain_zero, gain_one, gain_two, gain_three], 0)
    grad_gains = jnp.sum(
        lax.all_to_all(
            gain_terms.reshape(4, -1, own_rows), EVERY, split_axis=1, concat_axis=1, tiled=True
        ),
        1,
    )
    moment_qkv, square_qkv, new_qkv = adamw(
        w_qkv, first_qkv, second_qkv, grad_qkv, MATRIX_RATE, WEIGHT_DECAY
    )
    moment_out, square_out, new_out = adamw(
        w_out, first_out, second_out, grad_out, MATRIX_RATE, WEIGHT_DECAY
    )
    moment_gate_up, square_gate_up, new_gate_up = adamw(
        w_gate_up, first_gate_up, second_gate_up, grad_gate_up_w, MATRIX_RATE, WEIGHT_DECAY
    )
    moment_down, square_down, new_down = adamw(
        w_down, first_down, second_down, grad_down, MATRIX_RATE, WEIGHT_DECAY
    )
    moment_gains, square_gains, new_gains = adamw(
        norm_gains, first_gains, second_gains, grad_gains, GAIN_RATE, 0.0
    )
    return (
        output,
        token_grad,
        moment_qkv,
        moment_out,
        moment_gate_up,
        moment_down,
        moment_gains,
        square_qkv,
        square_out,
        square_gate_up,
        square_down,
        square_gains,
        new_qkv,
        new_out,
        new_gate_up,
        new_down,
        new_gains,
    )


def solution(mesh):
    ctx_count, fsdp_count = mesh.shape["ctx"], mesh.shape["fsdp"]
    fine_mesh = Mesh(mesh.devices.reshape(ctx_count // HEADS, 2, 2, 2, fsdp_count), EVERY)
    rows = P("fsdp", CTX, None)
    weight = P(EVERY, None)
    gain = P(None, EVERY)
    weights = (weight, weight, weight, weight, gain)
    return jax.shard_map(
        per_device,
        mesh=fine_mesh,
        in_specs=(rows, rows, P()) + weights * 3,
        out_specs=(rows, rows) + weights * 3,
        check_vma=False,
    )
```

time: 2110 us -> 1160 us (0.55)
  waiting for transfers between devices: 1640 us -> 693 us
  matrix products: 231 us -> 116 us
  blocking collectives: 115 us -> 194 us
    all_gather x14 -> x8, waiting for transfers between devices: 1320 us -> 274 us  [the longest x6 274 us: gather_rows(): return lax.all_gather(piece, axes, axis=0, tiled=True)]
    all_to_all x0 -> x4, blocking collectives: none -> 126 us  [columns_out(): lax.all_to_all(blocks, axes, split_axis=1, concat_axis=0, tiled=True)]
    dot_general x18 -> x19, matrix products: 231 us -> 116 us  [the longest x7 42.8 us: dot(): return jnp.dot(left, right, preferred_element_type=jnp.float32)]
    reduce_scatter x5 -> x8, waiting for transfers between devices: 301 us -> 370 us  [scatter_rows(): return lax.psum_scatter(terms, axes, scatter_dimension=0, tiled=True)]
    all_to_all x0 -> x5, waiting for transfers between devices: none -> 47.6 us  [the longest x4 47.6 us: columns_back(): lax.all_to_all(blocks, axes, split_axis=0, concat_axis=0, tiled=True)]
    unnamed x1 -> x0, blocking collectives: 44.3 us -> none
  transfers between devices with their start and end apart: 20 -> 23, of which waited for: 18 -> 14; matrix products, arithmetic and copies ran while one was open for 9% -> 12% of each run, Pallas kernels for 0% -> 0%
where the time goes in v1:
time: 1160 us; the launch traced here: 1150 us
  waiting for transfers between devices  693 us (60%)
  blocking collectives  194 us (17%)
  matrix products  116 us (10%)
  other arithmetic  73.5 us (6%)
  local copies, waits for them, and re-layouts  33.2 us (3%)
  starting transfers between devices  22.2 us (2%)
  between operations  17.5 us (2%)
    reduce_scatter x8, waiting for transfers between devices, scatter_rows(): return lax.psum_scatter(terms, axes, scatter_dimension=0, tiled=True)  370 us
    all_gather x6, waiting for transfers between devices, gather_rows(): return lax.all_gather(piece, axes, axis=0, tiled=True)  274 us
    all_to_all x4, blocking collectives, columns_out(): lax.all_to_all(blocks, axes, split_axis=1, concat_axis=0, tiled=True)  126 us
    all_gather x1, blocking collectives, per_device(): lax.all_gather(low(norm_gains), EVERY, axis=1, tiled=True)  67.5 us
    all_to_all x4, waiting for transfers between devices, columns_back(): lax.all_to_all(blocks, axes, split_axis=0, concat_axis=0, tiled=True)  47.6 us
    dot_general x7, matrix products, dot(): return jnp.dot(left, right, preferred_element_type=jnp.float32)  42.8 us
    dot_general x6, matrix products, dot_t(): lax.dot_general(left, right, (((1,), (1,)), ((), ())), preferred_element_...  37.9 us
    dot_general x6, matrix products, t_dot(): lax.dot_general(left, right, (((0,), (0,)), ((), ())), preferred_element_...  35.8 us
  transfers between devices with their start and end apart: 23, of which 14 were waited for; matrix products, arithmetic and copies ran while one was open for 12% of the time, Pallas kernels for 0%

profile of v1, /device:TPU:0, one launch (start us, length us, event | category | flops | bytes accessed | tf_op | source)
XLA Modules:
  0.0 1149.7 jit_solution(7203646613354423466)
XLA Ops:
  9.3 12.3 %all_to_all.85 = bf16[72,8,256]{2,0,1:T(8,128)(2,1)S(1)} all-to-all(bf16[72,8,256]{2,0,1:T(8,128)(2,1)S(1)} %bitcast.177), channel_id=1, replica_groups=mesh['row'=1,'y'=2,'x'=2,'core'=2,'fsdp'=4] {'y','x','core'}, dimensions={1} | all-to-all | bytes 589824 | tf_op jit(solution)/shard_map/all_to_all | solution.py:126
  23.3 12.8 %all_to_all.86 = bf16[72,8,512]{2,0,1:T(8,128)(2,1)S(1)} all-to-all(bf16[72,8,512]{2,0,1:T(8,128)(2,1)S(1)} %copy.103), channel_id=1, replica_groups=mesh['row'=1,'y'=2,'x'=2,'core'=2,'fsdp'=4] {'y','x','core'}, dimensions={1} | all-to-all | bytes 1179648 | tf_op jit(solution)/shard_map/all_to_all | solution.py:126
  38.0 67.5 %all-gather.3 = bf16[32,72,4]{1,2,0:T(4,128)(2,1)S(1)} all-gather(bf16[1,72,4]{1,2,0:T(4,128)(2,1)S(1)} %convert_bitcast_fusion.4), channel_id=1, replica_groups=mesh['row'=1,'y'=2,'x'=2,'core'=2,'fsdp'=4] {'row','y','x','core','fsdp'}, dimensions={0}, use_global_device_ids=true | all-gather | bytes 19008 | tf_op jit(solution)/shard_map/all_gather | solution.py:205
  105.7 2.8 convert.40
  108.8 2.5 copy.108
  111.3 4.1 copy.105
  115.3 28.7 %all-gather.23.cloned.1.call-done = bf16[1,1024,2304]{2,1,0:T(8,128)(2,1)} async-done(((bf16[1,128,2304]{2,1,0:T(8,128)(2,1)}), bf16[1,1024,2304]{2,1,0:T(8,128)(2,1)}) %all-gather.23.cloned.1.call-update) | async-done | bytes 4718608 | tf_op jit(solution)/shard_map/all_gather | solution.py:112
  144.1 3.5 fusion
  147.8 3.0 fusion.38
  150.9 2.5 fusion.77
  163.8 3.6 convolution_convert_fusion.5
  168.7 65.5 %all_to_all.87 = bf16[72,8,2304]{2,0,1:T(8,128)(2,1)} all-to-all(bf16[72,8,2304]{2,0,1:T(8,128)(2,1)S(1)} %copy.109), channel_id=1, replica_groups=mesh['row'=1,'y'=2,'x'=2,'core'=2,'fsdp'=4] {'core','fsdp'}, dimensions={1} | all-to-all | bytes 5308416 | tf_op jit(solution)/shard_map/all_to_all | solution.py:126
  237.8 2.4 multiply_convert_fusion.3
  240.5 35.7 %all_to_all.88 = bf16[72,8,1152]{2,0,1:T(8,128)(2,1)} all-to-all(bf16[72,8,1152]{2,0,1:T(8,128)(2,1)S(1)} %bitcast.151), channel_id=1, replica_groups=mesh['row'=1,'y'=2,'x'=2,'core'=2,'fsdp'=4] {'core','fsdp'}, dimensions={1} | all-to-all | bytes 2654208 | tf_op jit(solution)/shard_map/all_to_all | solution.py:126
  276.2 62.1 %all-gather.15.cloned.1.call-done = bf16[2304,2304]{1,0:T(8,128)(2,1)} async-done(((bf16[576,2304]{1,0:T(8,128)(2,1)}), bf16[2304,2304]{1,0:T(8,128)(2,1)}) %all-gather.15.cloned.1.call-update) | async-done | bytes 10616848 | tf_op jit(solution)/shard_map/all_gather | solution.py:112
  338.3 53.4 %all-gather.13.cloned.1.call-done = bf16[1024,2304]{1,0:T(8,128)(2,1)} async-done(((bf16[128,2304]{1,0:T(8,128)(2,1)}), bf16[1024,2304]{1,0:T(8,128)(2,1)}) %all-gather.13.cloned.1.call-update) | async-done | bytes 4718608 | tf_op jit(solution)/shard_map/all_gather | solution.py:112
  391.7 15.2 %fusion.116 = f32[1024,2304]{1,0:T(8,128)S(1)} fusion(bf16[1024,2304]{1,0:T(8,128)(2,1)} %all-gather.13.cloned.1.call-done, bf16[2304,2304]{1,0:T(8,128)(2,1)} %all-gather.15.cloned.1.call-done), kind=kOutput, calls=%fused_computation.224 | convolution fusion | flops 10871635968 | bytes 24772608 | tf_op jit(solution)/shard_map/dot_general | solution.py:100
  406.9 3.5 copy-done.9
  412.1 42.0 %all-gather.17.cloned.1.call-done = bf16[2304,1152]{1,0:T(8,128)(2,1)} async-done(((bf16[576,1152]{1,0:T(8,128)(2,1)}), bf16[2304,1152]{1,0:T(8,128)(2,1)}) %all-gather.17.cloned.1.call-update) | async-done | bytes 5308432 | tf_op jit(solution)/shard_map/all_gather | solution.py:112
  454.0 10.5 convolution_convert_fusion.4
  464.6 98.1 %reduce-scatter.11.cloned.1.call-done = bf16[128,2304]{1,0:T(8,128)(2,1)} async-done(((bf16[1024,2304]{1,0:T(8,128)(2,1)}), bf16[128,2304]{1,0:T(8,128)(2,1)}) %reduce-scatter.11.cloned.1.call-update) | async-done | bytes 589840 | tf_op jit(solution)/shard_map/reduce_scatter | solution.py:116
  568.5 51.2 %all-gather.19.cloned.1.call-done = bf16[1024,2304]{1,0:T(8,128)(2,1)} async-done(((bf16[128,2304]{1,0:T(8,128)(2,1)}), bf16[1024,2304]{1,0:T(8,128)(2,1)}) %all-gather.19.cloned.1.call-update) | async-done | bytes 4718608 | tf_op jit(solution)/shard_map/all_gather | solution.py:112
  619.8 16.3 %fusion.7 = (bf16[1024,1152]{1,0:T(8,128)(2,1)S(1)}, bf16[1024,1152]{1,0:T(8,128)(2,1)S(1)}) fusion(f32[1024,2304]{1,0:T(8,128)} %copy-done.9, bf16[1024,2304]{1,0:T(8,128)(2,1)} %all-gather.19.cloned.1.call-done, bf16[2304,1152]{1,0:T(8,128)(2,1)} %all-gather.17.cloned.1.call-done), kind=kOutput, calls=%fused_computation.23 | convolution fusion | flops 5468848128 | bytes 24182784 | tf_op jit(solution)/shard_map/dot_general | solution.py:100
  638.2 14.7 %convolution_convert_fusion.3 = bf16[1024,2304]{1,0:T(8,128)(2,1)} fusion(bf16[2304,2304]{1,0:T(8,128)(2,1)} %all-gather.15.cloned.1.call-done, bf16[1024,1152]{1,0:T(8,128)(2,1)S(1)} %get-tuple-element.47, bf16[1024,1152]{1,0:T(8,128)(2,1)S(1)} %get-tuple-element.46), kind=kOutput, calls=%fused_computation.13 | convolution fusion | flops 10883432448 | bytes 20054016 | tf_op jit(solution)/shard_map/dot_general | solution.py:104
  653.1 96.7 %reduce-scatter.13.cloned.1.call-done = bf16[128,2304]{1,0:T(8,128)(2,1)} async-done(((bf16[1024,2304]{1,0:T(8,128)(2,1)}), bf16[128,2304]{1,0:T(8,128)(2,1)}) %reduce-scatter.13.cloned.1.call-update) | async-done | bytes 589840 | tf_op jit(solution)/shard_map/reduce_scatter | solution.py:116
  752.1 3.7 fusion.22
  758.9 9.7 convolution_convert_fusion.1
  768.9 37.0 %all-gather.21.cloned.1.call-done = bf16[1024,2304]{1,0:T(8,128)(2,1)} async-done(((bf16[128,2304]{1,0:T(8,128)(2,1)}), bf16[1024,2304]{1,0:T(8,128)(2,1)}) %all-gather.21.cloned.1.call-update) | async-done | bytes 4718608 | tf_op jit(solution)/shard_map/all_gather | solution.py:112
  805.9 3.9 convolution_convert_fusion.8
  811.7 2.5 multiply_convert_fusion.2
  815.1 3.4 broadcast_select_fusion
  829.2 3.3 convolution_convert_fusion.6
  834.2 17.1 %convolution_convert_fusion = bf16[2304,2304]{1,0:T(8,128)(2,1)} fusion(bf16[1024,2304]{1,0:T(8,128)(2,1)} %all-gather.13.cloned.1.call-done, bf16[1024,1152]{1,0:T(8,128)(2,1)} %copy-done.68, bf16[1024,1152]{1,0:T(8,128)(2,1)} %copy-done.67), kind=kOutput, calls=%fused_computation | convolution fusion | flops 10886381568 | bytes 20054016 | tf_op jit(solution)/shard_map/dot_general | solution.py:108
  851.4 5.3 all-to-all-start.7
  856.9 6.0 convolution_convert_fusion.2
  863.0 39.0 %all-to-all-done.7 = bf16[8,72,1152]{2,1,0:T(8,128)(2,1)S(1)} async-done(((bf16[8,72,1152]{2,1,0:T(8,128)(2,1)}), bf16[8,72,1152]{2,1,0:T(8,128)(2,1)S(1)}, u32[]{:S(2)}, u32[]{:S(2)}) %all-to-all-start.7) | async-done | bytes 1327136 | tf_op jit(solution)/shard_map/all_to_all | solution.py:135
  902.0 3.6 all-to-all-start.5
  907.8 5.2 all-to-all-done.5
  912.9 35.6 %reduce-scatter.17.cloned.1.call-done = bf16[576,512]{1,0:T(8,128)(2,1)} async-done(((bf16[2304,512]{1,0:T(8,128)(2,1)}), bf16[576,512]{1,0:T(8,128)(2,1)}) %reduce-scatter.17.cloned.1.call-update) | async-done | bytes 589840 | tf_op jit(solution)/shard_map/reduce_scatter | solution.py:116
  948.5 3.6 all-to-all-start.4
  954.0 102.3 %reduce-scatter.21.cloned.1.call-done = bf16[576,2304]{1,0:T(8,128)(2,1)} async-done(((bf16[2304,2304]{1,0:T(8,128)(2,1)}), bf16[576,2304]{1,0:T(8,128)(2,1)}) %reduce-scatter.21.cloned.1.call-update) | async-done | bytes 2654224 | tf_op jit(solution)/shard_map/reduce_scatter | solution.py:116
  1057.1 4.9 all-to-all-start.6
  1062.0 8.2 multiply_subtract_fusion.1
  1074.6 2.4 multiply_subtract_fusion.2
  1076.9 37.4 %reduce-scatter.15.cloned.1.call-done = bf16[128,2304]{1,0:T(8,128)(2,1)} async-done(((bf16[1024,2304]{1,0:T(8,128)(2,1)}), bf16[128,2304]{1,0:T(8,128)(2,1)}) %reduce-scatter.15.cloned.1.call-update) | async-done | bytes 589840 | tf_op jit(solution)/shard_map/reduce_scatter | solution.py:116
  1119.2 3.4 all-to-all-done.6
  1122.6 2.9 all-to-all-start.8
  1132.3 8.9 multiply_subtract_fusion
  (294 shorter events, 72.6 us)
Async XLA Ops:
  8.0 14.4 %copy-start.14 = (f32[72,4096]{1,0:T(8,128)S(1)}, f32[72,4096]{1,0:T(8,128)}, u32[]{:S(2)}) copy-start(f32[72,4096]{1,0:T(8,128)} %param.21) | copy-start | bytes 3538948
  8.0 100.7 %all-gather.27.cloned.1.call-start = ((), (), s32[]{:S(2)}) async-start(), calls=%async_computation.32 | async-start | bytes 1474560 | tf_op jit(solution)/shard_map/all_gather | solution.py:183
  22.3 88.9 %all-gather.25.cloned.1.call-start = ((), (), s32[]{:S(2)}) async-start(), calls=%async_computation.31 | async-start | bytes 2949120 | tf_op jit(solution)/shard_map/all_gather | solution.py:183
  23.2 14.8 %copy-start.56 = (f32[4,72]{1,0:T(4,128)S(1)}, f32[4,72]{1,0:T(4,128)}, u32[]{:S(2)}) copy-start(f32[4,72]{1,0:T(4,128)} %param.25) | copy-start | bytes 3460
  37.2 106.9 %all-gather.23.cloned.1.call-start = ((), (), s32[]{:S(2)}) async-start(), calls=%async_computation.30 | async-start | bytes 5308416 | tf_op jit(solution)/shard_map/all_gather | solution.py:112
  37.9 196.4 %reduce-scatter.9.cloned.1.call-start = ((), (), s32[]{:S(2)}) async-start(), calls=%async_computation.17 | async-start | bytes 5308416 | tf_op jit(solution)/shard_map/reduce_scatter | solution.py:116
  108.5 47.3 %copy-start.54 = (f32[128]{0:T(128)}, f32[128]{0:T(128)S(1)}, u32[]{:S(2)}) copy-start(f32[128]{0:T(128)S(1)} %multiply_power_fusion) | copy-start | bytes 1540
  108.7 45.2 %copy-start.39 = (f32[2304]{0:T(1024)}, f32[2304]{0:T(1024)S(1)}, u32[]{:S(2)}) copy-start(f32[2304]{0:T(1024)S(1)} %get-tuple-element.29) | copy-start | bytes 27652
  108.7 52.3 %copy-start.41 = (s32[1024]{0:T(1024)}, s32[1024]{0:T(1024)S(1)}, u32[]{:S(2)}) copy-start(s32[1024]{0:T(1024)S(1)} %get-tuple-element.67) | copy-start | bytes 12292
  153.6 4.5 collective-permute-start
  167.5 170.9 %all-gather.15.cloned.1.call-start = ((), (), s32[]{:S(2)}) async-start(), calls=%async_computation.19 | async-start | bytes 13271040 | tf_op jit(solution)/shard_map/all_gather | solution.py:112
  234.3 157.4 %all-gather.13.cloned.1.call-start = ((), (), s32[]{:S(2)}) async-start(), calls=%async_computation.18 | async-start | bytes 5308416 | tf_op jit(solution)/shard_map/all_gather | solution.py:112
  235.8 516.4 %copy-start.53 = (f32[128]{0:T(128)}, f32[128]{0:T(128)S(1)}, u32[]{:S(2)}) copy-start(f32[128]{0:T(128)S(1)} %fusion.90) | copy-start | bytes 1540
  240.2 213.9 %all-gather.17.cloned.1.call-start = ((), (), s32[]{:S(2)}) async-start(), calls=%async_computation.20 | async-start | bytes 6635520 | tf_op jit(solution)/shard_map/all_gather | solution.py:112
  276.2 286.5 %reduce-scatter.11.cloned.1.call-start = ((), (), s32[]{:S(2)}) async-start(), calls=%async_computation.21 | async-start | bytes 5308416 | tf_op jit(solution)/shard_map/reduce_scatter | solution.py:116
  412.1 52.4 %copy-start.20 = (bf16[1024,1152]{1,0:T(8,128)(2,1)}, bf16[1024,1152]{1,0:T(8,128)(2,1)S(1)}, u32[]{:S(2)}) copy-start(bf16[1024,1152]{1,0:T(8,128)(2,1)S(1)} %multiply_convert_fusion.1) | copy-start | bytes 7077892
  464.5 99.4 %copy-start.10 = (bf16[1,128,2304]{2,1,0:T(8,128)(2,1)S(1)}, bf16[1,128,2304]{2,1,0:T(8,128)(2,1)}, u32[]{:S(2)}) copy-start(bf16[1,128,2304]{2,1,0:T(8,128)(2,1)} %param.19) | copy-start | bytes 1769476
  464.5 155.2 %all-gather.19.cloned.1.call-start = ((), (), s32[]{:S(2)}) async-start(), calls=%async_computation.22 | async-start | bytes 5308416 | tf_op jit(solution)/shard_map/all_gather | solution.py:112
  568.5 181.3 %reduce-scatter.13.cloned.1.call-start = ((), (), s32[]{:S(2)}) async-start(), calls=%async_computation.23 | async-start | bytes 5308416 | tf_op jit(solution)/shard_map/reduce_scatter | solution.py:116
  653.0 96.8 %copy-start.1 = (bf16[128,2304]{1,0:T(8,128)(2,1)S(1)}, bf16[128,2304]{1,0:T(8,128)(2,1)}, u32[]{:S(2)}) copy-start(bf16[128,2304]{1,0:T(8,128)(2,1)} %reduce-scatter.9.cloned.1.call-done) | copy-start | bytes 1769476
  653.0 99.1 %copy-start.8 = (bf16[128,2304]{1,0:T(8,128)(2,1)S(1)}, bf16[128,2304]{1,0:T(8,128)(2,1)}, u32[]{:S(2)}) copy-start(bf16[128,2304]{1,0:T(8,128)(2,1)} %reduce-scatter.11.cloned.1.call-done) | copy-start | bytes 1769476
  653.0 152.9 %all-gather.21.cloned.1.call-start = ((), (), s32[]{:S(2)}) async-start(), calls=%async_computation.24 | async-start | bytes 5308416 | tf_op jit(solution)/shard_map/all_gather | solution.py:112
  758.8 92.6 %reduce-scatter.23.cloned.1.call-start = ((), (), s32[]{:S(2)}) async-start(), calls=%async_computation.29 | async-start | bytes 6635520 | tf_op jit(solution)/shard_map/reduce_scatter | solution.py:116
  768.6 37.3 %copy-start.12 = (bf16[8,288,1,256]{3,1,0,2:T(8,128)(2,1)S(1)}, bf16[8,288,1,256]{3,1,0,2:T(8,128)(2,1)}, u32[]{:S(2)}) copy-start(bf16[8,288,1,256]{3,1,0,2:T(8,128)(2,1)} %copy.108) | copy-start | bytes 3538948
  768.6 41.2 %copy-start.23 = (bf16[1024,256]{0,1:T(8,128)(2,1)S(1)}, bf16[1024,256]{0,1:T(8,128)(2,1)}, u32[]{:S(2)}) copy-start(bf16[1024,256]{0,1:T(8,128)(2,1)} %copy-done.22) | copy-start | bytes 1572868
  768.6 41.2 %copy-start.34 = (bf16[1024,256]{0,1:T(8,128)(2,1)S(1)}, bf16[1024,256]{0,1:T(8,128)(2,1)}, u32[]{:S(2)}) copy-start(bf16[1024,256]{0,1:T(8,128)(2,1)} %copy-done.33) | copy-start | bytes 1572868
  768.6 41.2 %copy-start.42 = (s32[1024]{0:T(1024)S(1)}, s32[1024]{0:T(1024)}, u32[]{:S(2)}) copy-start(s32[1024]{0:T(1024)} %copy-done.41) | copy-start | bytes 12292
  768.7 41.2 %copy-start.50 = (f32[1024]{0:T(1024)S(1)}, f32[1024]{0:T(1024)}, u32[]{:S(2)}) copy-start(f32[1024]{0:T(1024)} %copy-done.49) | copy-start | bytes 12292
  768.7 41.2 %copy-start.52 = (f32[1024]{0:T(1024)S(1)}, f32[1024]{0:T(1024)}, u32[]{:S(2)}) copy-start(f32[1024]{0:T(1024)} %copy-done.51) | copy-start | bytes 12292
  768.7 133.3 %reduce-scatter.19.cloned.1.call-start = ((), (), s32[]{:S(2)}) async-start(), calls=%async_computation.27 | async-start | bytes 1474560 | tf_op jit(solution)/shard_map/reduce_scatter | solution.py:116
  818.5 6.2 collective-permute-start.1
  821.4 127.1 %reduce-scatter.17.cloned.1.call-start = ((), (), s32[]{:S(2)}) async-start(), calls=%async_computation.26 | async-start | bytes 2949120 | tf_op jit(solution)/shard_map/reduce_scatter | solution.py:116
  834.2 222.1 %reduce-scatter.21.cloned.1.call-start = ((), (), s32[]{:S(2)}) async-start(), calls=%async_computation.28 | async-start | bytes 13271040 | tf_op jit(solution)/shard_map/reduce_scatter | solution.py:116
  851.4 50.6 %all-to-all-start.7 = ((bf16[8,72,1152]{2,1,0:T(8,128)(2,1)}), bf16[8,72,1152]{2,1,0:T(8,128)(2,1)S(1)}, u32[]{:S(2)}, u32[]{:S(2)}) async-start(bf16[8,72,1152]{2,1,0:T(8,128)(2,1)} %bitcast.171), calls=%async_computation.15 | async-start | bytes 2654208 | tf_op jit(solution)/shard_map/all_to_all | solution.py:135
  856.6 257.7 %reduce-scatter.15.cloned.1.call-start = ((), (), s32[]{:S(2)}) async-start(), calls=%async_computation.25 | async-start | bytes 5308416 | tf_op jit(solution)/shard_map/reduce_scatter | solution.py:116
  862.9 42.7 %copy-start.46 = (f32[2304]{0:T(1024)S(1)}, f32[2304]{0:T(1024)}, u32[]{:S(2)}) copy-start(f32[2304]{0:T(1024)} %get-tuple-element.23) | copy-start | bytes 27652
  863.0 43.4 %copy-start.48 = (f32[2304]{0:T(1024)S(1)}, f32[2304]{0:T(1024)}, u32[]{:S(2)}) copy-start(f32[2304]{0:T(1024)} %get-tuple-element.19) | copy-start | bytes 27652
  863.0 44.1 %copy-start.47 = (f32[2304]{0:T(1024)S(1)}, f32[2304]{0:T(1024)}, u32[]{:S(2)}) copy-start(f32[2304]{0:T(1024)} %get-tuple-element.17) | copy-start | bytes 27652
  863.0 44.8 %copy-start.62 = (f32[128]{0:T(128)S(1)}, f32[128]{0:T(128)}, u32[]{:S(2)}) copy-start(f32[128]{0:T(128)} %get-tuple-element.25) | copy-start | bytes 1540
  902.0 10.9 all-to-all-start.5
  948.5 107.8 %all-to-all-start.4 = ((bf16[8,72,512]{2,1,0:T(8,128)(2,1)}), bf16[8,72,512]{2,1,0:T(8,128)(2,1)S(1)}, u32[]{:S(2)}, u32[]{:S(2)}) async-start(bf16[8,72,512]{2,1,0:T(8,128)(2,1)} %bitcast.183), calls=%async_computation.9 | async-start | bytes 1179648 | tf_op jit(solution)/shard_map/all_to_all | solution.py:135
  1057.1 65.5 %all-to-all-start.6 = ((bf16[8,72,2304]{2,1,0:T(8,128)(2,1)}), bf16[8,72,2304]{2,1,0:T(8,128)(2,1)}, u32[]{:S(2)}, u32[]{:S(2)}) async-start(bf16[8,72,2304]{2,1,0:T(8,128)(2,1)} %bitcast.162), calls=%async_computation.13 | async-start | bytes 5308416 | tf_op jit(solution)/shard_map/all_to_all | solution.py:135
  1074.5 41.6 %copy-start.43 = (f32[1,32,72]{2,0,1:T(1,128)S(1)}, f32[1,32,72]{2,0,1:T(1,128)}, u32[]{:S(2)}) copy-start(f32[1,32,72]{2,0,1:T(1,128)} %stack.18) | copy-start | bytes 27652
  1074.5 41.6 %copy-start.44 = (f32[1,32,72]{2,0,1:T(1,128)S(1)}, f32[1,32,72]{2,0,1:T(1,128)}, u32[]{:S(2)}) copy-start(f32[1,32,72]{2,0,1:T(1,128)} %stack.16) | copy-start | bytes 27652
  1074.5 41.6 %copy-start.45 = (f32[1,32,72]{2,0,1:T(1,128)S(1)}, f32[1,32,72]{2,0,1:T(1,128)}, u32[]{:S(2)}) copy-start(f32[1,32,72]{2,0,1:T(1,128)} %stack.17) | copy-start | bytes 27652
  1074.5 42.4 %copy-start.63 = (f32[128]{0:T(128)S(1)}, f32[128]{0:T(128)}, u32[]{:S(2)}) copy-start(f32[128]{0:T(128)} %get-tuple-element.25) | copy-start | bytes 1540
  1074.5 42.4 %copy-start.7 = (f32[128,2304]{1,0:T(8,128)S(1)}, f32[128,2304]{1,0:T(8,128)}, u32[]{:S(2)}) copy-start(f32[128,2304]{1,0:T(8,128)} %copy-done.6) | copy-start | bytes 3538948
  1122.6 18.5 %all-to-all-start.8 = ((f32[4,32,72]{2,0,1:T(4,128)}), f32[4,32,72]{2,0,1:T(4,128)S(1)}, u32[]{:S(2)}, u32[]{:S(2)}) async-start(f32[4,32,72]{2,0,1:T(4,128)} %pad_maximum_fusion.12), calls=%async_computation.16 | async-start | bytes 131072 | tf_op jit(solution)/shard_map/all_to_all | solution.py:323
  (52 other events, 190.4 us)
Sparse Core Ops, SparseCore 0:
  22.5 29.9 all-gather.26
  54.6 49.8 all-gather.24
  106.4 37.6 all-gather.22
  167.6 53.8 reduce-scatter.8
  758.9 46.9 all-gather.20
Sparse Core Ops, SparseCore 1:
  234.3 103.9 all-gather.14
  340.4 51.2 all-gather.12
  393.6 60.4 all-gather.16
  464.6 98.0 reduce-scatter.10
  568.6 51.1 all-gather.18
  653.1 96.6 reduce-scatter.12
  768.7 74.1 reduce-scatter.22
  845.7 51.3 reduce-scatter.18
  900.0 48.5 reduce-scatter.16
  951.9 104.3 reduce-scatter.20
  1060.6 53.7 reduce-scatter.14

commit v2 on v1

--- a/solution.py
+++ b/solution.py
@@ -120,20 +120,130 @@
     return lax.ppermute(piece, axis, [(0, 1), (1, 0)])
 
 
+def zero_after(*earlier):
+    zero = jnp.float32(0)
+    for array in earlier:
+        first = lax.slice(array, (0,) * array.ndim, (1,) * array.ndim).reshape(())
+        zero = zero + jnp.minimum(jnp.abs(first.astype(jnp.float32)), 0.0)
+    return zero
+
+
+def after(array, *earlier):
+    return array + zero_after(*earlier).astype(array.dtype)
+
+
+def in_order(mine, other, index, axis):
+    return jnp.where(index == 0, jnp.stack([mine, other], axis), jnp.stack([other, mine], axis))
+
+
+def gather_plane_near(block):
+    half = block.shape[0] // 2
+    return exchange(block[:half], "x"), exchange(block[half:], "y")
+
+
+def gather_plane_far(block, near, zero=0.0):
+    x_id, y_id = lax.axis_index("x"), lax.axis_index("y")
+    half = block.shape[0] // 2
+    upper_row = in_order(block[:half], near[0], x_id, 0)
+    lower_column = in_order(block[half:], near[1], y_id, 0)
+    upper_all = in_order(upper_row, exchange(upper_row, "y"), y_id, 0)
+    lower_all = in_order(lower_column, exchange(lower_column, "x"), x_id, 1)
+    whole = jnp.concatenate([upper_all, lower_all], 2) + jnp.asarray(zero, block.dtype)
+    return whole.reshape(4 * block.shape[0], block.shape[1])
+
+
+def gather_heads(block, earlier):
+    plane = gather_plane_far(block, gather_plane_near(block), zero_after(earlier))
+    both = in_order(
+        plane.reshape((HEADS // 2,) + block.shape),
+        exchange(plane, "core").reshape((HEADS // 2,) + block.shape),
+        lax.axis_index("core"),
+        1,
+    )
+    return both.reshape(HEADS * block.shape[0], block.shape[1])
+
+
+def scatter_plane_far(terms):
+    x_id, y_id = lax.axis_index("x"), lax.axis_index("y")
+    rows, columns = terms.shape[0] // 4, terms.shape[1]
+    half = rows // 2
+    start = (2 * (1 - y_id) + 1 - x_id) * rows
+    upper = lax.dynamic_slice(terms, (start, 0), (half, columns))
+    lower = lax.dynamic_slice(terms, (start + half, 0), (half, columns))
+    return exchange(upper, "x"), exchange(lower, "y")
+
+
+def scatter_plane_near(terms, far):
+    x_id, y_id = lax.axis_index("x"), lax.axis_index("y")
+    rows, columns = terms.shape[0] // 4, terms.shape[1]
+    half = rows // 2
+
+    def part(y_at, x_at, first):
+        start = (2 * y_at + x_at) * rows + first
+        return lax.dynamic_slice(terms, (start, 0), (half, columns))
+
+    def add(left, right):
+        return low(left.astype(jnp.float32) + right.astype(jnp.float32))
+
+    upper_far, lower_far = far
+    to_y = jnp.concatenate([add(part(1 - y_id, x_id, 0), upper_far), part(1 - y_id, x_id, half)], 0)
+    to_x = jnp.concatenate([part(y_id, 1 - x_id, 0), add(part(y_id, 1 - x_id, half), lower_far)], 0)
+    return to_y, to_x
+
+
+def scatter_plane_sum(terms, from_y, from_x):
+    x_id, y_id = lax.axis_index("x"), lax.axis_index("y")
+    rows, columns = terms.shape[0] // 4, terms.shape[1]
+    mine = lax.dynamic_slice(terms, ((2 * y_id + x_id) * rows, 0), (rows, columns))
+    return mine.astype(jnp.float32) + from_y.astype(jnp.float32) + from_x.astype(jnp.float32)
+
+
+def scatter_plane(terms):
+    to_y, to_x = scatter_plane_near(terms, scatter_plane_far(terms))
+    return scatter_plane_sum(terms, exchange(to_y, "y"), exchange(to_x, "x"))
+
+
+def my_half(first, second):
+    return jnp.where(lax.axis_index("core") == 0, first, second)
+
+
+def sum_cores(product, array):
+    half = array.shape[0] // 2
+    first, second = array[:half], array[half:]
+    came = exchange(low(product(my_half(second, first))), "core")
+    mine = lax.optimization_barrier(low(product(my_half(first, second))))
+    return low(mine.astype(jnp.float32) + came.astype(jnp.float32))
+
+
+def head_terms(terms):
+    rows, width = terms.shape
+    blocks = terms.reshape(HEADS // 2, 2, rows // HEADS, width)
+    came = exchange(my_half(blocks[:, 1], blocks[:, 0]), "core")
+    mine = my_half(blocks[:, 0], blocks[:, 1])
+    return low(mine.astype(jnp.float32) + came.astype(jnp.float32)).reshape(rows // 2, width)
+
+
+def over_fsdp(terms, fsdp_count):
+    blocks = terms.reshape(fsdp_count, terms.shape[0] // fsdp_count, terms.shape[1])
+    return lax.all_to_all(blocks, "fsdp", split_axis=0, concat_axis=0, tiled=True)
+
+
 def columns_out(weight_piece, axes, parts):
     rows = weight_piece.shape[0]
-    blocks = weight_piece.reshape(rows, parts, -1)
-    return lax.all_to_all(blocks, axes, split_axis=1, concat_axis=0, tiled=True).reshape(
+    blocks = jnp.transpose(weight_piece.reshape(rows, parts, -1), (1, 0, 2))
+    return lax.all_to_all(blocks, axes, split_axis=0, concat_axis=0, tiled=True).reshape(
         parts * rows, -1
     )
 
 
-def columns_back(grad_piece, axes, parts):
-    rows = grad_piece.shape[0] // parts
-    blocks = grad_piece.reshape(parts, rows, -1)
-    return jnp.transpose(
-        lax.all_to_all(blocks, axes, split_axis=0, concat_axis=0, tiled=True), (1, 0, 2)
-    )
+def blocks_back(grad_piece, axes, parts):
+    blocks = grad_piece.reshape(parts, -1, grad_piece.shape[1])
+    return lax.all_to_all(blocks, axes, split_axis=0, concat_axis=0, tiled=True)
+
+
+def side_by_side(blocks):
+    parts, rows, columns = blocks.shape
+    return jnp.swapaxes(blocks, 0, 1).reshape(rows, parts * columns).astype(jnp.float32)
 
 
 def per_device(
@@ -173,36 +283,48 @@
     ff_own = ff_width // tensor_parts
     scale = HEAD_DIM ** (-0.5)
 
+    gate_up_mine = columns_out(
+        jnp.concatenate(
+            [
+                low(w_gate_up[:, :ff_width]).reshape(own_rows, tensor_parts, ff_own),
+                low(w_gate_up[:, ff_width:]).reshape(own_rows, tensor_parts, ff_own),
+            ],
+            2,
+        ),
+        TENSOR,
+        tensor_parts,
+    )
+    own_gate_up = gather_rows(gate_up_mine, ("row",) + PLANE)
+    seq_tokens = gather_rows(tokens[0], CTX)
+
+    def to_heads(pieces):
+        copies = jnp.broadcast_to(
+            pieces[None, :, None], (row_parts, HEADS, fsdp_count) + pieces.shape[1:]
+        ).reshape((-1,) + pieces.shape[1:])
+        return lax.all_to_all(copies, EVERY, split_axis=0, concat_axis=0, tiled=True)
+
     q_cols = low(w_qkv[:, :q_width]).reshape(own_rows, HEADS, HEAD_DIM)
     k_cols = low(w_qkv[:, q_width : q_width + kv_width]).reshape(own_rows, KV_HEADS, 1, HEAD_DIM)
     v_cols = low(w_qkv[:, q_width + kv_width :]).reshape(own_rows, KV_HEADS, 1, HEAD_DIM)
     kv_cols = jnp.concatenate([k_cols, v_cols], 2).reshape(own_rows, HEADS, HEAD_DIM)
-
-    def head_weight(cols):
-        mine = columns_out(cols, HEAD_AXES, HEADS).reshape(HEADS, own_rows, -1)
-        every = lax.all_gather(mine, "fsdp", axis=1, tiled=False)
-        if row_parts > 1:
-            every = lax.all_gather(every, "row", axis=0, tiled=True)
-        return every.reshape(width, -1)
-
-    head_qkv = head_weight(jnp.concatenate([q_cols, kv_cols], 2))
-    head_out = head_weight(low(w_out).reshape(own_rows, HEADS, HEAD_DIM))
-
-    gate_up_cols = jnp.concatenate(
-        [
-            low(w_gate_up[:, :ff_width]).reshape(own_rows, tensor_parts, ff_own),
-            low(w_gate_up[:, ff_width:]).reshape(own_rows, tensor_parts, ff_own),
-        ],
-        2,
-    )
-    own_gate_up = gather_rows(
-        columns_out(gate_up_cols, TENSOR, tensor_parts), ("row",) + PLANE
-    )
-    own_down = gather_rows(
-        columns_out(low(w_down), TENSOR, tensor_parts), ("row",) + PLANE
-    )
-
-    gains = lax.all_gather(low(norm_gains), EVERY, axis=1, tiled=True).astype(jnp.float32)
+    qkv_cols = jnp.concatenate([q_cols, kv_cols], 2)
+    gain_piece = jnp.pad(
+        low(norm_gains).reshape(1, 1, 4 * own_rows),
+        ((0, HEADS - 1), (0, 7), (0, 2 * HEAD_DIM - 4 * own_rows)),
+        mode="edge",
+    )
+    pieces = jnp.concatenate([jnp.swapaxes(qkv_cols, 0, 1), gain_piece], 1)
+    received = to_heads(after(pieces, gate_up_mine))
+    head_qkv = received[:, :own_rows].reshape(width, 2 * HEAD_DIM)
+    gains = (
+        jnp.swapaxes(received[:, own_rows, : 4 * own_rows].reshape(-1, 4, own_rows), 0, 1)
+        .reshape(4, width)
+        .astype(jnp.float32)
+    )
+    out_pieces = jnp.swapaxes(low(w_out).reshape(own_rows, HEADS, HEAD_DIM), 0, 1)
+    head_out = to_heads(after(out_pieces, received)).reshape(width, HEAD_DIM)
+
+    down_mine = columns_out(after(low(w_down), head_out), TENSOR, tensor_parts)
 
     key_positions = positions_of(block_order, seq_length, block_size)
     cos_table, sin_table = rope_tables(key_positions, HEAD_DIM)
@@ -217,7 +339,6 @@
     allowed = key_positions[None, :] <= query_part(key_positions)[:, None]
 
     inputs = tokens[0].astype(jnp.float32)
-    seq_tokens = gather_rows(tokens[0], CTX)
     normed_one = low(rms_norm(seq_tokens.astype(jnp.float32), gains[0]))
     normed_query = query_part(normed_one)
     queries = low(rotate(dot(normed_query, head_qkv[:, :HEAD_DIM]), query_cos, query_sin))
@@ -233,48 +354,56 @@
     exp_total = jnp.sum(exp_scores, -1, keepdims=True)
     probs = exp_scores / exp_total
     probs_low = low(probs)
-    attended = low(dot(probs_low, values))
-    branch = scatter_rows(low(dot_t(attended, head_out)), HEAD_AXES).astype(jnp.float32)
+    attended = low(dot(probs_low, values) + zero_after(head_out))
+    branch = scatter_plane(head_terms(low(dot_t(attended, head_out))))
     hidden_in = inputs + rms_norm(branch, gains[1])
 
-    normed_two = gather_rows(low(rms_norm(hidden_in, gains[2])), TENSOR)
+    normed_two_mine = low(rms_norm(hidden_in, gains[2]) + zero_after(own_gate_up, down_mine))
+    normed_two = gather_rows(normed_two_mine, TENSOR)
+    down_mine = after(down_mine, normed_two_mine)
+    down_near = gather_plane_near(down_mine)
     gate_up = dot(normed_two, own_gate_up)
     gate_part, up_part = gate_up[:, :ff_own], gate_up[:, ff_own:]
+    own_down = gather_plane_far(down_mine, down_near, zero_after(gate_up))
+    if row_parts > 1:
+        own_down = gather_rows(own_down, "row")
     activated = low(gated_unit(gate_part, up_part))
-    lowered = scatter_rows(low(dot_t(activated, own_down)), TENSOR).astype(jnp.float32)
+    lowered_terms = sum_cores(lambda rows: dot_t(rows, own_down), activated)
+    lowered_pieces = over_fsdp(lowered_terms, fsdp_count)
+    later_gate_up = after(gate_up, lowered_terms)
+    _, pull_back = jax.vjp(gated_unit, later_gate_up[:, :ff_own], later_gate_up[:, ff_own:])
+    gate_factor, up_factor = lax.optimization_barrier(pull_back(jnp.ones_like(gate_part)))
+    lowered_pieces = after(lowered_pieces, gate_factor, up_factor)
+    lowered = jnp.sum(lowered_pieces.astype(jnp.float32), 0)
     output = low(hidden_in + rms_norm(lowered, gains[3]))[None]
 
     upstream = cotangent[0].astype(jnp.float32)
     grad_lowered, gain_three = norm_back(lowered, gains[3], upstream)
     grad_lowered = gather_rows(low(grad_lowered), TENSOR)
+    plane_down = scatter_rows(low(t_dot(grad_lowered, activated)), ("row",) + PLANE)
     grad_activated = dot(grad_lowered, own_down)
-    _, pull_back = jax.vjp(gated_unit, gate_part, up_part)
-    grad_gate_up = low(jnp.concatenate(pull_back(grad_activated), 1))
-    grad_normed_two = scatter_rows(low(dot_t(grad_gate_up, own_gate_up)), TENSOR).astype(
-        jnp.float32
-    )
-    term_gate_up = low(t_dot(normed_two, grad_gate_up))
-    term_down = low(t_dot(grad_lowered, activated))
-
-    def ff_grad(term):
-        return columns_back(
-            scatter_rows(term, ("row",) + PLANE), TENSOR, tensor_parts
-        ).astype(jnp.float32)
-
-    sum_gate_up = ff_grad(term_gate_up)
-    grad_gate_up_w = jnp.concatenate(
-        [
-            sum_gate_up[:, :, :ff_own].reshape(own_rows, ff_width),
-            sum_gate_up[:, :, ff_own:].reshape(own_rows, ff_width),
-        ],
-        1,
-    )
-    grad_down = ff_grad(term_down).reshape(own_rows, ff_width)
+    grad_gate_up = low(
+        jnp.concatenate([grad_activated * gate_factor, grad_activated * up_factor], 1)
+    )
+    normed_two_terms = sum_cores(lambda rows: dot_t(rows, own_gate_up), grad_gate_up)
+    normed_two_pieces = over_fsdp(normed_two_terms, fsdp_count)
+    term_gate = low(t_dot(normed_two, grad_gate_up[:, :ff_own]))
+    plane_gate = scatter_rows(term_gate, ("row",) + PLANE)
+    normed_two_pieces = after(normed_two_pieces, term_gate)
+    grad_normed_two = jnp.sum(normed_two_pieces.astype(jnp.float32), 0)
 
     grad_hidden_part, gain_two = norm_back(hidden_in, gains[2], grad_normed_two)
     grad_hidden = upstream + grad_hidden_part
     grad_branch, gain_one = norm_back(branch, gains[1], grad_hidden)
-    grad_branch = gather_rows(low(grad_branch), HEAD_AXES)
+    grad_branch_mine = low(grad_branch)
+    later_rows = after(normed_two, grad_branch_mine)
+    plane_up = scatter_rows(
+        low(t_dot(later_rows, grad_gate_up[:, ff_own:])), ("row",) + PLANE
+    )
+    blocks_down = blocks_back(after(plane_down, normed_two_pieces), TENSOR, tensor_parts)
+    grad_branch = gather_heads(grad_branch_mine, blocks_down)
+    blocks_gate = blocks_back(after(plane_gate, blocks_down), TENSOR, tensor_parts)
+    blocks_up = blocks_back(after(plane_up, blocks_gate), TENSOR, tensor_parts)
 
     grad_attended = low(dot(grad_branch, head_out))
     grad_probs = dot_t(grad_attended, values)
@@ -291,24 +420,41 @@
     kv_back = jnp.where(core_id == 0, rotate(kv_terms, query_cos, -query_sin), kv_terms)
     grad_projected = low(
         jnp.concatenate([rotate(grad_queries, query_cos, -query_sin), kv_back], 1)
-    )
-    grad_normed_one = scatter_rows(low(dot_t(grad_projected, head_qkv)), HEAD_AXES).astype(
-        jnp.float32
-    )
+        + zero_after(blocks_gate)
+    )
+    grad_normed_one = scatter_plane(head_terms(low(dot_t(grad_projected, head_qkv))))
     grad_input_part, gain_zero = norm_back(inputs, gains[0], grad_normed_one)
     token_grad = low(grad_hidden + grad_input_part)[None]
 
-    def head_grad(term):
-        term = low(term)
-        if row_parts > 1:
-            term = scatter_rows(term, "row")
-        by_owner = jnp.transpose(
-            term.reshape(HEADS, fsdp_count, own_rows, -1), (1, 0, 2, 3)
-        ).reshape(term.shape)
-        return columns_back(scatter_rows(by_owner, "fsdp"), HEAD_AXES, HEADS).astype(jnp.float32)
-
-    grad_out = head_grad(t_dot(grad_branch, attended)).reshape(own_rows, q_width)
-    sum_qkv = head_grad(t_dot(normed_query, grad_projected))
+    def to_owners(term):
+        blocks = term.reshape(row_parts * HEADS * fsdp_count, -1, term.shape[1])
+        return lax.all_to_all(blocks, EVERY, split_axis=0, concat_axis=0, tiled=True)
+
+    def head_grad(pieces):
+        pieces = pieces.reshape((row_parts, HEADS, fsdp_count) + pieces.shape[1:])
+        return jnp.swapaxes(jnp.sum(pieces.astype(jnp.float32), (0, 2)), 0, 1)
+
+    qkv_pieces = to_owners(after(low(t_dot(normed_query, grad_projected)), blocks_up))
+    sum_qkv = head_grad(qkv_pieces)
+
+    gain_terms = jnp.stack([gain_zero, gain_one, gain_two, gain_three], 0)
+    gain_terms = jnp.swapaxes(gain_terms.reshape(4, -1, own_rows), 0, 1).reshape(-1, 4 * own_rows)
+    gain_high = low(gain_terms)
+    gain_low = low(gain_terms - gain_high.astype(jnp.float32))
+    gain_rows = jnp.pad(
+        jnp.concatenate([gain_high, gain_low], 1), ((0, 0), (0, 8 * HEAD_DIM - 8 * own_rows))
+    ).reshape(-1, 8, HEAD_DIM)
+    out_term = after(low(t_dot(grad_branch, attended)), qkv_pieces)
+    out_pieces = to_owners(
+        jnp.concatenate([out_term.reshape(-1, own_rows, HEAD_DIM), gain_rows], 1).reshape(
+            -1, HEAD_DIM
+        )
+    )
+    grad_out = head_grad(out_pieces[:, :own_rows]).reshape(own_rows, q_width)
+    grad_gains = jnp.sum(
+        out_pieces[:, own_rows:].reshape(-1, 8 * HEAD_DIM)[:, : 8 * own_rows].astype(jnp.float32),
+        0,
+    ).reshape(2, 4, own_rows).sum(0)
     kv_sum = sum_qkv[:, :, HEAD_DIM:].reshape(own_rows, KV_HEADS, 2, HEAD_DIM)
     grad_qkv = jnp.concatenate(
         [
@@ -318,13 +464,8 @@
         ],
         1,
     )
-    gain_terms = jnp.stack([gain_zero, gain_one, gain_two, gain_three], 0)
-    grad_gains = jnp.sum(
-        lax.all_to_all(
-            gain_terms.reshape(4, -1, own_rows), EVERY, split_axis=1, concat_axis=1, tiled=True
-        ),
-        1,
-    )
+    grad_down = side_by_side(blocks_down)
+    grad_gate_up_w = jnp.concatenate([side_by_side(blocks_gate), side_by_side(blocks_up)], 1)
     moment_qkv, square_qkv, new_qkv = adamw(
         w_qkv, first_qkv, second_qkv, grad_qkv, MATRIX_RATE, WEIGHT_DECAY
     )

time: 1160 us -> 863 us (0.74)
  waiting for transfers between devices: 693 us -> 426 us
  blocking collectives: 194 us -> 0 us
  other arithmetic: 73.5 us -> 137 us
  starting transfers between devices: 22.2 us -> 72.1 us
  local copies, waits for them, and re-layouts: 33.2 us -> 67.6 us
    reduce_scatter x8 -> x3, waiting for transfers between devices: 370 us -> 0.01 us  [scatter_rows(): return lax.psum_scatter(terms, axes, scatter_dimension=0, tiled=True)]
    all_to_all x5 -> x11, waiting for transfers between devices: 47.6 us -> 273 us  [the longest x2 91.8 us: over_fsdp(): lax.all_to_all(blocks, 'fsdp', split_axis=0, concat_axis=0, tiled=True)]
    all_gather x6 -> x4, waiting for transfers between devices: 274 us -> 50 us  [gather_rows(): return lax.all_gather(piece, axes, axis=0, tiled=True)]
    all_to_all x4 -> x0, blocking collectives: 126 us -> none  [columns_out(): lax.all_to_all(blocks, axes, split_axis=1, concat_axis=0, tiled=True)]
    ppermute x2 -> x23, waiting for transfers between devices: 0.01 us -> 101 us  [exchange(): return lax.ppermute(piece, axis, [(0, 1), (1, 0)])]
    all_gather x1 -> x0, blocking collectives: 67.5 us -> none  [per_device(): lax.all_gather(low(norm_gains), EVERY, axis=1, tiled=True)]
    all_to_all x5 -> x11, starting transfers between devices: 20.3 us -> 50.9 us  [the longest x3 14.3 us: blocks_back(): return lax.all_to_all(blocks, axes, split_axis=0, concat_axis=0, tiled=True)]
    ppermute x2 -> x23, starting transfers between devices: 0.58 us -> 20.7 us  [exchange(): return lax.ppermute(piece, axis, [(0, 1), (1, 0)])]
  transfers between devices with their start and end apart: 23 -> 41, of which waited for: 14 -> 20; matrix products, arithmetic and copies ran while one was open for 12% -> 30% of each run, Pallas kernels for 0% -> 0%
where the time goes in v2:
time: 863 us; the launch traced here: 856 us
  waiting for transfers between devices  426 us (49%)
  other arithmetic  137 us (16%)
  matrix products  124 us (14%)
  starting transfers between devices  72.1 us (8%)
  local copies, waits for them, and re-layouts  67.6 us (8%)
  between operations  29 us (3%)
    ppermute x23, waiting for transfers between devices, exchange(): return lax.ppermute(piece, axis, [(0, 1), (1, 0)])  101 us
    all_to_all x2, waiting for transfers between devices, over_fsdp(): lax.all_to_all(blocks, 'fsdp', split_axis=0, concat_axis=0, tiled=True)  91.8 us
    all_to_all x2, waiting for transfers between devices, to_heads(): lax.all_to_all(copies, EVERY, split_axis=0, concat_axis=0, tiled=True)  65.3 us
    all_to_all x2, waiting for transfers between devices, columns_out(): lax.all_to_all(blocks, axes, split_axis=0, concat_axis=0, tiled=True)  63.9 us
    all_gather x4, waiting for transfers between devices, gather_rows(): return lax.all_gather(piece, axes, axis=0, tiled=True)  50 us
    dot_general x7, matrix products, t_dot(): lax.dot_general(left, right, (((0,), (0,)), ((), ())), preferred_element_...  46.4 us
    dot_general x7, matrix products, dot(): return jnp.dot(left, right, preferred_element_type=jnp.float32)  39.8 us
    dot_general x8, matrix products, dot_t(): lax.dot_general(left, right, (((1,), (1,)), ((), ())), preferred_element_...  38 us
  transfers between devices with their start and end apart: 41, of which 20 were waited for; matrix products, arithmetic and copies ran while one was open for 30% of the time, Pallas kernels for 0%

profile of v2, /device:TPU:0, one launch (start us, length us, event | category | flops | bytes accessed | tf_op | source)
XLA Modules:
  0.0 855.6 jit_solution(8587736780221079770)
XLA Ops:
  12.8 6.5 all-to-all-start
  20.4 59.4 %all-to-all-done = bf16[8,72,2304]{2,1,0:T(8,128)(2,1)} async-done(((bf16[8,72,2304]{2,1,0:T(8,128)(2,1)}), bf16[8,72,2304]{2,1,0:T(8,128)(2,1)}, u32[]{:S(2)}, u32[]{:S(2)}) %all-to-all-start) | async-done | bytes 2654240 | tf_op jit(solution)/shard_map/all_to_all | solution.py:234
  83.9 3.5 all-to-all-start.1
  88.4 3.4 fusion
  91.8 54.6 %all-to-all-done.1 = bf16[32,80,512]{2,1,0:T(8,128)(2,1)} async-done(((bf16[32,80,512]{2,1,0:T(8,128)(2,1)}), bf16[32,80,512]{2,1,0:T(8,128)(2,1)}, u32[]{:S(2)}, u32[]{:S(2)}) %all-to-all-start.1) | async-done | bytes 2621472 | tf_op jit(solution)/shard_map/all_to_all | solution.py:304
  151.6 5.0 all-to-all-start.2
  173.7 10.7 %all-to-all-done.2 = bf16[32,72,256]{2,1,0:T(8,128)(2,1)S(1)} async-done(((bf16[32,72,256]{2,1,0:T(8,128)(2,1)}), bf16[32,72,256]{2,1,0:T(8,128)(2,1)S(1)}, u32[]{:S(2)}, u32[]{:S(2)}) %all-to-all-start.2) | async-done | bytes 1179680 | tf_op jit(solution)/shard_map/all_to_all | solution.py:304
  185.6 4.1 fusion.36
  198.8 4.3 all-to-all-start.3
  203.3 4.0 fusion.17
  210.3 14.1 %collective-permute-done.2 = bf16[64,2304]{1,0:T(8,128)(2,1)S(1)} collective-permute-done((bf16[64,2304]{1,0:T(8,128)(2,1)}, bf16[64,2304]{1,0:T(8,128)(2,1)S(1)}, u32[]{:S(2)}, u32[]{:S(2)}) %collective-permute-start.2) | collective-permute-done | bytes 294944 | tf_op jit(solution)/shard_map/ppermute | solution.py:120
  230.8 4.4 all-to-all-done.3
  237.1 6.8 collective-permute-done.5
  256.7 14.5 %collective-permute-done.6 = bf16[288,1152]{1,0:T(8,128)(2,1)S(1)} collective-permute-done((bf16[288,1152]{1,0:T(8,128)(2,1)}, bf16[288,1152]{1,0:T(8,128)(2,1)S(1)}, u32[]{:S(2)}, u32[]{:S(2)}) %collective-permute-start.6) | collective-permute-done | bytes 663584 | tf_op jit(solution)/shard_map/ppermute | solution.py:120
  280.0 24.0 %collective-permute-done.7 = bf16[2,288,1152]{2,1,0:T(8,128)(2,1)} collective-permute-done((bf16[2,288,1152]{2,1,0:T(8,128)(2,1)}, bf16[2,288,1152]{2,1,0:T(8,128)(2,1)}, u32[]{:S(2)}, u32[]{:S(2)}) %collective-permute-start.7) | collective-permute-done | bytes 1327136 | tf_op jit(solution)/shard_map/ppermute | solution.py:120
  309.1 14.9 %fusion.139 = f32[1024,2304]{1,0:T(8,128)S(1)} fusion(bf16[1024,2304]{1,0:T(8,128)(2,1)} %all-gather.8.cloned.1.call-done, bf16[2304,2304]{1,0:T(8,128)(2,1)} %all-gather.6.cloned.1.call-done), kind=kOutput, calls=%fused_computation.310 | convolution fusion | flops 10871635968 | bytes 24772608 | tf_op jit(solution)/shard_map/dot_general | solution.py:100
  332.3 3.6 convolution_convert_fusion.5
  336.0 3.6 convolution_convert_fusion.6
  342.4 4.6 all-to-all-start.4
  349.1 4.3 broadcast_add_fusion
  353.4 4.1 add_multiply_fusion
  362.5 39.1 %all-to-all-done.4 = bf16[4,128,2304]{2,1,0:T(8,128)(2,1)} async-done(((bf16[4,128,2304]{2,1,0:T(8,128)(2,1)}), bf16[4,128,2304]{2,1,0:T(8,128)(2,1)}, u32[]{:S(2)}, u32[]{:S(2)}) %all-to-all-start.4) | async-done | bytes 2359328 | tf_op jit(solution)/shard_map/all_to_all | solution.py:228
  407.1 50.0 %all-gather.10.cloned.1.call-done = bf16[1024,2304]{1,0:T(8,128)(2,1)} async-done(((bf16[128,2304]{1,0:T(8,128)(2,1)}), bf16[1024,2304]{1,0:T(8,128)(2,1)}) %all-gather.10.cloned.1.call-update) | async-done | bytes 4718608 | tf_op jit(solution)/shard_map/all_gather | solution.py:112
  457.1 10.4 %convolution_convert_fusion.1 = bf16[2304,1152]{1,0:T(8,128)(2,1)} fusion(bf16[1024,2304]{1,0:T(8,128)(2,1)} %all-gather.10.cloned.1.call-done, bf16[1024,1152]{1,0:T(8,128)(2,1)} %copy-done.29), kind=kOutput, calls=%fused_computation.3 | convolution fusion | flops 5438472192 | bytes 12386304 | tf_op jit(solution)/shard_map/dot_general | solution.py:108
  467.6 13.8 %multiply_convert_fusion.1 = (bf16[1024,1152]{1,0:T(8,128)(2,1)}, bf16[1024,1152]{1,0:T(8,128)(2,1)S(1)}) fusion(f32[1024,1152]{1,0:T(8,128)} %copy-done.22, f32[1024,1152]{1,0:T(8,128)} %copy-done.21, bf16[1024,2304]{1,0:T(8,128)(2,1)} %all-gather.10.cloned.1.call-done, bf16[2304,1152]{1,0:T(8,128)(2,1)} %bitcast.260), kind=kOutput, calls=%fused_computation.44 | convolution fusion | flops 5440536576 | bytes 24182784 | tf_op jit(solution)/shard_map/dot_general | solution.py:100
  481.4 12.6 %convolution_convert_fusion.8 = bf16[512,2304]{1,0:T(8,128)(2,1)} fusion(bf16[2304,2304]{1,0:T(8,128)(2,1)} %all-gather.6.cloned.1.call-done, pred[]{:T(512)S(6)} %eq.14, bf16[1024,1152]{1,0:T(8,128)(2,1)S(1)} %get-tuple-element.60, bf16[1024,1152]{1,0:T(8,128)(2,1)} %get-tuple-element.59), kind=kOutput, calls=%fused_computation.52 | convolution fusion | flops 5447614464 | bytes 17694720 | tf_op jit(solution)/shard_map/dot_general | solution.py:104
  494.2 9.7 %convolution_convert_fusion.2 = bf16[2304,1152]{1,0:T(8,128)(2,1)} fusion(bf16[1024,2304]{1,0:T(8,128)(2,1)S(1)} %bitcast.309, bf16[1024,1152]{1,0:T(8,128)(2,1)} %get-tuple-element.59), kind=kOutput, calls=%fused_computation.4 | convolution fusion | flops 5438472192 | bytes 12386304 | tf_op jit(solution)/shard_map/dot_general | solution.py:108
  503.9 10.8 %convolution_convert_fusion.9 = bf16[512,2304]{1,0:T(8,128)(2,1)S(1)} fusion(bf16[2304,2304]{1,0:T(8,128)(2,1)} %all-gather.6.cloned.1.call-done, pred[]{:T(512)S(6)} %eq.14, bf16[1024,1152]{1,0:T(8,128)(2,1)} %copy-done.83, bf16[1024,1152]{1,0:T(8,128)(2,1)} %get-tuple-element.59), kind=kOutput, calls=%fused_computation.53 | convolution fusion | flops 5447614464 | bytes 17694720 | tf_op jit(solution)/shard_map/dot_general | solution.py:104
  514.8 3.7 add_convert_fusion
  518.5 4.7 all-to-all-start.5
  525.0 52.7 %all-to-all-done.5 = bf16[4,128,2304]{2,1,0:T(8,128)(2,1)} async-done(((bf16[4,128,2304]{2,1,0:T(8,128)(2,1)}), bf16[4,128,2304]{2,1,0:T(8,128)(2,1)}, u32[]{:S(2)}, u32[]{:S(2)}) %all-to-all-start.5) | async-done | bytes 2359328 | tf_op jit(solution)/shard_map/all_to_all | solution.py:228
  591.7 4.3 all-to-all-start.6
  596.1 10.5 %convolution_convert_fusion = bf16[2304,1152]{1,0:T(8,128)(2,1)} fusion(bf16[1024,1152]{1,0:T(8,128)(2,1)} %copy-done.83, bf16[1024,2304]{1,0:T(8,128)(2,1)} %all-gather.8.cloned.1.call-done, bf16[]{:T(256)} %bitcast.81), kind=kOutput, calls=%fused_computation.2 | convolution fusion | flops 5440831488 | bytes 12386306 | tf_op jit(solution)/shard_map/dot_general | solution.py:108
  608.7 21.2 %collective-permute-done.13 = bf16[2,64,2304]{2,1,0:T(8,128)(2,1)S(1)} collective-permute-done((bf16[2,64,2304]{2,1,0:T(8,128)(2,1)S(1)}, bf16[2,64,2304]{2,1,0:T(8,128)(2,1)S(1)}, u32[]{:S(2)}, u32[]{:S(2)}) %collective-permute-start.13) | collective-permute-done | bytes 589856 | tf_op jit(solution)/shard_map/ppermute | solution.py:120
  640.3 5.5 all-to-all-start.7
  660.7 3.4 broadcast_select_fusion
  670.5 7.4 all-to-all-done.7
  696.2 4.5 all-to-all-start.8
  700.7 8.8 %multiply_subtract_fusion.1 = (f32[72,9216]{1,0:T(8,128)}, f32[72,9216]{1,0:T(8,128)}, f32[72,9216]{1,0:T(8,128)}) fusion(f32[72,9216]{1,0:T(8,128)} %param.24, f32[72,9216]{1,0:T(8,128)} %bitcast.249, f32[72,9216]{1,0:T(8,128)} %param.34, f32[72,9216]{1,0:T(8,128)} %param.29), kind=kLoop, calls=%fused_computation.72 | loop fusion | flops 9953280 | bytes 18579456 | tf_op jit(solution)/shard_map/sub | solution.py:92
  717.7 15.1 %all-to-all-done.8 = bf16[8,72,1152]{2,1,0:T(8,128)(2,1)} async-done(((bf16[8,72,1152]{2,1,0:T(8,128)(2,1)}), bf16[8,72,1152]{2,1,0:T(8,128)(2,1)}, u32[]{:S(2)}, u32[]{:S(2)}) %all-to-all-start.8) | async-done | bytes 1327136 | tf_op jit(solution)/shard_map/all_to_all | solution.py:241
  734.6 7.6 fusion.19
  744.8 3.5 all-to-all-start.9
  754.0 13.0 %multiply_subtract_fusion = (f32[72,18432]{1,0:T(8,128)}, f32[72,18432]{1,0:T(8,128)}, f32[72,18432]{1,0:T(8,128)}) fusion(f32[72,18432]{1,0:T(8,128)} %param.23, bf16[72,9216]{1,0:T(8,128)(2,1)S(1)} %bitcast.257, bf16[72,9216]{1,0:T(8,128)(2,1)S(1)} %bitcast.256, f32[72,18432]{1,0:T(8,128)} %param.33, f32[72,18432]{1,0:T(8,128)} %param.28), kind=kLoop, calls=%fused_computation.20 | loop fusion | flops 25214976 | bytes 34504704 | tf_op jit(solution)/shard_map/sub | solution.py:92
  767.0 17.3 %collective-permute-done.22 = bf16[128,2304]{1,0:T(8,128)(2,1)S(1)} collective-permute-done((bf16[128,2304]{1,0:T(8,128)(2,1)S(1)}, bf16[128,2304]{1,0:T(8,128)(2,1)S(1)}, u32[]{:S(2)}, u32[]{:S(2)}) %collective-permute-start.22) | collective-permute-done | bytes 589856 | tf_op jit(solution)/shard_map/ppermute | solution.py:120
  792.9 8.7 %all-to-all-done.9 = bf16[32,72,512]{2,1,0:T(8,128)(2,1)} async-done(((bf16[32,72,512]{2,1,0:T(8,128)(2,1)}), bf16[32,72,512]{2,1,0:T(8,128)(2,1)}, u32[]{:S(2)}, u32[]{:S(2)}) %all-to-all-start.9) | async-done | bytes 2359328 | tf_op jit(solution)/shard_map/all_to_all | solution.py:431
  803.5 3.9 fusion.22
  808.6 4.4 all-to-all-start.10
  822.7 20.9 %all-to-all-done.10 = bf16[32,80,256]{2,1,0:T(8,128)(2,1)} async-done(((bf16[32,80,256]{2,1,0:T(8,128)(2,1)}), bf16[32,80,256]{2,1,0:T(8,128)(2,1)}, u32[]{:S(2)}, u32[]{:S(2)}) %all-to-all-start.10) | async-done | bytes 1310752 | tf_op jit(solution)/shard_map/all_to_all | solution.py:431
  (414 shorter events, 204.5 us)
Async XLA Ops:
  7.2 81.2 %all-gather.12.cloned.1.call-start = ((), (), s32[]{:S(2)}) async-start(), calls=%async_computation.20 | async-start | bytes 5308416 | tf_op jit(solution)/shard_map/all_gather | solution.py:112
  12.8 67.1 %all-to-all-start = ((bf16[8,72,2304]{2,1,0:T(8,128)(2,1)}), bf16[8,72,2304]{2,1,0:T(8,128)(2,1)}, u32[]{:S(2)}, u32[]{:S(2)}) async-start(bf16[8,72,2304]{2,1,0:T(8,128)(2,1)} %maximum_bitcast_fusion), calls=%async_computation | async-start | bytes 5308416 | tf_op jit(solution)/shard_map/all_to_all | solution.py:234
  83.9 62.5 %all-to-all-start.1 = ((bf16[32,80,512]{2,1,0:T(8,128)(2,1)}), bf16[32,80,512]{2,1,0:T(8,128)(2,1)}, u32[]{:S(2)}, u32[]{:S(2)}) async-start(bf16[32,80,512]{2,1,0:T(8,128)(2,1)} %bitcast.250), calls=%async_computation.1 | async-start | bytes 5242880 | tf_op jit(solution)/shard_map/all_to_all | solution.py:304
  87.5 158.9 %all-gather.6.cloned.1.call-start = ((), (), s32[]{:S(2)}) async-start(), calls=%async_computation.14 | async-start | bytes 13271040 | tf_op jit(solution)/shard_map/all_gather | solution.py:112
  88.3 78.3 %copy-start.70 = (f32[128]{0:T(128)}, f32[128]{0:T(128)S(1)}, u32[]{:S(2)}) copy-start(f32[128]{0:T(128)S(1)} %multiply_power_fusion) | copy-start | bytes 1540
  88.4 78.2 %copy-start.58 = (f32[1024]{0:T(1024)}, f32[1024]{0:T(1024)S(1)}, u32[]{:S(2)}) copy-start(f32[1024]{0:T(1024)S(1)} %get-tuple-element.107) | copy-start | bytes 12292
  88.4 97.2 %copy-start.56 = (s32[1024]{0:T(1024)}, s32[1024]{0:T(1024)S(1)}, u32[]{:S(2)}) copy-start(s32[1024]{0:T(1024)S(1)} %get-tuple-element.106) | copy-start | bytes 12292
  88.4 61.9 %copy-start.27 = (f32[72,2048]{1,0:T(8,128)S(1)}, f32[72,2048]{1,0:T(8,128)}, u32[]{:S(2)}) copy-start(f32[72,2048]{1,0:T(8,128)} %param.22) | copy-start | bytes 1769476
  91.8 72.8 %copy-start.74 = (f32[1024]{0:T(1024)}, f32[1024]{0:T(1024)S(1)}, u32[]{:S(2)}) copy-start(f32[1024]{0:T(1024)S(1)} %add_rsqrt_fusion) | copy-start | bytes 12292
  151.6 32.8 %all-to-all-start.2 = ((bf16[32,72,256]{2,1,0:T(8,128)(2,1)}), bf16[32,72,256]{2,1,0:T(8,128)(2,1)S(1)}, u32[]{:S(2)}, u32[]{:S(2)}) async-start(bf16[32,72,256]{2,1,0:T(8,128)(2,1)} %bitcast.17), calls=%async_computation.2 | async-start | bytes 2359296 | tf_op jit(solution)/shard_map/all_to_all | solution.py:304
  164.3 4.6 collective-permute-start
  194.1 9.2 %collective-permute-start.1 = (bf16[4,128,2304]{2,1,0:T(8,128)(2,1)}, bf16[4,128,2304]{2,1,0:T(8,128)(2,1)}, u32[]{:S(2)}, u32[]{:S(2)}) collective-permute-start(bf16[4,128,2304]{2,1,0:T(8,128)(2,1)} %fusion.24), channel_id=1, source_target_pairs={{0,4},{4,0},{1,5},{5,1},{2,6},{6,2},{3,7},{7,3},{8,12},{12,8},{9,1... | collective-permute-start | bytes 7077896 | tf_op jit(solution)/shard_map/ppermute | solution.py:120
  198.8 36.4 %all-to-all-start.3 = ((bf16[8,72,1152]{2,1,0:T(8,128)(2,1)}), bf16[8,72,1152]{2,1,0:T(8,128)(2,1)}, u32[]{:S(2)}, u32[]{:S(2)}) async-start(bf16[8,72,1152]{2,1,0:T(8,128)(2,1)} %bitcast.238), calls=%async_computation.3 | async-start | bytes 2654208 | tf_op jit(solution)/shard_map/all_to_all | solution.py:234
  203.1 106.0 %all-gather.8.cloned.1.call-start = ((), (), s32[]{:S(2)}) async-start(), calls=%async_computation.15 | async-start | bytes 5308416 | tf_op jit(solution)/shard_map/all_gather | solution.py:112
  208.3 16.2 %collective-permute-start.2 = (bf16[64,2304]{1,0:T(8,128)(2,1)}, bf16[64,2304]{1,0:T(8,128)(2,1)S(1)}, u32[]{:S(2)}, u32[]{:S(2)}) collective-permute-start(bf16[64,2304]{1,0:T(8,128)(2,1)} %get-tuple-element.71), channel_id=1, source_target_pairs={{0,8},{8,0},{1,9},{9,1},{2,10},{10,2},{3,11},{11,3},{4,12},{12,4},... | collective-permute-start | bytes 884744 | tf_op jit(solution)/shard_map/ppermute | solution.py:120
  209.8 16.0 %collective-permute-start.4 = (bf16[64,2304]{1,0:T(8,128)(2,1)S(1)}, bf16[64,2304]{1,0:T(8,128)(2,1)}, u32[]{:S(2)}, u32[]{:S(2)}) collective-permute-start(bf16[64,2304]{1,0:T(8,128)(2,1)S(1)} %get-tuple-element.72), channel_id=1, source_target_pairs={{0,16},{16,0},{1,17},{17,1},{2,18},{18,2},{3,19},{19,3},{4,20},{20... | collective-permute-start | bytes 884744 | tf_op jit(solution)/shard_map/ppermute | solution.py:120
  227.7 16.1 %collective-permute-start.5 = (bf16[128,2304]{1,0:T(8,128)(2,1)}, bf16[128,2304]{1,0:T(8,128)(2,1)}, u32[]{:S(2)}, u32[]{:S(2)}) collective-permute-start(bf16[128,2304]{1,0:T(8,128)(2,1)} %pad_maximum_fusion.4), channel_id=1, source_target_pairs={{0,8},{8,0},{1,9},{9,1},{2,10},{10,2},{3,11},{11,3},{4,12},{12,4},... | collective-permute-start | bytes 1769480 | tf_op jit(solution)/shard_map/ppermute | solution.py:120
  228.3 15.5 %collective-permute-start.3 = (bf16[128,2304]{1,0:T(8,128)(2,1)S(1)}, bf16[128,2304]{1,0:T(8,128)(2,1)S(1)}, u32[]{:S(2)}, u32[]{:S(2)}) collective-permute-start(bf16[128,2304]{1,0:T(8,128)(2,1)S(1)} %pad_maximum_fusion.3), channel_id=1, source_target_pairs={{0,16},{16,0},{1,17},{17,1},{2,18},{18,2},{3,19},{19,3},{4,20},{20... | collective-permute-start | bytes 1769480 | tf_op jit(solution)/shard_map/ppermute | solution.py:120
  229.9 351.4 %copy-start.53 = (f32[2304]{0:T(1024)}, f32[2304]{0:T(1024)S(1)}, u32[]{:S(2)}) copy-start(f32[2304]{0:T(1024)S(1)} %mul.688) | copy-start | bytes 27652
  254.6 16.6 %collective-permute-start.6 = (bf16[288,1152]{1,0:T(8,128)(2,1)}, bf16[288,1152]{1,0:T(8,128)(2,1)S(1)}, u32[]{:S(2)}, u32[]{:S(2)}) collective-permute-start(bf16[288,1152]{1,0:T(8,128)(2,1)} %get-tuple-element.80), channel_id=1, source_target_pairs={{0,8},{8,0},{1,9},{9,1},{2,10},{10,2},{3,11},{11,3},{4,12},{12,4},... | collective-permute-start | bytes 1990664 | tf_op jit(solution)/shard_map/ppermute | solution.py:120
  256.0 19.4 %collective-permute-start.8 = (bf16[288,1152]{1,0:T(8,128)(2,1)}, bf16[288,1152]{1,0:T(8,128)(2,1)}, u32[]{:S(2)}, u32[]{:S(2)}) collective-permute-start(bf16[288,1152]{1,0:T(8,128)(2,1)} %get-tuple-element.79), channel_id=1, source_target_pairs={{0,16},{16,0},{1,17},{17,1},{2,18},{18,2},{3,19},{19,3},{4,20},{20... | collective-permute-start | bytes 1990664 | tf_op jit(solution)/shard_map/ppermute | solution.py:120
  273.9 30.1 %collective-permute-start.7 = (bf16[2,288,1152]{2,1,0:T(8,128)(2,1)}, bf16[2,288,1152]{2,1,0:T(8,128)(2,1)}, u32[]{:S(2)}, u32[]{:S(2)}) collective-permute-start(bf16[2,288,1152]{2,1,0:T(8,128)(2,1)} %maximum_select_fusion.3), channel_id=1, source_target_pairs={{0,16},{16,0},{1,17},{17,1},{2,18},{18,2},{3,19},{19,3},{4,20},{20... | collective-permute-start | bytes 3981320 | tf_op jit(solution)/shard_map/ppermute | solution.py:120
  277.4 29.8 %collective-permute-start.9 = (bf16[2,288,1152]{2,1,0:T(8,128)(2,1)S(1)}, bf16[2,288,1152]{2,1,0:T(8,128)(2,1)S(1)}, u32[]{:S(2)}, u32[]{:S(2)}) collective-permute-start(bf16[2,288,1152]{2,1,0:T(8,128)(2,1)S(1)} %maximum_select_fusion.5), channel_id=1, source_target_pairs={{0,8},{8,0},{1,9},{9,1},{2,10},{10,2},{3,11},{11,3},{4,12},{12,4},... | collective-permute-start | bytes 3981320 | tf_op jit(solution)/shard_map/ppermute | solution.py:120
  335.9 4.6 collective-permute-start.10
  342.4 59.1 %all-to-all-start.4 = ((bf16[4,128,2304]{2,1,0:T(8,128)(2,1)}), bf16[4,128,2304]{2,1,0:T(8,128)(2,1)}, u32[]{:S(2)}, u32[]{:S(2)}) async-start(bf16[4,128,2304]{2,1,0:T(8,128)(2,1)} %bitcast.251), calls=%async_computation.4 | async-start | bytes 4718592 | tf_op jit(solution)/shard_map/all_to_all | solution.py:228
  347.1 110.0 %all-gather.10.cloned.1.call-start = ((), (), s32[]{:S(2)}) async-start(), calls=%async_computation.16 | async-start | bytes 5308416 | tf_op jit(solution)/shard_map/all_gather | solution.py:112
  407.0 182.2 %reduce-scatter.4.cloned.1.call-start = ((), (), s32[]{:S(2)}) async-start(), calls=%async_computation.17 | async-start | bytes 6635520 | tf_op jit(solution)/shard_map/reduce_scatter | solution.py:116
  467.5 170.1 %reduce-scatter.6.cloned.1.call-start = ((), (), s32[]{:S(2)}) async-start(), calls=%async_computation.18 | async-start | bytes 6635520 | tf_op jit(solution)/shard_map/reduce_scatter | solution.py:116
  494.0 20.8 %collective-permute-start.11 = (bf16[512,2304]{1,0:T(8,128)(2,1)}, bf16[512,2304]{1,0:T(8,128)(2,1)}, u32[]{:S(2)}, u32[]{:S(2)}) collective-permute-start(bf16[512,2304]{1,0:T(8,128)(2,1)} %convolution_convert_fusion.8), channel_id=1, source_target_pairs={{0,4},{4,0},{1,5},{5,1},{2,6},{6,2},{3,7},{7,3},{8,12},{12,8},{9,1... | collective-permute-start | bytes 7077896 | tf_op jit(solution)/shard_map/ppermute | solution.py:120
  518.5 59.3 %all-to-all-start.5 = ((bf16[4,128,2304]{2,1,0:T(8,128)(2,1)}), bf16[4,128,2304]{2,1,0:T(8,128)(2,1)}, u32[]{:S(2)}, u32[]{:S(2)}) async-start(bf16[4,128,2304]{2,1,0:T(8,128)(2,1)} %bitcast.252), calls=%async_computation.5 | async-start | bytes 4718592 | tf_op jit(solution)/shard_map/all_to_all | solution.py:228
  586.7 20.8 %collective-permute-start.14 = (bf16[64,2304]{1,0:T(8,128)(2,1)}, bf16[64,2304]{1,0:T(8,128)(2,1)S(1)}, u32[]{:S(2)}, u32[]{:S(2)}) collective-permute-start(bf16[64,2304]{1,0:T(8,128)(2,1)} %get-tuple-element.99), channel_id=1, source_target_pairs={{0,16},{16,0},{1,17},{17,1},{2,18},{18,2},{3,19},{19,3},{4,20},{20... | collective-permute-start | bytes 884744 | tf_op jit(solution)/shard_map/ppermute | solution.py:120
  587.9 18.7 %collective-permute-start.12 = (bf16[64,2304]{1,0:T(8,128)(2,1)}, bf16[64,2304]{1,0:T(8,128)(2,1)S(1)}, u32[]{:S(2)}, u32[]{:S(2)}) collective-permute-start(bf16[64,2304]{1,0:T(8,128)(2,1)} %get-tuple-element.100), channel_id=1, source_target_pairs={{0,8},{8,0},{1,9},{9,1},{2,10},{10,2},{3,11},{11,3},{4,12},{12,4},... | collective-permute-start | bytes 884744 | tf_op jit(solution)/shard_map/ppermute | solution.py:120
  591.7 39.9 %all-to-all-start.6 = ((bf16[8,72,1152]{2,1,0:T(8,128)(2,1)}), bf16[8,72,1152]{2,1,0:T(8,128)(2,1)}, u32[]{:S(2)}, u32[]{:S(2)}) async-start(bf16[8,72,1152]{2,1,0:T(8,128)(2,1)} %bitcast.68), calls=%async_computation.7 | async-start | bytes 2654208 | tf_op jit(solution)/shard_map/all_to_all | solution.py:241
  596.0 97.6 %reduce-scatter.8.cloned.1.call-start = ((), (), s32[]{:S(2)}) async-start(), calls=%async_computation.19 | async-start | bytes 6635520 | tf_op jit(solution)/shard_map/reduce_scatter | solution.py:116
  606.7 23.2 %collective-permute-start.13 = (bf16[2,64,2304]{2,1,0:T(8,128)(2,1)S(1)}, bf16[2,64,2304]{2,1,0:T(8,128)(2,1)S(1)}, u32[]{:S(2)}, u32[]{:S(2)}) collective-permute-start(bf16[2,64,2304]{2,1,0:T(8,128)(2,1)S(1)} %maximum_select_fusion.10), channel_id=1, source_target_pairs={{0,16},{16,0},{1,17},{17,1},{2,18},{18,2},{3,19},{19,3},{4,20},{20... | collective-permute-start | bytes 1769480 | tf_op jit(solution)/shard_map/ppermute | solution.py:120
  607.6 23.8 %collective-permute-start.15 = (bf16[2,64,2304]{2,1,0:T(8,128)(2,1)S(1)}, bf16[2,64,2304]{2,1,0:T(8,128)(2,1)S(1)}, u32[]{:S(2)}, u32[]{:S(2)}) collective-permute-start(bf16[2,64,2304]{2,1,0:T(8,128)(2,1)S(1)} %maximum_select_fusion.12), channel_id=1, source_target_pairs={{0,8},{8,0},{1,9},{9,1},{2,10},{10,2},{3,11},{11,3},{4,12},{12,4},... | collective-permute-start | bytes 1769480 | tf_op jit(solution)/shard_map/ppermute | solution.py:120
  635.5 12.4 %collective-permute-start.16 = (bf16[512,2304]{1,0:T(8,128)(2,1)}, bf16[512,2304]{1,0:T(8,128)(2,1)}, u32[]{:S(2)}, u32[]{:S(2)}) collective-permute-start(bf16[512,2304]{1,0:T(8,128)(2,1)} %bitcast.70), channel_id=1, source_target_pairs={{0,4},{4,0},{1,5},{5,1},{2,6},{6,2},{3,7},{7,3},{8,12},{12,8},{9,1... | collective-permute-start | bytes 7077896 | tf_op jit(solution)/shard_map/ppermute | solution.py:120
  640.3 37.6 %all-to-all-start.7 = ((bf16[8,72,1152]{2,1,0:T(8,128)(2,1)}), bf16[8,72,1152]{2,1,0:T(8,128)(2,1)}, u32[]{:S(2)}, u32[]{:S(2)}) async-start(bf16[8,72,1152]{2,1,0:T(8,128)(2,1)} %bitcast.73), calls=%async_computation.9 | async-start | bytes 2654208 | tf_op jit(solution)/shard_map/all_to_all | solution.py:241
  664.1 17.6 %collective-permute-start.17 = (f32[1024,256]{0,1:T(8,128)}, f32[1024,256]{0,1:T(8,128)}, u32[]{:S(2)}, u32[]{:S(2)}) collective-permute-start(f32[1024,256]{0,1:T(8,128)} %get-tuple-element.112), channel_id=1, source_target_pairs={{0,4},{4,0},{1,5},{5,1},{2,6},{6,2},{3,7},{7,3},{8,12},{12,8},{9,1... | collective-permute-start | bytes 3145736 | tf_op jit(solution)/shard_map/ppermute | solution.py:120
  693.4 18.7 %collective-permute-start.18 = (bf16[4,128,2304]{2,1,0:T(8,128)(2,1)S(1)}, bf16[4,128,2304]{2,1,0:T(8,128)(2,1)}, u32[]{:S(2)}, u32[]{:S(2)}) collective-permute-start(bf16[4,128,2304]{2,1,0:T(8,128)(2,1)S(1)} %select_bitcast_fusion), channel_id=1, source_target_pairs={{0,4},{4,0},{1,5},{5,1},{2,6},{6,2},{3,7},{7,3},{8,12},{12,8},{9,1... | collective-permute-start | bytes 7077896 | tf_op jit(solution)/shard_map/ppermute | solution.py:120
  696.2 36.6 %all-to-all-start.8 = ((bf16[8,72,1152]{2,1,0:T(8,128)(2,1)}), bf16[8,72,1152]{2,1,0:T(8,128)(2,1)}, u32[]{:S(2)}, u32[]{:S(2)}) async-start(bf16[8,72,1152]{2,1,0:T(8,128)(2,1)} %bitcast.82), calls=%async_computation.11 | async-start | bytes 2654208 | tf_op jit(solution)/shard_map/all_to_all | solution.py:241
  715.8 32.5 %collective-permute-start.19 = (bf16[64,2304]{1,0:T(8,128)(2,1)}, bf16[64,2304]{1,0:T(8,128)(2,1)}, u32[]{:S(2)}, u32[]{:S(2)}) collective-permute-start(bf16[64,2304]{1,0:T(8,128)(2,1)} %get-tuple-element.65), channel_id=1, source_target_pairs={{0,8},{8,0},{1,9},{9,1},{2,10},{10,2},{3,11},{11,3},{4,12},{12,4},... | collective-permute-start | bytes 884744 | tf_op jit(solution)/shard_map/ppermute | solution.py:120
  716.9 31.4 %collective-permute-start.21 = (bf16[64,2304]{1,0:T(8,128)(2,1)}, bf16[64,2304]{1,0:T(8,128)(2,1)}, u32[]{:S(2)}, u32[]{:S(2)}) collective-permute-start(bf16[64,2304]{1,0:T(8,128)(2,1)} %get-tuple-element.66), channel_id=1, source_target_pairs={{0,16},{16,0},{1,17},{17,1},{2,18},{18,2},{3,19},{19,3},{4,20},{20... | collective-permute-start | bytes 884744 | tf_op jit(solution)/shard_map/ppermute | solution.py:120
  744.8 56.9 %all-to-all-start.9 = ((bf16[32,72,512]{2,1,0:T(8,128)(2,1)}), bf16[32,72,512]{2,1,0:T(8,128)(2,1)}, u32[]{:S(2)}, u32[]{:S(2)}) async-start(bf16[32,72,512]{2,1,0:T(8,128)(2,1)} %bitcast.278), calls=%async_computation.12 | async-start | bytes 4718592 | tf_op jit(solution)/shard_map/all_to_all | solution.py:431
  750.7 33.6 %collective-permute-start.22 = (bf16[128,2304]{1,0:T(8,128)(2,1)S(1)}, bf16[128,2304]{1,0:T(8,128)(2,1)S(1)}, u32[]{:S(2)}, u32[]{:S(2)}) collective-permute-start(bf16[128,2304]{1,0:T(8,128)(2,1)S(1)} %pad_maximum_fusion.6), channel_id=1, source_target_pairs={{0,8},{8,0},{1,9},{9,1},{2,10},{10,2},{3,11},{11,3},{4,12},{12,4},... | collective-permute-start | bytes 1769480 | tf_op jit(solution)/shard_map/ppermute | solution.py:120
  752.4 31.9 %collective-permute-start.20 = (bf16[128,2304]{1,0:T(8,128)(2,1)S(1)}, bf16[128,2304]{1,0:T(8,128)(2,1)S(1)}, u32[]{:S(2)}, u32[]{:S(2)}) collective-permute-start(bf16[128,2304]{1,0:T(8,128)(2,1)S(1)} %pad_maximum_fusion.5), channel_id=1, source_target_pairs={{0,16},{16,0},{1,17},{17,1},{2,18},{18,2},{3,19},{19,3},{4,20},{20... | collective-permute-start | bytes 1769480 | tf_op jit(solution)/shard_map/ppermute | solution.py:120
  754.0 30.4 %copy-start.76 = (f32[128]{0:T(128)S(1)}, f32[128]{0:T(128)}, u32[]{:S(2)}) copy-start(f32[128]{0:T(128)} %fusion.113) | copy-start | bytes 1540
  808.6 34.9 %all-to-all-start.10 = ((bf16[32,80,256]{2,1,0:T(8,128)(2,1)}), bf16[32,80,256]{2,1,0:T(8,128)(2,1)}, u32[]{:S(2)}, u32[]{:S(2)}) async-start(bf16[32,80,256]{2,1,0:T(8,128)(2,1)} %pad_maximum_fusion.2), calls=%async_computation.13 | async-start | bytes 2621440 | tf_op jit(solution)/shard_map/all_to_all | solution.py:431
  (81 other events, 618.4 us)
Sparse Core Ops, SparseCore 0:
  9.9 41.6 all-gather.11
  90.2 142.2 all-gather.5
  249.4 51.7 all-gather.7
  407.2 49.8 all-gather.9
  467.7 60.7 reduce-scatter.3
  531.9 64.7 reduce-scatter.5
  606.7 69.6 reduce-scatter.7

commit v3 on v2

--- a/solution.py
+++ b/solution.py
@@ -356,9 +356,9 @@
     probs_low = low(probs)
     attended = low(dot(probs_low, values) + zero_after(head_out))
     branch = scatter_plane(head_terms(low(dot_t(attended, head_out))))
-    hidden_in = inputs + rms_norm(branch, gains[1])
-
-    normed_two_mine = low(rms_norm(hidden_in, gains[2]) + zero_after(own_gate_up, down_mine))
+    hidden_in = after(inputs, own_gate_up, down_mine) + rms_norm(branch, gains[1])
+
+    normed_two_mine = low(rms_norm(hidden_in, gains[2]))
     normed_two = gather_rows(normed_two_mine, TENSOR)
     down_mine = after(down_mine, normed_two_mine)
     down_near = gather_plane_near(down_mine)
@@ -385,25 +385,28 @@
     grad_gate_up = low(
         jnp.concatenate([grad_activated * gate_factor, grad_activated * up_factor], 1)
     )
-    normed_two_terms = sum_cores(lambda rows: dot_t(rows, own_gate_up), grad_gate_up)
+    normed_two_halves = low(dot_t(grad_gate_up, own_gate_up))
+    half = normed_two_halves.shape[0] // 2
+    sent = my_half(normed_two_halves[half:], normed_two_halves[:half])
+    normed_two_terms = low(
+        my_half(normed_two_halves[:half], normed_two_halves[half:]).astype(jnp.float32)
+        + exchange(sent, "core").astype(jnp.float32)
+    )
     normed_two_pieces = over_fsdp(normed_two_terms, fsdp_count)
-    term_gate = low(t_dot(normed_two, grad_gate_up[:, :ff_own]))
+    term_gate = low(t_dot(normed_two, after(grad_gate_up[:, :ff_own], normed_two_terms)))
     plane_gate = scatter_rows(term_gate, ("row",) + PLANE)
-    normed_two_pieces = after(normed_two_pieces, term_gate)
+    term_up = low(t_dot(normed_two, after(grad_gate_up[:, ff_own:], term_gate)))
+    plane_up = scatter_rows(term_up, ("row",) + PLANE)
+    normed_two_pieces = after(normed_two_pieces, term_up, plane_down)
     grad_normed_two = jnp.sum(normed_two_pieces.astype(jnp.float32), 0)
 
     grad_hidden_part, gain_two = norm_back(hidden_in, gains[2], grad_normed_two)
     grad_hidden = upstream + grad_hidden_part
     grad_branch, gain_one = norm_back(branch, gains[1], grad_hidden)
     grad_branch_mine = low(grad_branch)
-    later_rows = after(normed_two, grad_branch_mine)
-    plane_up = scatter_rows(
-        low(t_dot(later_rows, grad_gate_up[:, ff_own:])), ("row",) + PLANE
-    )
-    blocks_down = blocks_back(after(plane_down, normed_two_pieces), TENSOR, tensor_parts)
+    blocks_down = blocks_back(after(plane_down, grad_normed_two), TENSOR, tensor_parts)
     grad_branch = gather_heads(grad_branch_mine, blocks_down)
-    blocks_gate = blocks_back(after(plane_gate, blocks_down), TENSOR, tensor_parts)
-    blocks_up = blocks_back(after(plane_up, blocks_gate), TENSOR, tensor_parts)
+    blocks_gate = blocks_back(plane_gate, TENSOR, tensor_parts)
 
     grad_attended = low(dot(grad_branch, head_out))
     grad_probs = dot_t(grad_attended, values)
@@ -434,27 +437,24 @@
         pieces = pieces.reshape((row_parts, HEADS, fsdp_count) + pieces.shape[1:])
         return jnp.swapaxes(jnp.sum(pieces.astype(jnp.float32), (0, 2)), 0, 1)
 
-    qkv_pieces = to_owners(after(low(t_dot(normed_query, grad_projected)), blocks_up))
-    sum_qkv = head_grad(qkv_pieces)
+    out_term = lax.optimization_barrier(low(t_dot(grad_branch, attended)))
+    out_pieces = to_owners(out_term)
+    blocks_up = blocks_back(plane_up, TENSOR, tensor_parts)
+    qkv_term = low(t_dot(normed_query, grad_projected))
+    if row_parts > 1:
+        qkv_term = scatter_rows(qkv_term, "row")
+    by_owner = jnp.swapaxes(qkv_term.reshape(HEADS, fsdp_count, own_rows, -1), 0, 1)
+    qkv_mine = scatter_rows(by_owner.reshape(qkv_term.shape), "fsdp")
+    qkv_blocks = blocks_back(qkv_mine, HEAD_AXES, HEADS)
+    sum_qkv = jnp.swapaxes(qkv_blocks, 0, 1).astype(jnp.float32)
+    grad_out = head_grad(out_pieces).reshape(own_rows, q_width)
 
     gain_terms = jnp.stack([gain_zero, gain_one, gain_two, gain_three], 0)
-    gain_terms = jnp.swapaxes(gain_terms.reshape(4, -1, own_rows), 0, 1).reshape(-1, 4 * own_rows)
-    gain_high = low(gain_terms)
-    gain_low = low(gain_terms - gain_high.astype(jnp.float32))
-    gain_rows = jnp.pad(
-        jnp.concatenate([gain_high, gain_low], 1), ((0, 0), (0, 8 * HEAD_DIM - 8 * own_rows))
-    ).reshape(-1, 8, HEAD_DIM)
-    out_term = after(low(t_dot(grad_branch, attended)), qkv_pieces)
-    out_pieces = to_owners(
-        jnp.concatenate([out_term.reshape(-1, own_rows, HEAD_DIM), gain_rows], 1).reshape(
-            -1, HEAD_DIM
-        )
-    )
-    grad_out = head_grad(out_pieces[:, :own_rows]).reshape(own_rows, q_width)
-    grad_gains = jnp.sum(
-        out_pieces[:, own_rows:].reshape(-1, 8 * HEAD_DIM)[:, : 8 * own_rows].astype(jnp.float32),
-        0,
-    ).reshape(2, 4, own_rows).sum(0)
+    gain_terms = jnp.swapaxes(gain_terms.reshape(4, -1, own_rows), 0, 1)
+    gain_pieces = lax.all_to_all(
+        after(gain_terms, qkv_blocks), EVERY, split_axis=0, concat_axis=0, tiled=True
+    )
+    grad_gains = jnp.sum(gain_pieces, 0)
     kv_sum = sum_qkv[:, :, HEAD_DIM:].reshape(own_rows, KV_HEADS, 2, HEAD_DIM)
     grad_qkv = jnp.concatenate(
         [

time: 863 us -> 817 us (0.947)
  other arithmetic: 137 us -> 119 us
  waiting for transfers between devices: 426 us -> 414 us
  matrix products: 124 us -> 114 us
  local copies, waits for them, and re-layouts: 67.6 us -> 58.6 us
    reduce_scatter x3 -> x4, waiting for transfers between devices: 0.01 us -> 35.9 us  [scatter_rows(): return lax.psum_scatter(terms, axes, scatter_dimension=0, tiled=True)]
    all_to_all x2 -> x1, waiting for transfers between devices: 29.6 us -> 10.2 us  [to_owners(): lax.all_to_all(blocks, EVERY, split_axis=0, concat_axis=0, tiled=True)]
    all_to_all x2, waiting for transfers between devices: 91.8 us -> 77.6 us  [over_fsdp(): lax.all_to_all(blocks, 'fsdp', split_axis=0, concat_axis=0, tiled=True)]
    all_to_all x3 -> x4, waiting for transfers between devices: 22.5 us -> 15.2 us  [blocks_back(): return lax.all_to_all(blocks, axes, split_axis=0, concat_axis=0, tiled=True)]
    dot_general x8 -> x7, matrix products: 38 us -> 31.9 us  [dot_t(): lax.dot_general(left, right, (((1,), (1,)), ((), ())), preferred_element_...]
    all_to_all x3 -> x4, starting transfers between devices: 14.3 us -> 18.1 us  [blocks_back(): return lax.all_to_all(blocks, axes, split_axis=0, concat_axis=0, tiled=True)]
    convert_element_type x14 -> x13, other arithmetic: 23.1 us -> 19.7 us  [low(): return values.astype(jnp.bfloat16)]
    unnamed x184 -> x174, local copies, waits for them, and re-layouts: 18.8 us -> 21.3 us
  transfers between devices with their start and end apart: 41 -> 43, of which waited for: 20 -> 25; matrix products, arithmetic and copies ran while one was open for 30% -> 28% of each run, Pallas kernels for 0% -> 0%
where the time goes in v3:
time: 817 us; the launch traced here: 811 us
  waiting for transfers between devices  414 us (51%)
  other arithmetic  119 us (15%)
  matrix products  114 us (14%)
  starting transfers between devices  75.8 us (9%)
  local copies, waits for them, and re-layouts  58.6 us (7%)
  between operations  29.5 us (4%)
    ppermute x23, waiting for transfers between devices, exchange(): return lax.ppermute(piece, axis, [(0, 1), (1, 0)])  93.2 us
    all_to_all x2, waiting for transfers between devices, over_fsdp(): lax.all_to_all(blocks, 'fsdp', split_axis=0, concat_axis=0, tiled=True)  77.6 us
    all_to_all x2, waiting for transfers between devices, to_heads(): lax.all_to_all(copies, EVERY, split_axis=0, concat_axis=0, tiled=True)  65.2 us
    all_to_all x2, waiting for transfers between devices, columns_out(): lax.all_to_all(blocks, axes, split_axis=0, concat_axis=0, tiled=True)  62.3 us
    all_gather x4, waiting for transfers between devices, gather_rows(): return lax.all_gather(piece, axes, axis=0, tiled=True)  50 us
    dot_general x7, matrix products, t_dot(): lax.dot_general(left, right, (((0,), (0,)), ((), ())), preferred_element_...  41.3 us
    dot_general x7, matrix products, dot(): return jnp.dot(left, right, preferred_element_type=jnp.float32)  40.3 us
    reduce_scatter x4, waiting for transfers between devices, scatter_rows(): return lax.psum_scatter(terms, axes, scatter_dimension=0, tiled=True)  35.9 us
  transfers between devices with their start and end apart: 43, of which 25 were waited for; matrix products, arithmetic and copies ran while one was open for 28% of the time, Pallas kernels for 0%

profile of v3, /device:TPU:0, one launch (start us, length us, event | category | flops | bytes accessed | tf_op | source)
XLA Modules:
  0.0 810.7 jit_solution(1402194792364351383)
XLA Ops:
  12.8 6.5 all-to-all-start
  22.4 57.3 %all-to-all-done = bf16[8,72,2304]{2,1,0:T(8,128)(2,1)S(1)} async-done(((bf16[8,72,2304]{2,1,0:T(8,128)(2,1)}), bf16[8,72,2304]{2,1,0:T(8,128)(2,1)S(1)}, u32[]{:S(2)}, u32[]{:S(2)}) %all-to-all-start) | async-done | bytes 2654240 | tf_op jit(solution)/shard_map/all_to_all | solution.py:234
  91.5 54.6 %all-to-all-done.1 = bf16[32,80,512]{2,1,0:T(8,128)(2,1)S(1)} async-done(((bf16[32,80,512]{2,1,0:T(8,128)(2,1)}), bf16[32,80,512]{2,1,0:T(8,128)(2,1)S(1)}, u32[]{:S(2)}, u32[]{:S(2)}) %all-to-all-start.1) | async-done | bytes 2621472 | tf_op jit(solution)/shard_map/all_to_all | solution.py:304
  149.7 4.8 all-to-all-start.2
  171.6 10.7 %all-to-all-done.2 = bf16[32,72,256]{2,1,0:T(8,128)(2,1)} async-done(((bf16[32,72,256]{2,1,0:T(8,128)(2,1)}), bf16[32,72,256]{2,1,0:T(8,128)(2,1)}, u32[]{:S(2)}, u32[]{:S(2)}) %all-to-all-start.2) | async-done | bytes 1179680 | tf_op jit(solution)/shard_map/all_to_all | solution.py:304
  184.2 4.1 fusion.32
  197.4 4.3 all-to-all-start.3
  202.2 4.0 fusion.20
  209.1 14.2 %collective-permute-done.2 = bf16[64,2304]{1,0:T(8,128)(2,1)S(1)} collective-permute-done((bf16[64,2304]{1,0:T(8,128)(2,1)}, bf16[64,2304]{1,0:T(8,128)(2,1)S(1)}, u32[]{:S(2)}, u32[]{:S(2)}) %collective-permute-start.2) | collective-permute-done | bytes 294944 | tf_op jit(solution)/shard_map/ppermute | solution.py:120
  228.9 4.9 all-to-all-done.3
  235.6 8.0 collective-permute-done.5
  256.5 14.6 %collective-permute-done.6 = bf16[288,1152]{1,0:T(8,128)(2,1)S(1)} collective-permute-done((bf16[288,1152]{1,0:T(8,128)(2,1)}, bf16[288,1152]{1,0:T(8,128)(2,1)S(1)}, u32[]{:S(2)}, u32[]{:S(2)}) %collective-permute-start.6) | collective-permute-done | bytes 663584 | tf_op jit(solution)/shard_map/ppermute | solution.py:120
  279.9 24.0 %collective-permute-done.7 = bf16[2,288,1152]{2,1,0:T(8,128)(2,1)} collective-permute-done((bf16[2,288,1152]{2,1,0:T(8,128)(2,1)}, bf16[2,288,1152]{2,1,0:T(8,128)(2,1)}, u32[]{:S(2)}, u32[]{:S(2)}) %collective-permute-start.7) | collective-permute-done | bytes 1327136 | tf_op jit(solution)/shard_map/ppermute | solution.py:120
  309.1 14.9 %fusion.134 = f32[1024,2304]{1,0:T(8,128)S(1)} fusion(bf16[1024,2304]{1,0:T(8,128)(2,1)} %all-gather.8.cloned.1.call-done, bf16[2304,2304]{1,0:T(8,128)(2,1)} %all-gather.6.cloned.1.call-done), kind=kOutput, calls=%fused_computation.296 | convolution fusion | flops 10871635968 | bytes 24772608 | tf_op jit(solution)/shard_map/dot_general | solution.py:100
  332.3 3.6 convolution_convert_fusion.6
  335.9 4.9 convolution_convert_fusion.7
  342.9 4.5 all-to-all-start.4
  349.4 4.3 broadcast_add_fusion
  353.7 4.1 add_multiply_fusion
  362.7 39.5 %all-to-all-done.4 = bf16[4,128,2304]{2,1,0:T(8,128)(2,1)} async-done(((bf16[4,128,2304]{2,1,0:T(8,128)(2,1)}), bf16[4,128,2304]{2,1,0:T(8,128)(2,1)}, u32[]{:S(2)}, u32[]{:S(2)}) %all-to-all-start.4) | async-done | bytes 2359328 | tf_op jit(solution)/shard_map/all_to_all | solution.py:228
  407.1 50.0 %all-gather.10.cloned.1.call-done = bf16[1024,2304]{1,0:T(8,128)(2,1)} async-done(((bf16[128,2304]{1,0:T(8,128)(2,1)}), bf16[1024,2304]{1,0:T(8,128)(2,1)}) %all-gather.10.cloned.1.call-update) | async-done | bytes 4718608 | tf_op jit(solution)/shard_map/all_gather | solution.py:112
  457.1 10.4 %convolution_convert_fusion = bf16[2304,1152]{1,0:T(8,128)(2,1)} fusion(bf16[1024,2304]{1,0:T(8,128)(2,1)} %all-gather.10.cloned.1.call-done, bf16[1024,1152]{1,0:T(8,128)(2,1)} %copy-done.34), kind=kOutput, calls=%fused_computation.2 | convolution fusion | flops 5438472192 | bytes 12386304 | tf_op jit(solution)/shard_map/dot_general | solution.py:108
  467.6 12.0 %multiply_convert_fusion.1 = (bf16[1024,1152]{1,0:T(8,128)(2,1)S(1)}, bf16[1024,1152]{1,0:T(8,128)(2,1)S(1)}) fusion(f32[1024,1152]{1,0:T(8,128)} %copy-done.25, f32[1024,1152]{1,0:T(8,128)} %copy-done.24, bf16[1024,2304]{1,0:T(8,128)(2,1)} %all-gather.10.cloned.1.call-done, bf16[2304,1152]{1,0:T(8,128)(2,1)} %bitcast.259), kind=kOutput, calls=%fused_computation.44 | convolution fusion | flops 5440536576 | bytes 24182784 | tf_op jit(solution)/shard_map/dot_general | solution.py:100
  479.7 14.6 %convolution_convert_fusion.4 = bf16[1024,2304]{1,0:T(8,128)(2,1)S(1)} fusion(bf16[2304,2304]{1,0:T(8,128)(2,1)} %all-gather.6.cloned.1.call-done, bf16[1024,1152]{1,0:T(8,128)(2,1)S(1)} %get-tuple-element.56, bf16[1024,1152]{1,0:T(8,128)(2,1)S(1)} %get-tuple-element.55), kind=kOutput, calls=%fused_computation.16 | convolution fusion | flops 10883432448 | bytes 20054016 | tf_op jit(solution)/shard_map/dot_general | solution.py:104
  494.7 4.4 collective-permute-done.11
  502.7 8.1 convolution_convert_fusion.2
  510.8 4.5 all-to-all-start.5
  517.2 10.7 %convolution_convert_fusion.1 = bf16[2304,1152]{1,0:T(8,128)(2,1)} fusion(bf16[1024,2304]{1,0:T(8,128)(2,1)} %all-gather.8.cloned.1.call-done, bf16[1024,1152]{1,0:T(8,128)(2,1)} %copy-done.76, bf16[]{:T(256)} %bitcast.53), kind=kOutput, calls=%fused_computation.3 | convolution fusion | flops 5439651840 | bytes 12386306 | tf_op jit(solution)/shard_map/dot_general | solution.py:108
  531.7 38.1 %all-to-all-done.5 = bf16[4,128,2304]{2,1,0:T(8,128)(2,1)} async-done(((bf16[4,128,2304]{2,1,0:T(8,128)(2,1)}), bf16[4,128,2304]{2,1,0:T(8,128)(2,1)}, u32[]{:S(2)}, u32[]{:S(2)}) %all-to-all-start.5) | async-done | bytes 2359328 | tf_op jit(solution)/shard_map/all_to_all | solution.py:228
  578.2 4.3 all-to-all-start.6
  583.9 6.6 collective-permute-done.12
  592.1 6.5 collective-permute-done.14
  599.8 11.4 %collective-permute-done.13 = bf16[2,64,2304]{2,1,0:T(8,128)(2,1)S(1)} collective-permute-done((bf16[2,64,2304]{2,1,0:T(8,128)(2,1)S(1)}, bf16[2,64,2304]{2,1,0:T(8,128)(2,1)S(1)}, u32[]{:S(2)}, u32[]{:S(2)}) %collective-permute-start.13) | collective-permute-done | bytes 589856 | tf_op jit(solution)/shard_map/ppermute | solution.py:120
  619.2 4.7 all-to-all-start.7
  627.6 3.9 convolution_convert_fusion.10
  646.9 20.0 %reduce-scatter.11.cloned.1.call-done = bf16[576,1152]{1,0:T(8,128)(2,1)} async-done(((bf16[2304,1152]{1,0:T(8,128)(2,1)}), bf16[576,1152]{1,0:T(8,128)(2,1)}) %reduce-scatter.11.cloned.1.call-update) | async-done | bytes 1327120 | tf_op jit(solution)/shard_map/reduce_scatter | solution.py:116
  667.0 4.8 all-to-all-start.10
  687.4 4.6 multiply_subtract_fusion.1
  697.2 6.8 all-to-all-done.10
  710.1 5.5 convolution_convert_fusion.8
  717.3 4.1 fusion.19
  724.7 11.6 %multiply_subtract_fusion = (f32[72,18432]{1,0:T(8,128)}, f32[72,18432]{1,0:T(8,128)}, f32[72,18432]{1,0:T(8,128)}) fusion(f32[72,18432]{1,0:T(8,128)S(1)} %bitcast.238, bf16[72,9216]{1,0:T(8,128)(2,1)S(1)} %bitcast.256, bf16[72,9216]{1,0:T(8,128)(2,1)S(1)} %bitcast.255, f32[72,18432]{1,0:T(8,128)} %param.33, f32[72,18432]{1,0:T(8,128)} %param.28), kind=kLoop, calls=%fused_computation.21 | loop fusion | flops 25214976 | bytes 34504704 | tf_op jit(solution)/shard_map/sub | solution.py:92
  739.7 10.2 %all-to-all-done.9 = bf16[32,72,256]{2,1,0:T(8,128)(2,1)} async-done(((bf16[32,72,256]{2,1,0:T(8,128)(2,1)}), bf16[32,72,256]{2,1,0:T(8,128)(2,1)}, u32[]{:S(2)}, u32[]{:S(2)}) %all-to-all-start.9) | async-done | bytes 1179680 | tf_op jit(solution)/shard_map/all_to_all | solution.py:434
  756.7 15.8 %reduce-scatter.9.cloned.1.call-done = bf16[576,512]{1,0:T(8,128)(2,1)} async-done(((bf16[2304,512]{1,0:T(8,128)(2,1)}), bf16[576,512]{1,0:T(8,128)(2,1)}) %reduce-scatter.9.cloned.1.call-update) | async-done | bytes 589840 | tf_op jit(solution)/shard_map/reduce_scatter | solution.py:116
  772.5 4.2 all-to-all-start.8
  779.6 7.5 all-to-all-done.8
  791.5 3.9 all-to-all-start.11
  795.5 4.0 multiply_subtract_fusion.2
  (401 shorter events, 200.3 us)
Async XLA Ops:
  7.2 80.9 %all-gather.12.cloned.1.call-start = ((), (), s32[]{:S(2)}) async-start(), calls=%async_computation.23 | async-start | bytes 5308416 | tf_op jit(solution)/shard_map/all_gather | solution.py:112
  12.8 67.0 %all-to-all-start = ((bf16[8,72,2304]{2,1,0:T(8,128)(2,1)}), bf16[8,72,2304]{2,1,0:T(8,128)(2,1)S(1)}, u32[]{:S(2)}, u32[]{:S(2)}) async-start(bf16[8,72,2304]{2,1,0:T(8,128)(2,1)} %maximum_bitcast_fusion), calls=%async_computation | async-start | bytes 5308416 | tf_op jit(solution)/shard_map/all_to_all | solution.py:234
  84.0 62.1 %all-to-all-start.1 = ((bf16[32,80,512]{2,1,0:T(8,128)(2,1)}), bf16[32,80,512]{2,1,0:T(8,128)(2,1)S(1)}, u32[]{:S(2)}, u32[]{:S(2)}) async-start(bf16[32,80,512]{2,1,0:T(8,128)(2,1)} %bitcast.248), calls=%async_computation.1 | async-start | bytes 5242880 | tf_op jit(solution)/shard_map/all_to_all | solution.py:304
  87.2 158.1 %all-gather.6.cloned.1.call-start = ((), (), s32[]{:S(2)}) async-start(), calls=%async_computation.16 | async-start | bytes 13271040 | tf_op jit(solution)/shard_map/all_gather | solution.py:112
  87.9 76.5 %copy-start.67 = (f32[128]{0:T(128)}, f32[128]{0:T(128)S(1)}, u32[]{:S(2)}) copy-start(f32[128]{0:T(128)S(1)} %multiply_power_fusion) | copy-start | bytes 1540
  88.1 76.4 %copy-start.57 = (f32[1024]{0:T(1024)}, f32[1024]{0:T(1024)S(1)}, u32[]{:S(2)}) copy-start(f32[1024]{0:T(1024)S(1)} %get-tuple-element.103) | copy-start | bytes 12292
  88.1 96.1 %copy-start.55 = (s32[1024]{0:T(1024)}, s32[1024]{0:T(1024)S(1)}, u32[]{:S(2)}) copy-start(s32[1024]{0:T(1024)S(1)} %get-tuple-element.102) | copy-start | bytes 12292
  88.1 60.3 %copy-start.33 = (f32[72,2048]{1,0:T(8,128)S(1)}, f32[72,2048]{1,0:T(8,128)}, u32[]{:S(2)}) copy-start(f32[72,2048]{1,0:T(8,128)} %param.22) | copy-start | bytes 1769476
  91.5 71.1 %copy-start.69 = (f32[1024]{0:T(1024)}, f32[1024]{0:T(1024)S(1)}, u32[]{:S(2)}) copy-start(f32[1024]{0:T(1024)S(1)} %add_rsqrt_fusion) | copy-start | bytes 12292
  149.7 32.6 %all-to-all-start.2 = ((bf16[32,72,256]{2,1,0:T(8,128)(2,1)}), bf16[32,72,256]{2,1,0:T(8,128)(2,1)}, u32[]{:S(2)}, u32[]{:S(2)}) async-start(bf16[32,72,256]{2,1,0:T(8,128)(2,1)} %bitcast.269), calls=%async_computation.2 | async-start | bytes 2359296 | tf_op jit(solution)/shard_map/all_to_all | solution.py:304
  162.2 4.6 collective-permute-start
  194.4 7.7 collective-permute-start.1
  197.4 36.4 %all-to-all-start.3 = ((bf16[8,72,1152]{2,1,0:T(8,128)(2,1)}), bf16[8,72,1152]{2,1,0:T(8,128)(2,1)}, u32[]{:S(2)}, u32[]{:S(2)}) async-start(bf16[8,72,1152]{2,1,0:T(8,128)(2,1)} %bitcast.234), calls=%async_computation.3 | async-start | bytes 2654208 | tf_op jit(solution)/shard_map/all_to_all | solution.py:234
  201.7 107.4 %all-gather.8.cloned.1.call-start = ((), (), s32[]{:S(2)}) async-start(), calls=%async_computation.17 | async-start | bytes 5308416 | tf_op jit(solution)/shard_map/all_gather | solution.py:112
  207.1 16.2 %collective-permute-start.2 = (bf16[64,2304]{1,0:T(8,128)(2,1)}, bf16[64,2304]{1,0:T(8,128)(2,1)S(1)}, u32[]{:S(2)}, u32[]{:S(2)}) collective-permute-start(bf16[64,2304]{1,0:T(8,128)(2,1)} %get-tuple-element.67), channel_id=1, source_target_pairs={{0,8},{8,0},{1,9},{9,1},{2,10},{10,2},{3,11},{11,3},{4,12},{12,4},... | collective-permute-start | bytes 884744 | tf_op jit(solution)/shard_map/ppermute | solution.py:120
  208.5 16.0 %collective-permute-start.4 = (bf16[64,2304]{1,0:T(8,128)(2,1)S(1)}, bf16[64,2304]{1,0:T(8,128)(2,1)}, u32[]{:S(2)}, u32[]{:S(2)}) collective-permute-start(bf16[64,2304]{1,0:T(8,128)(2,1)S(1)} %get-tuple-element.68), channel_id=1, source_target_pairs={{0,16},{16,0},{1,17},{17,1},{2,18},{18,2},{3,19},{19,3},{4,20},{20... | collective-permute-start | bytes 884744 | tf_op jit(solution)/shard_map/ppermute | solution.py:120
  226.5 17.1 %collective-permute-start.5 = (bf16[128,2304]{1,0:T(8,128)(2,1)}, bf16[128,2304]{1,0:T(8,128)(2,1)}, u32[]{:S(2)}, u32[]{:S(2)}) collective-permute-start(bf16[128,2304]{1,0:T(8,128)(2,1)} %pad_maximum_fusion.2), channel_id=1, source_target_pairs={{0,8},{8,0},{1,9},{9,1},{2,10},{10,2},{3,11},{11,3},{4,12},{12,4},... | collective-permute-start | bytes 1769480 | tf_op jit(solution)/shard_map/ppermute | solution.py:120
  227.1 16.5 %collective-permute-start.3 = (bf16[128,2304]{1,0:T(8,128)(2,1)S(1)}, bf16[128,2304]{1,0:T(8,128)(2,1)S(1)}, u32[]{:S(2)}, u32[]{:S(2)}) collective-permute-start(bf16[128,2304]{1,0:T(8,128)(2,1)S(1)} %pad_maximum_fusion.1), channel_id=1, source_target_pairs={{0,16},{16,0},{1,17},{17,1},{2,18},{18,2},{3,19},{19,3},{4,20},{20... | collective-permute-start | bytes 1769480 | tf_op jit(solution)/shard_map/ppermute | solution.py:120
  254.5 16.6 %collective-permute-start.6 = (bf16[288,1152]{1,0:T(8,128)(2,1)}, bf16[288,1152]{1,0:T(8,128)(2,1)S(1)}, u32[]{:S(2)}, u32[]{:S(2)}) collective-permute-start(bf16[288,1152]{1,0:T(8,128)(2,1)} %get-tuple-element.76), channel_id=1, source_target_pairs={{0,8},{8,0},{1,9},{9,1},{2,10},{10,2},{3,11},{11,3},{4,12},{12,4},... | collective-permute-start | bytes 1990664 | tf_op jit(solution)/shard_map/ppermute | solution.py:120
  255.8 19.4 %collective-permute-start.8 = (bf16[288,1152]{1,0:T(8,128)(2,1)}, bf16[288,1152]{1,0:T(8,128)(2,1)}, u32[]{:S(2)}, u32[]{:S(2)}) collective-permute-start(bf16[288,1152]{1,0:T(8,128)(2,1)} %get-tuple-element.75), channel_id=1, source_target_pairs={{0,16},{16,0},{1,17},{17,1},{2,18},{18,2},{3,19},{19,3},{4,20},{20... | collective-permute-start | bytes 1990664 | tf_op jit(solution)/shard_map/ppermute | solution.py:120
  273.7 30.1 %collective-permute-start.7 = (bf16[2,288,1152]{2,1,0:T(8,128)(2,1)}, bf16[2,288,1152]{2,1,0:T(8,128)(2,1)}, u32[]{:S(2)}, u32[]{:S(2)}) collective-permute-start(bf16[2,288,1152]{2,1,0:T(8,128)(2,1)} %maximum_select_fusion.3), channel_id=1, source_target_pairs={{0,16},{16,0},{1,17},{17,1},{2,18},{18,2},{3,19},{19,3},{4,20},{20... | collective-permute-start | bytes 3981320 | tf_op jit(solution)/shard_map/ppermute | solution.py:120
  277.4 29.9 %collective-permute-start.9 = (bf16[2,288,1152]{2,1,0:T(8,128)(2,1)S(1)}, bf16[2,288,1152]{2,1,0:T(8,128)(2,1)S(1)}, u32[]{:S(2)}, u32[]{:S(2)}) collective-permute-start(bf16[2,288,1152]{2,1,0:T(8,128)(2,1)S(1)} %maximum_select_fusion.5), channel_id=1, source_target_pairs={{0,8},{8,0},{1,9},{9,1},{2,10},{10,2},{3,11},{11,3},{4,12},{12,4},... | collective-permute-start | bytes 3981320 | tf_op jit(solution)/shard_map/ppermute | solution.py:120
  335.9 5.0 collective-permute-start.10
  342.9 59.3 %all-to-all-start.4 = ((bf16[4,128,2304]{2,1,0:T(8,128)(2,1)}), bf16[4,128,2304]{2,1,0:T(8,128)(2,1)}, u32[]{:S(2)}, u32[]{:S(2)}) async-start(bf16[4,128,2304]{2,1,0:T(8,128)(2,1)} %bitcast.249), calls=%async_computation.4 | async-start | bytes 4718592 | tf_op jit(solution)/shard_map/all_to_all | solution.py:228
  347.4 109.8 %all-gather.10.cloned.1.call-start = ((), (), s32[]{:S(2)}) async-start(), calls=%async_computation.18 | async-start | bytes 5308416 | tf_op jit(solution)/shard_map/all_gather | solution.py:112
  407.1 122.8 %reduce-scatter.5.cloned.1.call-start = ((), (), s32[]{:S(2)}) async-start(), calls=%async_computation.19 | async-start | bytes 6635520 | tf_op jit(solution)/shard_map/reduce_scatter | solution.py:116
  467.6 151.6 %reduce-scatter.7.cloned.1.call-start = ((), (), s32[]{:S(2)}) async-start(), calls=%async_computation.20 | async-start | bytes 6635520 | tf_op jit(solution)/shard_map/reduce_scatter | solution.py:116
  494.5 4.6 collective-permute-start.11
  510.8 59.0 %all-to-all-start.5 = ((bf16[4,128,2304]{2,1,0:T(8,128)(2,1)}), bf16[4,128,2304]{2,1,0:T(8,128)(2,1)}, u32[]{:S(2)}, u32[]{:S(2)}) async-start(bf16[4,128,2304]{2,1,0:T(8,128)(2,1)} %bitcast.254), calls=%async_computation.5 | async-start | bytes 4718592 | tf_op jit(solution)/shard_map/all_to_all | solution.py:228
  515.3 151.7 %reduce-scatter.11.cloned.1.call-start = ((), (), s32[]{:S(2)}) async-start(), calls=%async_computation.22 | async-start | bytes 6635520 | tf_op jit(solution)/shard_map/reduce_scatter | solution.py:116
  575.6 15.0 %collective-permute-start.12 = (bf16[64,2304]{1,0:T(8,128)(2,1)S(1)}, bf16[64,2304]{1,0:T(8,128)(2,1)S(1)}, u32[]{:S(2)}, u32[]{:S(2)}) collective-permute-start(bf16[64,2304]{1,0:T(8,128)(2,1)S(1)} %get-tuple-element.96), channel_id=1, source_target_pairs={{0,8},{8,0},{1,9},{9,1},{2,10},{10,2},{3,11},{11,3},{4,12},{12,4},... | collective-permute-start | bytes 884744 | tf_op jit(solution)/shard_map/ppermute | solution.py:120
  578.2 36.4 %all-to-all-start.6 = ((bf16[8,72,1152]{2,1,0:T(8,128)(2,1)}), bf16[8,72,1152]{2,1,0:T(8,128)(2,1)}, u32[]{:S(2)}, u32[]{:S(2)}) async-start(bf16[8,72,1152]{2,1,0:T(8,128)(2,1)} %bitcast.70), calls=%async_computation.7 | async-start | bytes 2654208 | tf_op jit(solution)/shard_map/all_to_all | solution.py:241
  582.5 16.2 %collective-permute-start.14 = (bf16[64,2304]{1,0:T(8,128)(2,1)S(1)}, bf16[64,2304]{1,0:T(8,128)(2,1)S(1)}, u32[]{:S(2)}, u32[]{:S(2)}) collective-permute-start(bf16[64,2304]{1,0:T(8,128)(2,1)S(1)} %get-tuple-element.95), channel_id=1, source_target_pairs={{0,16},{16,0},{1,17},{17,1},{2,18},{18,2},{3,19},{19,3},{4,20},{20... | collective-permute-start | bytes 884744 | tf_op jit(solution)/shard_map/ppermute | solution.py:120
  590.6 20.6 %collective-permute-start.13 = (bf16[2,64,2304]{2,1,0:T(8,128)(2,1)S(1)}, bf16[2,64,2304]{2,1,0:T(8,128)(2,1)S(1)}, u32[]{:S(2)}, u32[]{:S(2)}) collective-permute-start(bf16[2,64,2304]{2,1,0:T(8,128)(2,1)S(1)} %maximum_select_fusion.10), channel_id=1, source_target_pairs={{0,16},{16,0},{1,17},{17,1},{2,18},{18,2},{3,19},{19,3},{4,20},{20... | collective-permute-start | bytes 1769480 | tf_op jit(solution)/shard_map/ppermute | solution.py:120
  598.7 14.8 %collective-permute-start.15 = (bf16[2,64,2304]{2,1,0:T(8,128)(2,1)S(1)}, bf16[2,64,2304]{2,1,0:T(8,128)(2,1)S(1)}, u32[]{:S(2)}, u32[]{:S(2)}) collective-permute-start(bf16[2,64,2304]{2,1,0:T(8,128)(2,1)S(1)} %maximum_select_fusion.12), channel_id=1, source_target_pairs={{0,8},{8,0},{1,9},{9,1},{2,10},{10,2},{3,11},{11,3},{4,12},{12,4},... | collective-permute-start | bytes 1769480 | tf_op jit(solution)/shard_map/ppermute | solution.py:120
  618.3 5.6 collective-permute-start.16
  619.2 47.8 %all-to-all-start.7 = ((bf16[8,72,1152]{2,1,0:T(8,128)(2,1)}), bf16[8,72,1152]{2,1,0:T(8,128)(2,1)}, u32[]{:S(2)}, u32[]{:S(2)}) async-start(bf16[8,72,1152]{2,1,0:T(8,128)(2,1)} %bitcast.281), calls=%async_computation.9 | async-start | bytes 2654208 | tf_op jit(solution)/shard_map/all_to_all | solution.py:241
  641.3 32.5 %collective-permute-start.17 = (f32[1024,256]{0,1:T(8,128)}, f32[1024,256]{0,1:T(8,128)}, u32[]{:S(2)}, u32[]{:S(2)}) collective-permute-start(f32[1024,256]{0,1:T(8,128)} %get-tuple-element.108), channel_id=1, source_target_pairs={{0,4},{4,0},{1,5},{5,1},{2,6},{6,2},{3,7},{7,3},{8,12},{12,8},{9,1... | collective-permute-start | bytes 3145736 | tf_op jit(solution)/shard_map/ppermute | solution.py:120
  667.0 37.0 %all-to-all-start.10 = ((bf16[8,72,1152]{2,1,0:T(8,128)(2,1)}), bf16[8,72,1152]{2,1,0:T(8,128)(2,1)}, u32[]{:S(2)}, u32[]{:S(2)}) async-start(bf16[8,72,1152]{2,1,0:T(8,128)(2,1)} %bitcast.280), calls=%async_computation.14 | async-start | bytes 2654208 | tf_op jit(solution)/shard_map/all_to_all | solution.py:241
  686.9 30.4 %collective-permute-start.18 = (bf16[4,128,2304]{2,1,0:T(8,128)(2,1)}, bf16[4,128,2304]{2,1,0:T(8,128)(2,1)}, u32[]{:S(2)}, u32[]{:S(2)}) collective-permute-start(bf16[4,128,2304]{2,1,0:T(8,128)(2,1)} %select_bitcast_fusion), channel_id=1, source_target_pairs={{0,4},{4,0},{1,5},{5,1},{2,6},{6,2},{3,7},{7,3},{8,12},{12,8},{9,1... | collective-permute-start | bytes 7077896 | tf_op jit(solution)/shard_map/ppermute | solution.py:120
  704.0 45.9 %all-to-all-start.9 = ((bf16[32,72,256]{2,1,0:T(8,128)(2,1)}), bf16[32,72,256]{2,1,0:T(8,128)(2,1)}, u32[]{:S(2)}, u32[]{:S(2)}) async-start(bf16[32,72,256]{2,1,0:T(8,128)(2,1)} %bitcast.89), calls=%async_computation.12 | async-start | bytes 2359296 | tf_op jit(solution)/shard_map/all_to_all | solution.py:434
  707.5 65.0 %reduce-scatter.9.cloned.1.call-start = ((), (), s32[]{:S(2)}) async-start(), calls=%async_computation.21 | async-start | bytes 2949120 | tf_op jit(solution)/shard_map/reduce_scatter | solution.py:116
  721.5 14.7 %collective-permute-start.19 = (bf16[64,2304]{1,0:T(8,128)(2,1)S(1)}, bf16[64,2304]{1,0:T(8,128)(2,1)S(1)}, u32[]{:S(2)}, u32[]{:S(2)}) collective-permute-start(bf16[64,2304]{1,0:T(8,128)(2,1)S(1)} %get-tuple-element.61), channel_id=1, source_target_pairs={{0,8},{8,0},{1,9},{9,1},{2,10},{10,2},{3,11},{11,3},{4,12},{12,4},... | collective-permute-start | bytes 884744 | tf_op jit(solution)/shard_map/ppermute | solution.py:120
  723.1 13.1 %collective-permute-start.21 = (bf16[64,2304]{1,0:T(8,128)(2,1)S(1)}, bf16[64,2304]{1,0:T(8,128)(2,1)S(1)}, u32[]{:S(2)}, u32[]{:S(2)}) collective-permute-start(bf16[64,2304]{1,0:T(8,128)(2,1)S(1)} %get-tuple-element.62), channel_id=1, source_target_pairs={{0,16},{16,0},{1,17},{17,1},{2,18},{18,2},{3,19},{19,3},{4,20},{20... | collective-permute-start | bytes 884744 | tf_op jit(solution)/shard_map/ppermute | solution.py:120
  737.3 17.2 %collective-permute-start.22 = (bf16[128,2304]{1,0:T(8,128)(2,1)}, bf16[128,2304]{1,0:T(8,128)(2,1)}, u32[]{:S(2)}, u32[]{:S(2)}) collective-permute-start(bf16[128,2304]{1,0:T(8,128)(2,1)} %pad_maximum_fusion.4), channel_id=1, source_target_pairs={{0,8},{8,0},{1,9},{9,1},{2,10},{10,2},{3,11},{11,3},{4,12},{12,4},... | collective-permute-start | bytes 1769480 | tf_op jit(solution)/shard_map/ppermute | solution.py:120
  739.1 15.6 %collective-permute-start.20 = (bf16[128,2304]{1,0:T(8,128)(2,1)}, bf16[128,2304]{1,0:T(8,128)(2,1)}, u32[]{:S(2)}, u32[]{:S(2)}) collective-permute-start(bf16[128,2304]{1,0:T(8,128)(2,1)} %pad_maximum_fusion.3), channel_id=1, source_target_pairs={{0,16},{16,0},{1,17},{17,1},{2,18},{18,2},{3,19},{19,3},{4,20},{20... | collective-permute-start | bytes 1769480 | tf_op jit(solution)/shard_map/ppermute | solution.py:120
  772.5 14.7 %all-to-all-start.8 = ((bf16[8,72,512]{2,1,0:T(8,128)(2,1)}), bf16[8,72,512]{2,1,0:T(8,128)(2,1)}, u32[]{:S(2)}, u32[]{:S(2)}) async-start(bf16[8,72,512]{2,1,0:T(8,128)(2,1)} %bitcast.298), calls=%async_computation.11 | async-start | bytes 1179648 | tf_op jit(solution)/shard_map/all_to_all | solution.py:241
  791.5 11.4 %all-to-all-start.11 = ((f32[32,4,72]{2,1,0:T(4,128)}), f32[32,4,72]{2,1,0:T(4,128)S(1)}, u32[]{:S(2)}, u32[]{:S(2)}) async-start(f32[32,4,72]{2,1,0:T(4,128)} %fusion.96), calls=%async_computation.15 | async-start | bytes 131072 | tf_op jit(solution)/shard_map/all_to_all | solution.py:454
  (78 other events, 449.3 us)
Sparse Core Ops, SparseCore 0:
  9.9 41.6 all-gather.11
  90.4 142.7 all-gather.5
  249.2 51.7 all-gather.7
  407.2 49.8 all-gather.9
  467.7 60.7 reduce-scatter.4
  532.0 68.7 reduce-scatter.6
  604.3 62.6 reduce-scatter.10
  717.4 55.0 reduce-scatter.8

commit v4 on v3

--- a/solution.py
+++ b/solution.py
@@ -1,6 +1,8 @@
 import jax
 import jax.numpy as jnp
 from jax import lax
+from jax.experimental import pallas as pl
+from jax.experimental.pallas import tpu as pltpu
 from jax.sharding import Mesh
 from jax.sharding import PartitionSpec as P
 
@@ -108,6 +110,156 @@
     return lax.dot_general(left, right, (((0,), (0,)), ((), ())), preferred_element_type=jnp.float32)
 
 
+def scores(query_rows, keys, row_positions, key_positions):
+    raw = dot_t(query_rows, keys) * (HEAD_DIM ** (-0.5) / SOFT_CAP)
+    tanh_part = jnp.tanh(raw)
+    return jnp.where(key_positions <= row_positions, SOFT_CAP * tanh_part, -1e30), tanh_part
+
+
+def attend_kernel(q_ref, k_ref, v_ref, row_ref, key_ref, out_ref, total_ref):
+    capped, _ = scores(q_ref[...], k_ref[...], row_ref[...], key_ref[...])
+    top_score = jnp.max(capped, -1, keepdims=True)
+    exp_scores = jnp.exp(capped - top_score)
+    exp_total = jnp.sum(exp_scores, -1, keepdims=True)
+    probs = low(exp_scores * (1.0 / exp_total))
+    out_ref[...] = low(dot(probs, v_ref[...]))
+    total_ref[...] = top_score + jnp.log(exp_total)
+
+
+def attend_back_kernel(
+    core_ref, q_ref, k_ref, v_ref, grad_ref, total_ref, row_ref, key_ref, cos_ref, sin_ref,
+    grad_q_ref, mine_ref, sent_ref, key_sum, value_sum,
+):
+    step = pl.program_id(0)
+    query_rows, keys, grad_rows = q_ref[...], k_ref[...], grad_ref[...]
+    capped, tanh_part = scores(query_rows, keys, row_ref[...], key_ref[...])
+    probs = jnp.exp(capped - total_ref[...])
+    grad_probs = dot_t(grad_rows, v_ref[...])
+    inner_sum = jnp.sum(probs * grad_probs, -1, keepdims=True)
+    grad_raw = low(probs * (grad_probs - inner_sum) * (1.0 - tanh_part * tanh_part))
+    scale = HEAD_DIM ** (-0.5)
+    grad_q = dot(grad_raw, keys) * scale
+    grad_q_ref[...] = low(rotate(grad_q, cos_ref[...], -sin_ref[...]))
+    key_terms = t_dot(grad_raw, query_rows)
+    value_terms = t_dot(low(probs), grad_rows)
+
+    @pl.when(step == 0)
+    def _():
+        key_sum[...] = key_terms
+        value_sum[...] = value_terms
+
+    @pl.when(step > 0)
+    def _():
+        key_sum[...] += key_terms
+        value_sum[...] += value_terms
+
+    @pl.when(step == pl.num_programs(0) - 1)
+    def _():
+        first = core_ref[0] == 0
+        key_total, value_total = key_sum[...] * scale, value_sum[...]
+        mine_ref[...] = jnp.where(first, key_total, value_total)
+        sent_ref[...] = jnp.where(first, value_total, key_total)
+
+
+def row_block(rows, columns):
+    return pl.BlockSpec((rows, columns), lambda i: (i, 0))
+
+
+def whole_block(rows, columns):
+    return pl.BlockSpec((rows, columns), lambda i: (0, 0))
+
+
+def kernel_params():
+    return pltpu.CompilerParams(
+        dimension_semantics=("arbitrary",), vmem_limit_bytes=48 * 1024 * 1024
+    )
+
+
+def attend(queries, keys, values, row_positions, key_positions):
+    rows, columns = queries.shape
+    length = keys.shape[0]
+    block = min(rows, 256)
+    return pl.pallas_call(
+        attend_kernel,
+        grid=(rows // block,),
+        in_specs=[
+            row_block(block, columns),
+            whole_block(length, columns),
+            whole_block(length, columns),
+            row_block(block, 1),
+            whole_block(1, length),
+        ],
+        out_specs=[row_block(block, columns), row_block(block, 1)],
+        out_shape=[
+            jax.ShapeDtypeStruct((rows, columns), jnp.bfloat16),
+            jax.ShapeDtypeStruct((rows, 1), jnp.float32),
+        ],
+        compiler_params=kernel_params(),
+        cost_estimate=pl.CostEstimate(
+            flops=4 * rows * length * columns,
+            bytes_accessed=4 * (rows + length) * columns,
+            transcendentals=2 * rows * length,
+        ),
+        name="attend",
+    )(queries, keys, values, row_positions[:, None], key_positions[None, :])
+
+
+def attend_back(
+    core_id, queries, keys, values, grads, totals, row_positions, key_positions, cos, sin
+):
+    rows, columns = queries.shape
+    length = keys.shape[0]
+    block = min(rows, 256)
+    return pl.pallas_call(
+        attend_back_kernel,
+        grid=(rows // block,),
+        in_specs=[
+            pl.BlockSpec(memory_space=pltpu.SMEM),
+            row_block(block, columns),
+            whole_block(length, columns),
+            whole_block(length, columns),
+            row_block(block, columns),
+            row_block(block, 1),
+            row_block(block, 1),
+            whole_block(1, length),
+            row_block(block, columns // 2),
+            row_block(block, columns // 2),
+        ],
+        out_specs=[
+            row_block(block, columns),
+            whole_block(length, columns),
+            whole_block(length, columns),
+        ],
+        out_shape=[
+            jax.ShapeDtypeStruct((rows, columns), jnp.bfloat16),
+            jax.ShapeDtypeStruct((length, columns), jnp.float32),
+            jax.ShapeDtypeStruct((length, columns), jnp.float32),
+        ],
+        scratch_shapes=[
+            pltpu.VMEM((length, columns), jnp.float32),
+            pltpu.VMEM((length, columns), jnp.float32),
+        ],
+        compiler_params=kernel_params(),
+        cost_estimate=pl.CostEstimate(
+            flops=10 * rows * length * columns,
+            bytes_accessed=8 * (rows + 2 * length) * columns,
+            transcendentals=2 * rows * length,
+        ),
+        name="attend_back",
+    )(
+        core_id.reshape(1),
+        queries,
+        keys,
+        values,
+        grads,
+        totals,
+        row_positions[:, None],
+        key_positions[None, :],
+        cos,
+        sin,
+    )
+
+
 def gather_rows(piece, axes):
     return lax.all_gather(piece, axes, axis=0, tiled=True)
 
@@ -146,9 +298,10 @@
     half = block.shape[0] // 2
     upper_row = in_order(block[:half], near[0], x_id, 0)
     lower_column = in_order(block[half:], near[1], y_id, 0)
-    upper_all = in_order(upper_row, exchange(upper_row, "y"), y_id, 0)
-    lower_all = in_order(lower_column, exchange(lower_column, "x"), x_id, 1)
-    whole = jnp.concatenate([upper_all, lower_all], 2) + jnp.asarray(zero, block.dtype)
+    late = jnp.asarray(zero, block.dtype)
+    upper_all = in_order(upper_row + late, exchange(upper_row, "y"), y_id, 0)
+    lower_all = in_order(lower_column + late, exchange(lower_column, "x"), x_id, 1)
+    whole = jnp.concatenate([upper_all, lower_all], 2)
     return whole.reshape(4 * block.shape[0], block.shape[1])
 
 
@@ -207,12 +360,11 @@
     return jnp.where(lax.axis_index("core") == 0, first, second)
 
 
-def sum_cores(product, array):
-    half = array.shape[0] // 2
-    first, second = array[:half], array[half:]
-    came = exchange(low(product(my_half(second, first))), "core")
-    mine = lax.optimization_barrier(low(product(my_half(first, second))))
-    return low(mine.astype(jnp.float32) + came.astype(jnp.float32))
+def tensor_terms(terms, zero=0.0):
+    half = terms.shape[0] // 2
+    came = exchange(my_half(terms[half:], terms[:half]), "core")
+    mine = my_half(terms[:half], terms[half:])
+    return low(mine.astype(jnp.float32) + (came.astype(jnp.float32) + zero))
 
 
 def head_terms(terms):
@@ -336,7 +488,7 @@
         return lax.dynamic_slice_in_dim(array, first_row, query_rows, 0)
 
     query_cos, query_sin = query_part(cos_table), query_part(sin_table)
-    allowed = key_positions[None, :] <= query_part(key_positions)[:, None]
+    row_positions = query_part(key_positions)
 
     inputs = tokens[0].astype(jnp.float32)
     normed_one = low(rms_norm(seq_tokens.astype(jnp.float32), gains[0]))
@@ -347,58 +499,90 @@
     kv_other = exchange(kv_mine, "core")
     keys = jnp.where(core_id == 0, kv_mine, kv_other)
     values = jnp.where(core_id == 0, kv_other, kv_mine)
-    tanh_part = jnp.tanh(dot_t(queries, keys) * (scale / SOFT_CAP))
-    capped = jnp.where(allowed, SOFT_CAP * tanh_part, -1e30)
-    top_score = jnp.max(capped, -1, keepdims=True)
-    exp_scores = jnp.exp(capped - top_score)
-    exp_total = jnp.sum(exp_scores, -1, keepdims=True)
-    probs = exp_scores / exp_total
-    probs_low = low(probs)
-    attended = low(dot(probs_low, values) + zero_after(head_out))
+    attended, log_total = attend(queries, keys, values, row_positions, key_positions)
     branch = scatter_plane(head_terms(low(dot_t(attended, head_out))))
     hidden_in = after(inputs, own_gate_up, down_mine) + rms_norm(branch, gains[1])
 
+    part_rows = row_count // 2
+
+    def part(array, index):
+        return array[index * part_rows : (index + 1) * part_rows]
+
     normed_two_mine = low(rms_norm(hidden_in, gains[2]))
-    normed_two = gather_rows(normed_two_mine, TENSOR)
     down_mine = after(down_mine, normed_two_mine)
     down_near = gather_plane_near(down_mine)
-    gate_up = dot(normed_two, own_gate_up)
-    gate_part, up_part = gate_up[:, :ff_own], gate_up[:, ff_own:]
-    own_down = gather_plane_far(down_mine, down_near, zero_after(gate_up))
+    upstream = cotangent[0].astype(jnp.float32)
+
+    def forward_part(gate_up, own_down, zero):
+        activated = low(gated_unit(gate_up[:, :ff_own], gate_up[:, ff_own:]))
+        terms = tensor_terms(low(dot_t(activated, own_down)), zero)
+        return activated, terms, over_fsdp(terms, fsdp_count)
+
+    def factors_of(gate_up, zero):
+        gate_part, up_part = gate_up[:, :ff_own] + zero, gate_up[:, ff_own:] + zero
+        _, pull_back = jax.vjp(gated_unit, gate_part, up_part)
+        factors = pull_back(jnp.ones_like(gate_part))
+        return lax.optimization_barrier(tuple(low(factor) for factor in factors))
+
+    def turn_part(index, pieces, zero):
+        lowered = jnp.sum(pieces.astype(jnp.float32), 0)
+        output = low(part(hidden_in, index) + rms_norm(lowered, gains[3]))
+        grad_lowered, gain = norm_back(lowered, gains[3], part(upstream, index))
+        return output, low(grad_lowered + zero), gain
+
+    def backward_part(grad_lowered, factors, zero, terms_zero):
+        grad_activated = dot(grad_lowered, own_down) + zero
+        grad_gate_up = lax.optimization_barrier(
+            low(jnp.concatenate([grad_activated * factors[0], grad_activated * factors[1]], 1))
+        )
+        terms = tensor_terms(low(dot_t(grad_gate_up, own_gate_up)), terms_zero)
+        return grad_gate_up, terms, over_fsdp(terms, fsdp_count)
+
+    def both(first, second, zero=0.0):
+        whole = jnp.concatenate(lax.optimization_barrier((first, second)), 0)
+        return lax.optimization_barrier(whole + jnp.asarray(zero, whole.dtype))
+
+    rows_one = gather_rows(part(normed_two_mine, 0), TENSOR)
+    rows_two = gather_rows(part(normed_two_mine, 1), TENSOR)
+    product_one = dot(rows_one, own_gate_up)
+    own_down = gather_plane_far(down_mine, down_near, zero_after(product_one))
     if row_parts > 1:
         own_down = gather_rows(own_down, "row")
-    activated = low(gated_unit(gate_part, up_part))
-    lowered_terms = sum_cores(lambda rows: dot_t(rows, own_down), activated)
-    lowered_pieces = over_fsdp(lowered_terms, fsdp_count)
-    later_gate_up = after(gate_up, lowered_terms)
-    _, pull_back = jax.vjp(gated_unit, later_gate_up[:, :ff_own], later_gate_up[:, ff_own:])
-    gate_factor, up_factor = lax.optimization_barrier(pull_back(jnp.ones_like(gate_part)))
-    lowered_pieces = after(lowered_pieces, gate_factor, up_factor)
-    lowered = jnp.sum(lowered_pieces.astype(jnp.float32), 0)
-    output = low(hidden_in + rms_norm(lowered, gains[3]))[None]
-
-    upstream = cotangent[0].astype(jnp.float32)
-    grad_lowered, gain_three = norm_back(lowered, gains[3], upstream)
-    grad_lowered = gather_rows(low(grad_lowered), TENSOR)
-    plane_down = scatter_rows(low(t_dot(grad_lowered, activated)), ("row",) + PLANE)
-    grad_activated = dot(grad_lowered, own_down)
-    grad_gate_up = low(
-        jnp.concatenate([grad_activated * gate_factor, grad_activated * up_factor], 1)
-    )
-    normed_two_halves = low(dot_t(grad_gate_up, own_gate_up))
-    half = normed_two_halves.shape[0] // 2
-    sent = my_half(normed_two_halves[half:], normed_two_halves[:half])
-    normed_two_terms = low(
-        my_half(normed_two_halves[:half], normed_two_halves[half:]).astype(jnp.float32)
-        + exchange(sent, "core").astype(jnp.float32)
-    )
-    normed_two_pieces = over_fsdp(normed_two_terms, fsdp_count)
-    term_gate = low(t_dot(normed_two, after(grad_gate_up[:, :ff_own], normed_two_terms)))
+    activated_one, lowered_terms, pieces_one = forward_part(product_one, own_down, 0.0)
+    output_one, sent_one, gain_three_one = turn_part(0, pieces_one, 0.0)
+    lowered_one = gather_rows(sent_one, TENSOR)
+    product_two = dot(after(rows_two, lowered_terms), own_gate_up)
+    activated_two, lowered_terms, pieces_two = forward_part(
+        product_two, own_down, zero_after(sent_one)
+    )
+    later = zero_after(lowered_terms)
+    factors_one, factors_two = factors_of(product_one, later), factors_of(product_two, later)
+    normed_two = both(rows_one, rows_two, later)
+    activated = both(activated_one, activated_two, later)
+    output_two, sent_two, gain_three_two = turn_part(
+        1, pieces_two, zero_after(normed_two, activated, *factors_one, *factors_two)
+    )
+    lowered_two = gather_rows(sent_two, TENSOR)
+    output = jnp.concatenate([output_one, output_two], 0)[None]
+    gain_three = gain_three_one + gain_three_two
+    gate_up_one, terms_one, back_one = backward_part(
+        lowered_one, factors_one, zero_after(sent_two), 0.0
+    )
+    normed_two_one = jnp.sum(back_one.astype(jnp.float32), 0)
+    grad_lowered = both(lowered_one, lowered_two, zero_after(terms_one))
+    term_down = low(t_dot(grad_lowered, activated))
+    gate_up_two, terms_two, back_two = backward_part(
+        lowered_two, factors_two, zero_after(term_down), zero_after(normed_two_one)
+    )
+
+    plane_down = scatter_rows(term_down, ("row",) + PLANE)
+    grad_gate_up = both(gate_up_one, gate_up_two)
+    term_gate = low(t_dot(normed_two, after(grad_gate_up[:, :ff_own], terms_two)))
     plane_gate = scatter_rows(term_gate, ("row",) + PLANE)
     term_up = low(t_dot(normed_two, after(grad_gate_up[:, ff_own:], term_gate)))
     plane_up = scatter_rows(term_up, ("row",) + PLANE)
-    normed_two_pieces = after(normed_two_pieces, term_up, plane_down)
-    grad_normed_two = jnp.sum(normed_two_pieces.astype(jnp.float32), 0)
+    normed_two_two = jnp.sum(after(back_two, term_up).astype(jnp.float32), 0)
+    grad_normed_two = jnp.concatenate([normed_two_one, normed_two_two], 0)
 
     grad_hidden_part, gain_two = norm_back(hidden_in, gains[2], grad_normed_two)
     grad_hidden = upstream + grad_hidden_part
@@ -409,22 +593,23 @@
     blocks_gate = blocks_back(plane_gate, TENSOR, tensor_parts)
 
     grad_attended = low(dot(grad_branch, head_out))
-    grad_probs = dot_t(grad_attended, values)
-    inner_sum = jnp.sum(probs * grad_probs, -1, keepdims=True)
-    grad_raw = low(probs * (grad_probs - inner_sum) * (1.0 - tanh_part * tanh_part))
-    grad_queries = dot(grad_raw, keys) * scale
-    key_terms = t_dot(grad_raw, queries) * scale
-    value_terms = t_dot(probs_low, grad_attended)
-    kv_terms = jnp.where(core_id == 0, key_terms, value_terms) + exchange(
-        jnp.where(core_id == 0, value_terms, key_terms), "core"
-    )
+    query_back, kv_terms, kv_sent = attend_back(
+        core_id,
+        queries,
+        keys,
+        values,
+        grad_attended,
+        log_total,
+        row_positions,
+        key_positions,
+        query_cos,
+        query_sin,
+    )
+    kv_terms = kv_terms + exchange(kv_sent, "core")
     if row_parts > 1:
         kv_terms = scatter_rows(kv_terms, "row")
     kv_back = jnp.where(core_id == 0, rotate(kv_terms, query_cos, -query_sin), kv_terms)
-    grad_projected = low(
-        jnp.concatenate([rotate(grad_queries, query_cos, -query_sin), kv_back], 1)
-        + zero_after(blocks_gate)
-    )
+    grad_projected = jnp.concatenate([query_back, low(kv_back + zero_after(blocks_gate))], 1)
     grad_normed_one = scatter_plane(head_terms(low(dot_t(grad_projected, head_qkv))))
     grad_input_part, gain_zero = norm_back(inputs, gains[0], grad_normed_one)
     token_grad = low(grad_hidden + grad_input_part)[None]
@@ -437,24 +622,23 @@
         pieces = pieces.reshape((row_parts, HEADS, fsdp_count) + pieces.shape[1:])
         return jnp.swapaxes(jnp.sum(pieces.astype(jnp.float32), (0, 2)), 0, 1)
 
-    out_term = lax.optimization_barrier(low(t_dot(grad_branch, attended)))
-    out_pieces = to_owners(out_term)
-    blocks_up = blocks_back(plane_up, TENSOR, tensor_parts)
     qkv_term = low(t_dot(normed_query, grad_projected))
     if row_parts > 1:
         qkv_term = scatter_rows(qkv_term, "row")
     by_owner = jnp.swapaxes(qkv_term.reshape(HEADS, fsdp_count, own_rows, -1), 0, 1)
     qkv_mine = scatter_rows(by_owner.reshape(qkv_term.shape), "fsdp")
+    out_term = lax.optimization_barrier(low(t_dot(grad_branch, attended)))
+    out_pieces = to_owners(out_term)
+    blocks_up = blocks_back(after(plane_up, qkv_term), TENSOR, tensor_parts)
     qkv_blocks = blocks_back(qkv_mine, HEAD_AXES, HEADS)
     sum_qkv = jnp.swapaxes(qkv_blocks, 0, 1).astype(jnp.float32)
-    grad_out = head_grad(out_pieces).reshape(own_rows, q_width)
-
     gain_terms = jnp.stack([gain_zero, gain_one, gain_two, gain_three], 0)
     gain_terms = jnp.swapaxes(gain_terms.reshape(4, -1, own_rows), 0, 1)
     gain_pieces = lax.all_to_all(
         after(gain_terms, qkv_blocks), EVERY, split_axis=0, concat_axis=0, tiled=True
     )
     grad_gains = jnp.sum(gain_pieces, 0)
+    grad_out = head_grad(out_pieces).reshape(own_rows, q_width)
     kv_sum = sum_qkv[:, :, HEAD_DIM:].reshape(own_rows, KV_HEADS, 2, HEAD_DIM)
     grad_qkv = jnp.concatenate(
         [
@@ -465,7 +649,9 @@
         1,
     )
     grad_down = side_by_side(blocks_down)
-    grad_gate_up_w = jnp.concatenate([side_by_side(blocks_gate), side_by_side(blocks_up)], 1)
+    grad_gate_up_w = jnp.concatenate(
+        [after(side_by_side(blocks_gate), qkv_mine), side_by_side(blocks_up)], 1
+    )
     moment_qkv, square_qkv, new_qkv = adamw(
         w_qkv, first_qkv, second_qkv, grad_qkv, MATRIX_RATE, WEIGHT_DECAY
     )

time: 817 us -> 810 us (level)
  waiting for transfers between devices: 414 us -> 340 us
  other arithmetic: 119 us -> 146 us
  local copies, waits for them, and re-layouts: 58.6 us -> 74.1 us
  Pallas kernels: 0 us -> 11.7 us
  starting transfers between devices: 75.8 us -> 84.5 us
    all_to_all x4, waiting for transfers between devices: 15.2 us -> 70.5 us  [blocks_back(): return lax.all_to_all(blocks, axes, split_axis=0, concat_axis=0, tiled=True)]
    all_gather x4 -> x6, waiting for transfers between devices: 50 us -> 8.98 us  [gather_rows(): return lax.all_gather(piece, axes, axis=0, tiled=True)]
    reduce_scatter x4, waiting for transfers between devices: 35.9 us -> 3.38 us  [scatter_rows(): return lax.psum_scatter(terms, axes, scatter_dimension=0, tiled=True)]
    all_to_all x2 -> x4, waiting for transfers between devices: 77.6 us -> 49 us  [over_fsdp(): lax.all_to_all(blocks, 'fsdp', split_axis=0, concat_axis=0, tiled=True)]
    ppermute x23 -> x25, waiting for transfers between devices: 93.2 us -> 76 us  [exchange(): return lax.ppermute(piece, axis, [(0, 1), (1, 0)])]
    pallas_call x0 -> x2, Pallas kernels: none -> 11.7 us  [the longest x1 7.36 us: attend_back(): pl.pallas_call(attend_back_kernel, grid=(rows // block,), in_specs=[pl.Bl...]
    convert_element_type x13 -> x19, other arithmetic: 19.7 us -> 31.1 us  [low(): return values.astype(jnp.bfloat16)]
    all_to_all x1, waiting for transfers between devices: 10.2 us -> 0.01 us  [to_owners(): lax.all_to_all(blocks, EVERY, split_axis=0, concat_axis=0, tiled=True)]
  transfers between devices with their start and end apart: 43 -> 49, of which waited for: 25 -> 27; matrix products, arithmetic and copies ran while one was open for 28% -> 35% of each run, Pallas kernels for 0% -> 1%
where the time goes in v4:
time: 810 us; the launch traced here: 803 us
  waiting for transfers between devices  340 us (42%)
  other arithmetic  146 us (18%)
  matrix products  112 us (14%)
  starting transfers between devices  84.5 us (10%)
  local copies, waits for them, and re-layouts  74.1 us (9%)
  between operations  35.5 us (4%)
  Pallas kernels  11.7 us (1%)
    ppermute x25, waiting for transfers between devices, exchange(): return lax.ppermute(piece, axis, [(0, 1), (1, 0)])  76 us
    all_to_all x4, waiting for transfers between devices, blocks_back(): return lax.all_to_all(blocks, axes, split_axis=0, concat_axis=0, tiled=True)  70.5 us
    all_to_all x2, waiting for transfers between devices, columns_out(): lax.all_to_all(blocks, axes, split_axis=0, concat_axis=0, tiled=True)  63.5 us
    all_to_all x2, waiting for transfers between devices, to_heads(): lax.all_to_all(copies, EVERY, split_axis=0, concat_axis=0, tiled=True)  63.4 us
    all_to_all x4, waiting for transfers between devices, over_fsdp(): lax.all_to_all(blocks, 'fsdp', split_axis=0, concat_axis=0, tiled=True)  49 us
    dot_general x7, matrix products, dot(): return jnp.dot(left, right, preferred_element_type=jnp.float32)  38.5 us
    dot_general x6, matrix products, dot_t(): lax.dot_general(left, right, (((1,), (1,)), ((), ())), preferred_element_...  36.8 us
    dot_general x5, matrix products, t_dot(): lax.dot_general(left, right, (((0,), (0,)), ((), ())), preferred_element_...  36.3 us
  transfers between devices with their start and end apart: 49, of which 27 were waited for; matrix products, arithmetic and copies ran while one was open for 35% of the time, Pallas kernels for 1%

profile of v4, /device:TPU:0, one launch (start us, length us, event | category | flops | bytes accessed | tf_op | source)
XLA Modules:
  0.0 803.2 jit_solution(7257136098544422133)
XLA Ops:
  12.8 6.5 all-to-all-start
  20.4 59.4 %all-to-all-done = bf16[8,72,2304]{2,1,0:T(8,128)(2,1)} async-done(((bf16[8,72,2304]{2,1,0:T(8,128)(2,1)}), bf16[8,72,2304]{2,1,0:T(8,128)(2,1)}, u32[]{:S(2)}, u32[]{:S(2)}) %all-to-all-start) | async-done | bytes 2654240 | tf_op jit(solution)/shard_map/all_to_all | solution.py:386
  92.3 54.1 %all-to-all-done.1 = bf16[32,80,512]{2,1,0:T(8,128)(2,1)} async-done(((bf16[32,80,512]{2,1,0:T(8,128)(2,1)}), bf16[32,80,512]{2,1,0:T(8,128)(2,1)}, u32[]{:S(2)}, u32[]{:S(2)}) %all-to-all-start.1) | async-done | bytes 2621472 | tf_op jit(solution)/shard_map/all_to_all | solution.py:456
  151.0 4.9 all-to-all-start.2
  168.4 4.4 attend.1
  174.4 9.3 %all-to-all-done.2 = bf16[32,72,256]{2,1,0:T(8,128)(2,1)} async-done(((bf16[32,72,256]{2,1,0:T(8,128)(2,1)}), bf16[32,72,256]{2,1,0:T(8,128)(2,1)}, u32[]{:S(2)}, u32[]{:S(2)}) %all-to-all-start.2) | async-done | bytes 1179680 | tf_op jit(solution)/shard_map/all_to_all | solution.py:456
  195.9 4.3 all-to-all-start.3
  200.2 4.0 fusion.5
  207.8 13.9 %collective-permute-done.2 = bf16[64,2304]{1,0:T(8,128)(2,1)S(1)} collective-permute-done((bf16[64,2304]{1,0:T(8,128)(2,1)S(1)}, bf16[64,2304]{1,0:T(8,128)(2,1)S(1)}, u32[]{:S(2)}, u32[]{:S(2)}) %collective-permute-start.2) | collective-permute-done | bytes 294944 | tf_op jit(solution)/shard_map/ppermute | solution.py:272
  228.2 4.0 all-to-all-done.3
  234.1 9.7 %collective-permute-done.5 = bf16[128,2304]{1,0:T(8,128)(2,1)} collective-permute-done((bf16[128,2304]{1,0:T(8,128)(2,1)}, bf16[128,2304]{1,0:T(8,128)(2,1)}, u32[]{:S(2)}, u32[]{:S(2)}) %collective-permute-start.5) | collective-permute-done | bytes 589856 | tf_op jit(solution)/shard_map/ppermute | solution.py:272
  259.0 14.5 %collective-permute-done.6 = bf16[288,1152]{1,0:T(8,128)(2,1)S(1)} collective-permute-done((bf16[288,1152]{1,0:T(8,128)(2,1)}, bf16[288,1152]{1,0:T(8,128)(2,1)S(1)}, u32[]{:S(2)}, u32[]{:S(2)}) %collective-permute-start.6) | collective-permute-done | bytes 663584 | tf_op jit(solution)/shard_map/ppermute | solution.py:272
  283.4 8.9 %fusion.130 = f32[512,2304]{1,0:T(8,128)S(1)} fusion(bf16[512,2304]{1,0:T(8,128)(2,1)} %all-gather.10.cloned.1.call-done, bf16[2304,2304]{1,0:T(8,128)(2,1)} %all-gather.8.cloned.1.call-done), kind=kOutput, calls=%fused_computation.328 | convolution fusion | flops 5435817984 | bytes 17694720 | tf_op jit(solution)/shard_map/dot_general | solution.py:102
  296.0 10.3 %collective-permute-done.7 = bf16[2,288,1152]{2,1,0:T(8,128)(2,1)} collective-permute-done((bf16[2,288,1152]{2,1,0:T(8,128)(2,1)}, bf16[2,288,1152]{2,1,0:T(8,128)(2,1)}, u32[]{:S(2)}, u32[]{:S(2)}) %collective-permute-start.7) | collective-permute-done | bytes 1327136 | tf_op jit(solution)/shard_map/ppermute | solution.py:272
  327.1 4.5 all-to-all-start.4
  331.7 8.8 %fusion.33 = f32[512,2304]{1,0:T(8,128)S(1)} fusion(bf16[2304,2304]{1,0:T(8,128)(2,1)} %all-gather.8.cloned.1.call-done, bf16[512,2304]{1,0:T(8,128)(2,1)} %all-gather.12.cloned.1.call-done, bf16[]{:T(256)} %bitcast.47), kind=kOutput, calls=%fused_computation.106 | convolution fusion | flops 5436997632 | bytes 17694722 | tf_op jit(solution)/shard_map/dot_general | solution.py:102
  343.5 6.5 convolution_convert_fusion.5
  352.6 7.9 all-to-all-done.4
  377.7 4.3 all-to-all-start.5
  382.0 4.0 multiply_convert_fusion.4
  388.5 3.9 multiply_convert_fusion.5
  395.8 22.4 %all-to-all-done.5 = bf16[4,64,2304]{2,1,0:T(8,128)(2,1)} async-done(((bf16[4,64,2304]{2,1,0:T(8,128)(2,1)}), bf16[4,64,2304]{2,1,0:T(8,128)(2,1)}, u32[]{:S(2)}, u32[]{:S(2)}) %all-to-all-start.5) | async-done | bytes 1179680 | tf_op jit(solution)/shard_map/all_to_all | solution.py:380
  423.7 7.1 multiply_convert_fusion.3
  431.0 10.9 %convolution_convert_fusion.9 = bf16[512,2304]{1,0:T(8,128)(2,1)S(1)} fusion(bf16[512,2304]{1,0:T(8,128)(2,1)S(1)} %pad_maximum_fusion.2, bf16[2304,2304]{1,0:T(8,128)(2,1)} %all-gather.8.cloned.1.call-done), kind=kOutput, calls=%fused_computation.28 | convolution fusion | flops 5436997632 | bytes 15335424 | tf_op jit(solution)/shard_map/dot_general | solution.py:106
  447.6 6.4 all-gather.16.cloned.1.call-done
  457.4 8.1 %convolution_convert_fusion.2 = bf16[2304,1152]{1,0:T(8,128)(2,1)} fusion(bf16[1024,2304]{1,0:T(8,128)(2,1)S(1)} %maximum_add_fusion.1, bf16[1024,1152]{1,0:T(8,128)(2,1)S(1)} %copy-done.59), kind=kOutput, calls=%fused_computation.4 | convolution fusion | flops 5438472192 | bytes 12386304 | tf_op jit(solution)/shard_map/dot_general | solution.py:110
  465.5 4.3 all-to-all-start.6
  472.1 7.1 multiply_convert_fusion.1
  479.4 10.3 %convolution_convert_fusion.8 = bf16[512,2304]{1,0:T(8,128)(2,1)S(1)} fusion(bf16[512,2304]{1,0:T(8,128)(2,1)S(1)} %pad_maximum_fusion.3, bf16[2304,2304]{1,0:T(8,128)(2,1)} %all-gather.8.cloned.1.call-done), kind=kOutput, calls=%fused_computation.27 | convolution fusion | flops 5436997632 | bytes 15335424 | tf_op jit(solution)/shard_map/dot_general | solution.py:106
  506.8 9.8 %convolution_convert_fusion.1 = bf16[2304,1152]{1,0:T(8,128)(2,1)} fusion(bf16[1024,2304]{1,0:T(8,128)(2,1)} %copy-done.41, bf16[1024,2304]{1,0:T(8,128)(2,1)S(1)} %copy-done.42, bf16[]{:T(256)} %bitcast.62), kind=kOutput, calls=%fused_computation.3 | convolution fusion | flops 5439651840 | bytes 12386306 | tf_op jit(solution)/shard_map/dot_general | solution.py:110
  517.8 4.4 all-to-all-start.7
  522.9 10.5 %convolution_convert_fusion = bf16[2304,1152]{1,0:T(8,128)(2,1)} fusion(bf16[1024,2304]{1,0:T(8,128)(2,1)} %copy-done.41, bf16[1024,2304]{1,0:T(8,128)(2,1)} %pad_maximum_fusion.1, bf16[]{:T(256)} %bitcast.63), kind=kOutput, calls=%fused_computation.2 | convolution fusion | flops 5439651840 | bytes 12386816 | tf_op jit(solution)/shard_map/dot_general | solution.py:110
  535.3 15.3 %all-to-all-done.7 = bf16[4,64,2304]{2,1,0:T(8,128)(2,1)} async-done(((bf16[4,64,2304]{2,1,0:T(8,128)(2,1)}), bf16[4,64,2304]{2,1,0:T(8,128)(2,1)}, u32[]{:S(2)}, u32[]{:S(2)}) %all-to-all-start.7) | async-done | bytes 1179680 | tf_op jit(solution)/shard_map/all_to_all | solution.py:380
  557.4 4.3 all-to-all-start.8
  567.1 6.7 collective-permute-done.14
  578.2 15.6 %all-to-all-done.8 = bf16[8,72,1152]{2,1,0:T(8,128)(2,1)} async-done(((bf16[8,72,1152]{2,1,0:T(8,128)(2,1)}), bf16[8,72,1152]{2,1,0:T(8,128)(2,1)}, u32[]{:S(2)}, u32[]{:S(2)}) %all-to-all-start.8) | async-done | bytes 1327136 | tf_op jit(solution)/shard_map/all_to_all | solution.py:393
  595.9 7.3 collective-permute-done.15
  607.9 4.8 all-to-all-start.9
  623.4 7.4 attend_back.1
  635.7 9.2 %all-to-all-done.9 = bf16[8,72,1152]{2,1,0:T(8,128)(2,1)} async-done(((bf16[8,72,1152]{2,1,0:T(8,128)(2,1)}), bf16[8,72,1152]{2,1,0:T(8,128)(2,1)}, u32[]{:S(2)}, u32[]{:S(2)}) %all-to-all-start.9) | async-done | bytes 1327136 | tf_op jit(solution)/shard_map/all_to_all | solution.py:393
  646.8 4.8 convolution_convert_fusion.10
  668.2 4.6 multiply_subtract_fusion.1
  684.7 5.4 all-to-all-start.12
  691.8 4.0 fusion.4
  699.6 5.8 collective-permute-done.21
  709.8 45.7 %all-to-all-done.12 = bf16[8,72,1152]{2,1,0:T(8,128)(2,1)S(1)} async-done(((bf16[8,72,1152]{2,1,0:T(8,128)(2,1)}), bf16[8,72,1152]{2,1,0:T(8,128)(2,1)S(1)}, u32[]{:S(2)}, u32[]{:S(2)}) %all-to-all-start.12) | async-done | bytes 1327136 | tf_op jit(solution)/shard_map/all_to_all | solution.py:393
  772.3 9.6 %multiply_subtract_fusion = (f32[72,18432]{1,0:T(8,128)}, f32[72,18432]{1,0:T(8,128)}, f32[72,18432]{1,0:T(8,128)}) fusion(f32[72,18432]{1,0:T(8,128)S(1)} %bitcast.264, f32[72,18432]{1,0:T(8,128)S(1)} %constant_dynamic-update-slice_fusion.3, f32[72,18432]{1,0:T(8,128)} %param.33, f32[72,18432]{1,0:T(8,128)} %param.28), kind=kLoop, calls=%fused_computation.13 | loop fusion | flops 19906560 | bytes 37158912 | tf_op jit(solution)/shard_map/sub | solution.py:94
  788.1 4.0 multiply_subtract_fusion.2
  (493 shorter events, 264.1 us)
Async XLA Ops:
  7.2 81.6 %all-gather.18.cloned.1.call-start = ((), (), s32[]{:S(2)}) async-start(), calls=%async_computation.27 | async-start | bytes 5308416 | tf_op jit(solution)/shard_map/all_gather | solution.py:264
  12.8 67.1 %all-to-all-start = ((bf16[8,72,2304]{2,1,0:T(8,128)(2,1)}), bf16[8,72,2304]{2,1,0:T(8,128)(2,1)}, u32[]{:S(2)}, u32[]{:S(2)}) async-start(bf16[8,72,2304]{2,1,0:T(8,128)(2,1)} %maximum_bitcast_fusion), calls=%async_computation | async-start | bytes 5308416 | tf_op jit(solution)/shard_map/all_to_all | solution.py:386
  83.9 62.5 %all-to-all-start.1 = ((bf16[32,80,512]{2,1,0:T(8,128)(2,1)}), bf16[32,80,512]{2,1,0:T(8,128)(2,1)}, u32[]{:S(2)}, u32[]{:S(2)}) async-start(bf16[32,80,512]{2,1,0:T(8,128)(2,1)} %bitcast.274), calls=%async_computation.1 | async-start | bytes 5242880 | tf_op jit(solution)/shard_map/all_to_all | solution.py:456
  87.5 158.9 %all-gather.8.cloned.1.call-start = ((), (), s32[]{:S(2)}) async-start(), calls=%async_computation.18 | async-start | bytes 13271040 | tf_op jit(solution)/shard_map/all_gather | solution.py:264
  151.0 32.7 %all-to-all-start.2 = ((bf16[32,72,256]{2,1,0:T(8,128)(2,1)}), bf16[32,72,256]{2,1,0:T(8,128)(2,1)}, u32[]{:S(2)}, u32[]{:S(2)}) async-start(bf16[32,72,256]{2,1,0:T(8,128)(2,1)} %bitcast.13), calls=%async_computation.2 | async-start | bytes 2359296 | tf_op jit(solution)/shard_map/all_to_all | solution.py:456
  163.3 4.3 collective-permute-start
  189.3 10.9 %collective-permute-start.1 = (bf16[4,128,2304]{2,1,0:T(8,128)(2,1)}, bf16[4,128,2304]{2,1,0:T(8,128)(2,1)}, u32[]{:S(2)}, u32[]{:S(2)}) collective-permute-start(bf16[4,128,2304]{2,1,0:T(8,128)(2,1)} %fusion.31), channel_id=1, source_target_pairs={{0,4},{4,0},{1,5},{5,1},{2,6},{6,2},{3,7},{7,3},{8,12},{12,8},{9,1... | collective-permute-start | bytes 7077896 | tf_op jit(solution)/shard_map/ppermute | solution.py:272
  195.9 36.4 %all-to-all-start.3 = ((bf16[8,72,1152]{2,1,0:T(8,128)(2,1)}), bf16[8,72,1152]{2,1,0:T(8,128)(2,1)}, u32[]{:S(2)}, u32[]{:S(2)}) async-start(bf16[8,72,1152]{2,1,0:T(8,128)(2,1)} %bitcast.260), calls=%async_computation.3 | async-start | bytes 2654208 | tf_op jit(solution)/shard_map/all_to_all | solution.py:386
  200.2 83.2 %all-gather.10.cloned.1.call-start = ((), (), s32[]{:S(2)}) async-start(), calls=%async_computation.19 | async-start | bytes 2654208 | tf_op jit(solution)/shard_map/all_gather | solution.py:264
  205.7 16.0 %collective-permute-start.2 = (bf16[64,2304]{1,0:T(8,128)(2,1)S(1)}, bf16[64,2304]{1,0:T(8,128)(2,1)S(1)}, u32[]{:S(2)}, u32[]{:S(2)}) collective-permute-start(bf16[64,2304]{1,0:T(8,128)(2,1)S(1)} %get-tuple-element.103), channel_id=1, source_target_pairs={{0,8},{8,0},{1,9},{9,1},{2,10},{10,2},{3,11},{11,3},{4,12},{12,4},... | collective-permute-start | bytes 884744 | tf_op jit(solution)/shard_map/ppermute | solution.py:272
  207.2 15.9 %collective-permute-start.4 = (bf16[64,2304]{1,0:T(8,128)(2,1)S(1)}, bf16[64,2304]{1,0:T(8,128)(2,1)S(1)}, u32[]{:S(2)}, u32[]{:S(2)}) collective-permute-start(bf16[64,2304]{1,0:T(8,128)(2,1)S(1)} %get-tuple-element.104), channel_id=1, source_target_pairs={{0,16},{16,0},{1,17},{17,1},{2,18},{18,2},{3,19},{19,3},{4,20},{20... | collective-permute-start | bytes 884744 | tf_op jit(solution)/shard_map/ppermute | solution.py:272
  225.1 18.7 %collective-permute-start.5 = (bf16[128,2304]{1,0:T(8,128)(2,1)}, bf16[128,2304]{1,0:T(8,128)(2,1)}, u32[]{:S(2)}, u32[]{:S(2)}) collective-permute-start(bf16[128,2304]{1,0:T(8,128)(2,1)} %pad_maximum_fusion.10), channel_id=1, source_target_pairs={{0,8},{8,0},{1,9},{9,1},{2,10},{10,2},{3,11},{11,3},{4,12},{12,4},... | collective-permute-start | bytes 1769480 | tf_op jit(solution)/shard_map/ppermute | solution.py:272
  226.5 17.3 %collective-permute-start.3 = (bf16[128,2304]{1,0:T(8,128)(2,1)}, bf16[128,2304]{1,0:T(8,128)(2,1)S(1)}, u32[]{:S(2)}, u32[]{:S(2)}) collective-permute-start(bf16[128,2304]{1,0:T(8,128)(2,1)} %pad_maximum_fusion.9), channel_id=1, source_target_pairs={{0,16},{16,0},{1,17},{17,1},{2,18},{18,2},{3,19},{19,3},{4,20},{20... | collective-permute-start | bytes 1769480 | tf_op jit(solution)/shard_map/ppermute | solution.py:272
  251.6 70.2 %all-gather.12.cloned.1.call-start = ((), (), s32[]{:S(2)}) async-start(), calls=%async_computation.20 | async-start | bytes 2654208 | tf_op jit(solution)/shard_map/all_gather | solution.py:264
  256.9 16.6 %collective-permute-start.6 = (bf16[288,1152]{1,0:T(8,128)(2,1)}, bf16[288,1152]{1,0:T(8,128)(2,1)S(1)}, u32[]{:S(2)}, u32[]{:S(2)}) collective-permute-start(bf16[288,1152]{1,0:T(8,128)(2,1)} %get-tuple-element.112), channel_id=1, source_target_pairs={{0,8},{8,0},{1,9},{9,1},{2,10},{10,2},{3,11},{11,3},{4,12},{12,4},... | collective-permute-start | bytes 1990664 | tf_op jit(solution)/shard_map/ppermute | solution.py:272
  258.2 19.4 %collective-permute-start.8 = (bf16[288,1152]{1,0:T(8,128)(2,1)}, bf16[288,1152]{1,0:T(8,128)(2,1)}, u32[]{:S(2)}, u32[]{:S(2)}) collective-permute-start(bf16[288,1152]{1,0:T(8,128)(2,1)} %get-tuple-element.111), channel_id=1, source_target_pairs={{0,16},{16,0},{1,17},{17,1},{2,18},{18,2},{3,19},{19,3},{4,20},{20... | collective-permute-start | bytes 1990664 | tf_op jit(solution)/shard_map/ppermute | solution.py:272
  276.2 30.1 %collective-permute-start.7 = (bf16[2,288,1152]{2,1,0:T(8,128)(2,1)}, bf16[2,288,1152]{2,1,0:T(8,128)(2,1)}, u32[]{:S(2)}, u32[]{:S(2)}) collective-permute-start(bf16[2,288,1152]{2,1,0:T(8,128)(2,1)} %maximum_select_fusion.4), channel_id=1, source_target_pairs={{0,16},{16,0},{1,17},{17,1},{2,18},{18,2},{3,19},{19,3},{4,20},{20... | collective-permute-start | bytes 3981320 | tf_op jit(solution)/shard_map/ppermute | solution.py:272
  280.3 29.8 %collective-permute-start.9 = (bf16[2,288,1152]{2,1,0:T(8,128)(2,1)}, bf16[2,288,1152]{2,1,0:T(8,128)(2,1)}, u32[]{:S(2)}, u32[]{:S(2)}) collective-permute-start(bf16[2,288,1152]{2,1,0:T(8,128)(2,1)} %maximum_select_fusion.6), channel_id=1, source_target_pairs={{0,8},{8,0},{1,9},{9,1},{2,10},{10,2},{3,11},{11,3},{4,12},{12,4},... | collective-permute-start | bytes 3981320 | tf_op jit(solution)/shard_map/ppermute | solution.py:272
  320.2 3.2 collective-permute-start.10
  327.1 33.5 %all-to-all-start.4 = ((bf16[4,64,2304]{2,1,0:T(8,128)(2,1)}), bf16[4,64,2304]{2,1,0:T(8,128)(2,1)}, u32[]{:S(2)}, u32[]{:S(2)}) async-start(bf16[4,64,2304]{2,1,0:T(8,128)(2,1)} %bitcast.292), calls=%async_computation.4 | async-start | bytes 2359296 | tf_op jit(solution)/shard_map/all_to_all | solution.py:380
  331.5 92.2 %all-gather.14.cloned.1.call-start = ((), (), s32[]{:S(2)}) async-start(), calls=%async_computation.21 | async-start | bytes 2654208 | tf_op jit(solution)/shard_map/all_gather | solution.py:264
  352.6 12.6 %collective-permute-start.11 = (bf16[256,2304]{1,0:T(8,128)(2,1)}, bf16[256,2304]{1,0:T(8,128)(2,1)}, u32[]{:S(2)}, u32[]{:S(2)}) collective-permute-start(bf16[256,2304]{1,0:T(8,128)(2,1)} %broadcast_select_fusion.2), channel_id=1, source_target_pairs={{0,4},{4,0},{1,5},{5,1},{2,6},{6,2},{3,7},{7,3},{8,12},{12,8},{9,1... | collective-permute-start | bytes 3538952 | tf_op jit(solution)/shard_map/ppermute | solution.py:272
  377.7 40.5 %all-to-all-start.5 = ((bf16[4,64,2304]{2,1,0:T(8,128)(2,1)}), bf16[4,64,2304]{2,1,0:T(8,128)(2,1)}, u32[]{:S(2)}, u32[]{:S(2)}) async-start(bf16[4,64,2304]{2,1,0:T(8,128)(2,1)} %bitcast.289), calls=%async_computation.5 | async-start | bytes 2359296 | tf_op jit(solution)/shard_map/all_to_all | solution.py:380
  382.0 72.1 %all-gather.16.cloned.1.call-start = ((), (), s32[]{:S(2)}) async-start(), calls=%async_computation.22 | async-start | bytes 2654208 | tf_op jit(solution)/shard_map/all_gather | solution.py:264
  423.4 131.3 %reduce-scatter.5.cloned.1.call-start = ((), (), s32[]{:S(2)}) async-start(), calls=%async_computation.23 | async-start | bytes 6635520 | tf_op jit(solution)/shard_map/reduce_scatter | solution.py:268
  465.5 33.6 %all-to-all-start.6 = ((bf16[4,64,2304]{2,1,0:T(8,128)(2,1)}), bf16[4,64,2304]{2,1,0:T(8,128)(2,1)}, u32[]{:S(2)}, u32[]{:S(2)}) async-start(bf16[4,64,2304]{2,1,0:T(8,128)(2,1)} %bitcast.290), calls=%async_computation.6 | async-start | bytes 2359296 | tf_op jit(solution)/shard_map/all_to_all | solution.py:380
  469.8 138.1 %reduce-scatter.7.cloned.1.call-start = ((), (), s32[]{:S(2)}) async-start(), calls=%async_computation.24 | async-start | bytes 6635520 | tf_op jit(solution)/shard_map/reduce_scatter | solution.py:268
  492.3 9.5 %collective-permute-start.13 = (bf16[256,2304]{1,0:T(8,128)(2,1)}, bf16[256,2304]{1,0:T(8,128)(2,1)}, u32[]{:S(2)}, u32[]{:S(2)}) collective-permute-start(bf16[256,2304]{1,0:T(8,128)(2,1)} %broadcast_select_fusion), channel_id=1, source_target_pairs={{0,4},{4,0},{1,5},{5,1},{2,6},{6,2},{3,7},{7,3},{8,12},{12,8},{9,1... | collective-permute-start | bytes 3538952 | tf_op jit(solution)/shard_map/ppermute | solution.py:272
  517.8 32.8 %all-to-all-start.7 = ((bf16[4,64,2304]{2,1,0:T(8,128)(2,1)}), bf16[4,64,2304]{2,1,0:T(8,128)(2,1)}, u32[]{:S(2)}, u32[]{:S(2)}) async-start(bf16[4,64,2304]{2,1,0:T(8,128)(2,1)} %bitcast.291), calls=%async_computation.7 | async-start | bytes 2359296 | tf_op jit(solution)/shard_map/all_to_all | solution.py:380
  557.4 36.4 %all-to-all-start.8 = ((bf16[8,72,1152]{2,1,0:T(8,128)(2,1)}), bf16[8,72,1152]{2,1,0:T(8,128)(2,1)}, u32[]{:S(2)}, u32[]{:S(2)}) async-start(bf16[8,72,1152]{2,1,0:T(8,128)(2,1)} %bitcast.283), calls=%async_computation.9 | async-start | bytes 2654208 | tf_op jit(solution)/shard_map/all_to_all | solution.py:393
  561.7 120.5 %reduce-scatter.11.cloned.1.call-start = ((), (), s32[]{:S(2)}) async-start(), calls=%async_computation.26 | async-start | bytes 6635520 | tf_op jit(solution)/shard_map/reduce_scatter | solution.py:268
  564.3 9.5 %collective-permute-start.14 = (bf16[64,2304]{1,0:T(8,128)(2,1)}, bf16[64,2304]{1,0:T(8,128)(2,1)S(1)}, u32[]{:S(2)}, u32[]{:S(2)}) collective-permute-start(bf16[64,2304]{1,0:T(8,128)(2,1)} %get-tuple-element.133), channel_id=1, source_target_pairs={{0,8},{8,0},{1,9},{9,1},{2,10},{10,2},{3,11},{11,3},{4,12},{12,4},... | collective-permute-start | bytes 884744 | tf_op jit(solution)/shard_map/ppermute | solution.py:272
  565.8 10.3 %collective-permute-start.16 = (bf16[64,2304]{1,0:T(8,128)(2,1)}, bf16[64,2304]{1,0:T(8,128)(2,1)S(1)}, u32[]{:S(2)}, u32[]{:S(2)}) collective-permute-start(bf16[64,2304]{1,0:T(8,128)(2,1)} %get-tuple-element.132), channel_id=1, source_target_pairs={{0,16},{16,0},{1,17},{17,1},{2,18},{18,2},{3,19},{19,3},{4,20},{20... | collective-permute-start | bytes 884744 | tf_op jit(solution)/shard_map/ppermute | solution.py:272
  574.6 28.5 %collective-permute-start.15 = (bf16[2,64,2304]{2,1,0:T(8,128)(2,1)}, bf16[2,64,2304]{2,1,0:T(8,128)(2,1)}, u32[]{:S(2)}, u32[]{:S(2)}) collective-permute-start(bf16[2,64,2304]{2,1,0:T(8,128)(2,1)} %maximum_select_fusion.12), channel_id=1, source_target_pairs={{0,16},{16,0},{1,17},{17,1},{2,18},{18,2},{3,19},{19,3},{4,20},{20... | collective-permute-start | bytes 1769480 | tf_op jit(solution)/shard_map/ppermute | solution.py:272
  577.0 27.6 %collective-permute-start.17 = (bf16[2,64,2304]{2,1,0:T(8,128)(2,1)}, bf16[2,64,2304]{2,1,0:T(8,128)(2,1)}, u32[]{:S(2)}, u32[]{:S(2)}) collective-permute-start(bf16[2,64,2304]{2,1,0:T(8,128)(2,1)} %maximum_select_fusion.14), channel_id=1, source_target_pairs={{0,8},{8,0},{1,9},{9,1},{2,10},{10,2},{3,11},{11,3},{4,12},{12,4},... | collective-permute-start | bytes 1769480 | tf_op jit(solution)/shard_map/ppermute | solution.py:272
  607.9 7.7 collective-permute-start.18
  607.9 37.0 %all-to-all-start.9 = ((bf16[8,72,1152]{2,1,0:T(8,128)(2,1)}), bf16[8,72,1152]{2,1,0:T(8,128)(2,1)}, u32[]{:S(2)}, u32[]{:S(2)}) async-start(bf16[8,72,1152]{2,1,0:T(8,128)(2,1)} %bitcast.307), calls=%async_computation.11 | async-start | bytes 2654208 | tf_op jit(solution)/shard_map/all_to_all | solution.py:393
  631.6 23.8 %collective-permute-start.19 = (f32[1024,256]{1,0:T(8,128)}, f32[1024,256]{1,0:T(8,128)S(1)}, u32[]{:S(2)}, u32[]{:S(2)}) collective-permute-start(f32[1024,256]{1,0:T(8,128)} %get-tuple-element.50), channel_id=1, source_target_pairs={{0,4},{4,0},{1,5},{5,1},{2,6},{6,2},{3,7},{7,3},{8,12},{12,8},{9,1... | collective-permute-start | bytes 3145736 | tf_op jit(solution)/shard_map/ppermute | solution.py:272
  651.6 33.2 %all-to-all-start.11 = ((bf16[32,72,256]{2,1,0:T(8,128)(2,1)}), bf16[32,72,256]{2,1,0:T(8,128)(2,1)}, u32[]{:S(2)}, u32[]{:S(2)}) async-start(bf16[32,72,256]{2,1,0:T(8,128)(2,1)} %bitcast.309), calls=%async_computation.14 | async-start | bytes 2359296 | tf_op jit(solution)/shard_map/all_to_all | solution.py:619
  655.1 106.7 %reduce-scatter.9.cloned.1.call-start = ((), (), s32[]{:S(2)}) async-start(), calls=%async_computation.25 | async-start | bytes 2949120 | tf_op jit(solution)/shard_map/reduce_scatter | solution.py:268
  666.7 25.1 %collective-permute-start.20 = (bf16[4,128,2304]{2,1,0:T(8,128)(2,1)}, bf16[4,128,2304]{2,1,0:T(8,128)(2,1)}, u32[]{:S(2)}, u32[]{:S(2)}) collective-permute-start(bf16[4,128,2304]{2,1,0:T(8,128)(2,1)} %select_bitcast_fusion), channel_id=1, source_target_pairs={{0,4},{4,0},{1,5},{5,1},{2,6},{6,2},{3,7},{7,3},{8,12},{12,8},{9,1... | collective-permute-start | bytes 7077896 | tf_op jit(solution)/shard_map/ppermute | solution.py:272
  684.7 70.8 %all-to-all-start.12 = ((bf16[8,72,1152]{2,1,0:T(8,128)(2,1)}), bf16[8,72,1152]{2,1,0:T(8,128)(2,1)S(1)}, u32[]{:S(2)}, u32[]{:S(2)}) async-start(bf16[8,72,1152]{2,1,0:T(8,128)(2,1)} %bitcast.104), calls=%async_computation.16 | async-start | bytes 2654208 | tf_op jit(solution)/shard_map/all_to_all | solution.py:393
  695.9 9.4 %collective-permute-start.21 = (bf16[64,2304]{1,0:T(8,128)(2,1)S(1)}, bf16[64,2304]{1,0:T(8,128)(2,1)S(1)}, u32[]{:S(2)}, u32[]{:S(2)}) collective-permute-start(bf16[64,2304]{1,0:T(8,128)(2,1)S(1)} %get-tuple-element.93), channel_id=1, source_target_pairs={{0,8},{8,0},{1,9},{9,1},{2,10},{10,2},{3,11},{11,3},{4,12},{12,4},... | collective-permute-start | bytes 884744 | tf_op jit(solution)/shard_map/ppermute | solution.py:272
  696.3 9.2 %collective-permute-start.23 = (bf16[64,2304]{1,0:T(8,128)(2,1)S(1)}, bf16[64,2304]{1,0:T(8,128)(2,1)S(1)}, u32[]{:S(2)}, u32[]{:S(2)}) collective-permute-start(bf16[64,2304]{1,0:T(8,128)(2,1)S(1)} %get-tuple-element.94), channel_id=1, source_target_pairs={{0,16},{16,0},{1,17},{17,1},{2,18},{18,2},{3,19},{19,3},{4,20},{20... | collective-permute-start | bytes 884744 | tf_op jit(solution)/shard_map/ppermute | solution.py:272
  706.4 51.0 %collective-permute-start.24 = (bf16[128,2304]{1,0:T(8,128)(2,1)}, bf16[128,2304]{1,0:T(8,128)(2,1)S(1)}, u32[]{:S(2)}, u32[]{:S(2)}) collective-permute-start(bf16[128,2304]{1,0:T(8,128)(2,1)} %pad_maximum_fusion.12), channel_id=1, source_target_pairs={{0,8},{8,0},{1,9},{9,1},{2,10},{10,2},{3,11},{11,3},{4,12},{12,4},... | collective-permute-start | bytes 1769480 | tf_op jit(solution)/shard_map/ppermute | solution.py:272
  709.0 48.5 %collective-permute-start.22 = (bf16[128,2304]{1,0:T(8,128)(2,1)}, bf16[128,2304]{1,0:T(8,128)(2,1)S(1)}, u32[]{:S(2)}, u32[]{:S(2)}) collective-permute-start(bf16[128,2304]{1,0:T(8,128)(2,1)} %pad_maximum_fusion.11), channel_id=1, source_target_pairs={{0,16},{16,0},{1,17},{17,1},{2,18},{18,2},{3,19},{19,3},{4,20},{20... | collective-permute-start | bytes 1769480 | tf_op jit(solution)/shard_map/ppermute | solution.py:272
  763.7 18.2 %all-to-all-start.10 = ((bf16[8,72,512]{2,1,0:T(8,128)(2,1)}), bf16[8,72,512]{2,1,0:T(8,128)(2,1)S(1)}, u32[]{:S(2)}, u32[]{:S(2)}) async-start(bf16[8,72,512]{2,1,0:T(8,128)(2,1)} %bitcast.322), calls=%async_computation.13 | async-start | bytes 1179648 | tf_op jit(solution)/shard_map/all_to_all | solution.py:393
  784.6 10.9 %all-to-all-start.13 = ((f32[32,4,72]{2,1,0:T(4,128)}), f32[32,4,72]{2,1,0:T(4,128)S(1)}, u32[]{:S(2)}, u32[]{:S(2)}) async-start(f32[32,4,72]{2,1,0:T(4,128)} %fusion.95), calls=%async_computation.17 | async-start | bytes 131072 | tf_op jit(solution)/shard_map/all_to_all | solution.py:637
  (104 other events, 1022.9 us)
Sparse Core Ops, SparseCore 0:
  9.9 41.6 all-gather.17
  90.1 144.6 all-gather.7
  251.7 31.6 all-gather.9
  285.4 30.7 all-gather.11
  364.7 39.8 all-gather.13
  423.5 30.4 all-gather.15
  465.6 61.0 reduce-scatter.4
  530.3 74.4 reduce-scatter.6
  608.5 73.7 reduce-scatter.10
  684.4 72.8 reduce-scatter.8

commit v5 on v4

--- a/solution.py
+++ b/solution.py
@@ -362,9 +362,10 @@
 
 def tensor_terms(terms, zero=0.0):
     half = terms.shape[0] // 2
-    came = exchange(my_half(terms[half:], terms[:half]), "core")
+    sent = my_half(terms[half:], terms[:half])
+    came = exchange(sent, "core")
     mine = my_half(terms[:half], terms[half:])
-    return low(mine.astype(jnp.float32) + (came.astype(jnp.float32) + zero))
+    return low(mine.astype(jnp.float32) + (came.astype(jnp.float32) + zero)), sent
 
 
 def head_terms(terms):
@@ -515,7 +516,7 @@
 
     def forward_part(gate_up, own_down, zero):
         activated = low(gated_unit(gate_up[:, :ff_own], gate_up[:, ff_own:]))
-        terms = tensor_terms(low(dot_t(activated, own_down)), zero)
+        terms, _ = tensor_terms(low(dot_t(activated, own_down)), zero)
         return activated, terms, over_fsdp(terms, fsdp_count)
 
     def factors_of(gate_up, zero):
@@ -535,8 +536,8 @@
         grad_gate_up = lax.optimization_barrier(
             low(jnp.concatenate([grad_activated * factors[0], grad_activated * factors[1]], 1))
         )
-        terms = tensor_terms(low(dot_t(grad_gate_up, own_gate_up)), terms_zero)
-        return grad_gate_up, terms, over_fsdp(terms, fsdp_count)
+        terms, sent = tensor_terms(low(dot_t(grad_gate_up, own_gate_up)), terms_zero)
+        return grad_gate_up, terms, sent, over_fsdp(terms, fsdp_count)
 
     def both(first, second, zero=0.0):
         whole = jnp.concatenate(lax.optimization_barrier((first, second)), 0)
@@ -565,21 +566,21 @@
     lowered_two = gather_rows(sent_two, TENSOR)
     output = jnp.concatenate([output_one, output_two], 0)[None]
     gain_three = gain_three_one + gain_three_two
-    gate_up_one, terms_one, back_one = backward_part(
+    gate_up_one, terms_one, _, back_one = backward_part(
         lowered_one, factors_one, zero_after(sent_two), 0.0
     )
     normed_two_one = jnp.sum(back_one.astype(jnp.float32), 0)
     grad_lowered = both(lowered_one, lowered_two, zero_after(terms_one))
     term_down = low(t_dot(grad_lowered, activated))
-    gate_up_two, terms_two, back_two = backward_part(
+    gate_up_two, terms_two, halves_sent, back_two = backward_part(
         lowered_two, factors_two, zero_after(term_down), zero_after(normed_two_one)
     )
 
     plane_down = scatter_rows(term_down, ("row",) + PLANE)
     grad_gate_up = both(gate_up_one, gate_up_two)
-    term_gate = low(t_dot(normed_two, after(grad_gate_up[:, :ff_own], terms_two)))
+    term_gate = low(t_dot(normed_two, after(grad_gate_up[:, :ff_own], halves_sent, normed_two_one)))
     plane_gate = scatter_rows(term_gate, ("row",) + PLANE)
-    term_up = low(t_dot(normed_two, after(grad_gate_up[:, ff_own:], term_gate)))
+    term_up = low(t_dot(normed_two, after(grad_gate_up[:, ff_own:], term_gate, terms_two)))
     plane_up = scatter_rows(term_up, ("row",) + PLANE)
     normed_two_two = jnp.sum(after(back_two, term_up).astype(jnp.float32), 0)
     grad_normed_two = jnp.concatenate([normed_two_one, normed_two_two], 0)

time: 810 us -> 809 us (level)
    slice x28 -> x29, local copies, waits for them, and re-layouts: 23.3 us -> 23.7 us  [zero_after(): first = lax.slice(array, (0,) * array.ndim, (1,) * array.ndim).reshape(())]
  transfers between devices with their start and end apart: 49 -> 49, of which waited for: 27 -> 29; matrix products, arithmetic and copies ran while one was open for 35% -> 35% of each run, Pallas kernels for 1% -> 1%
where the time goes in v5:
time: 809 us; the launch traced here: 802 us
  waiting for transfers between devices  338 us (42%)
  other arithmetic  145 us (18%)
  matrix products  112 us (14%)
  starting transfers between devices  84.9 us (10%)
  local copies, waits for them, and re-layouts  74.6 us (9%)
  between operations  36.2 us (4%)
  Pallas kernels  11.7 us (1%)
    ppermute x25, waiting for transfers between devices, exchange(): return lax.ppermute(piece, axis, [(0, 1), (1, 0)])  77.9 us
    all_to_all x4, waiting for transfers between devices, blocks_back(): return lax.all_to_all(blocks, axes, split_axis=0, concat_axis=0, tiled=True)  69.4 us
    all_to_all x2, waiting for transfers between devices, columns_out(): lax.all_to_all(blocks, axes, split_axis=0, concat_axis=0, tiled=True)  63.5 us
    all_to_all x2, waiting for transfers between devices, to_heads(): lax.all_to_all(copies, EVERY, split_axis=0, concat_axis=0, tiled=True)  63.4 us
    all_to_all x4, waiting for transfers between devices, over_fsdp(): lax.all_to_all(blocks, 'fsdp', split_axis=0, concat_axis=0, tiled=True)  48.1 us
    dot_general x7, matrix products, dot(): return jnp.dot(left, right, preferred_element_type=jnp.float32)  38.7 us
    dot_general x5, matrix products, t_dot(): lax.dot_general(left, right, (((0,), (0,)), ((), ())), preferred_element_...  37 us
    dot_general x6, matrix products, dot_t(): lax.dot_general(left, right, (((1,), (1,)), ((), ())), preferred_element_...  36.7 us
  transfers between devices with their start and end apart: 49, of which 29 were waited for; matrix products, arithmetic and copies ran while one was open for 35% of the time, Pallas kernels for 1%

profile of v5, /device:TPU:0, one launch (start us, length us, event | category | flops | bytes accessed | tf_op | source)
XLA Modules:
  0.0 802.2 jit_solution(9536423544730599153)
XLA Ops:
  12.8 6.5 all-to-all-start
  20.4 59.4 %all-to-all-done = bf16[8,72,2304]{2,1,0:T(8,128)(2,1)} async-done(((bf16[8,72,2304]{2,1,0:T(8,128)(2,1)}), bf16[8,72,2304]{2,1,0:T(8,128)(2,1)}, u32[]{:S(2)}, u32[]{:S(2)}) %all-to-all-start) | async-done | bytes 2654240 | tf_op jit(solution)/shard_map/all_to_all | solution.py:387
  92.3 54.1 %all-to-all-done.1 = bf16[32,80,512]{2,1,0:T(8,128)(2,1)} async-done(((bf16[32,80,512]{2,1,0:T(8,128)(2,1)}), bf16[32,80,512]{2,1,0:T(8,128)(2,1)}, u32[]{:S(2)}, u32[]{:S(2)}) %all-to-all-start.1) | async-done | bytes 2621472 | tf_op jit(solution)/shard_map/all_to_all | solution.py:457
  151.0 4.9 all-to-all-start.2
  168.4 4.4 attend.1
  174.4 9.3 %all-to-all-done.2 = bf16[32,72,256]{2,1,0:T(8,128)(2,1)} async-done(((bf16[32,72,256]{2,1,0:T(8,128)(2,1)}), bf16[32,72,256]{2,1,0:T(8,128)(2,1)}, u32[]{:S(2)}, u32[]{:S(2)}) %all-to-all-start.2) | async-done | bytes 1179680 | tf_op jit(solution)/shard_map/all_to_all | solution.py:457
  195.9 4.3 all-to-all-start.3
  200.2 4.0 fusion.5
  207.8 13.9 %collective-permute-done.2 = bf16[64,2304]{1,0:T(8,128)(2,1)S(1)} collective-permute-done((bf16[64,2304]{1,0:T(8,128)(2,1)S(1)}, bf16[64,2304]{1,0:T(8,128)(2,1)S(1)}, u32[]{:S(2)}, u32[]{:S(2)}) %collective-permute-start.2) | collective-permute-done | bytes 294944 | tf_op jit(solution)/shard_map/ppermute | solution.py:272
  228.2 4.0 all-to-all-done.3
  234.1 9.7 %collective-permute-done.5 = bf16[128,2304]{1,0:T(8,128)(2,1)} collective-permute-done((bf16[128,2304]{1,0:T(8,128)(2,1)}, bf16[128,2304]{1,0:T(8,128)(2,1)}, u32[]{:S(2)}, u32[]{:S(2)}) %collective-permute-start.5) | collective-permute-done | bytes 589856 | tf_op jit(solution)/shard_map/ppermute | solution.py:272
  258.9 14.5 %collective-permute-done.6 = bf16[288,1152]{1,0:T(8,128)(2,1)S(1)} collective-permute-done((bf16[288,1152]{1,0:T(8,128)(2,1)}, bf16[288,1152]{1,0:T(8,128)(2,1)S(1)}, u32[]{:S(2)}, u32[]{:S(2)}) %collective-permute-start.6) | collective-permute-done | bytes 663584 | tf_op jit(solution)/shard_map/ppermute | solution.py:272
  283.4 8.9 %fusion.130 = f32[512,2304]{1,0:T(8,128)S(1)} fusion(bf16[512,2304]{1,0:T(8,128)(2,1)} %all-gather.10.cloned.1.call-done, bf16[2304,2304]{1,0:T(8,128)(2,1)} %all-gather.8.cloned.1.call-done), kind=kOutput, calls=%fused_computation.328 | convolution fusion | flops 5435817984 | bytes 17694720 | tf_op jit(solution)/shard_map/dot_general | solution.py:102
  295.9 10.2 %collective-permute-done.7 = bf16[2,288,1152]{2,1,0:T(8,128)(2,1)} collective-permute-done((bf16[2,288,1152]{2,1,0:T(8,128)(2,1)}, bf16[2,288,1152]{2,1,0:T(8,128)(2,1)}, u32[]{:S(2)}, u32[]{:S(2)}) %collective-permute-start.7) | collective-permute-done | bytes 1327136 | tf_op jit(solution)/shard_map/ppermute | solution.py:272
  327.0 4.5 all-to-all-start.4
  331.6 8.8 %fusion.33 = f32[512,2304]{1,0:T(8,128)S(1)} fusion(bf16[2304,2304]{1,0:T(8,128)(2,1)} %all-gather.8.cloned.1.call-done, bf16[512,2304]{1,0:T(8,128)(2,1)} %all-gather.12.cloned.1.call-done, bf16[]{:T(256)} %bitcast.47), kind=kOutput, calls=%fused_computation.106 | convolution fusion | flops 5436997632 | bytes 17694722 | tf_op jit(solution)/shard_map/dot_general | solution.py:102
  343.4 6.5 convolution_convert_fusion.5
  352.5 7.9 all-to-all-done.4
  377.6 4.3 all-to-all-start.5
  381.9 4.0 multiply_convert_fusion.4
  388.4 3.9 multiply_convert_fusion.5
  395.7 22.4 %all-to-all-done.5 = bf16[4,64,2304]{2,1,0:T(8,128)(2,1)} async-done(((bf16[4,64,2304]{2,1,0:T(8,128)(2,1)}), bf16[4,64,2304]{2,1,0:T(8,128)(2,1)}, u32[]{:S(2)}, u32[]{:S(2)}) %all-to-all-start.5) | async-done | bytes 1179680 | tf_op jit(solution)/shard_map/all_to_all | solution.py:381
  423.6 7.1 multiply_convert_fusion.3
  430.9 10.8 %convolution_convert_fusion.9 = bf16[512,2304]{1,0:T(8,128)(2,1)S(1)} fusion(bf16[512,2304]{1,0:T(8,128)(2,1)S(1)} %pad_maximum_fusion.2, bf16[2304,2304]{1,0:T(8,128)(2,1)} %all-gather.8.cloned.1.call-done), kind=kOutput, calls=%fused_computation.28 | convolution fusion | flops 5436997632 | bytes 15335424 | tf_op jit(solution)/shard_map/dot_general | solution.py:106
  447.6 6.3 all-gather.16.cloned.1.call-done
  457.3 8.0 %convolution_convert_fusion.2 = bf16[2304,1152]{1,0:T(8,128)(2,1)} fusion(bf16[1024,2304]{1,0:T(8,128)(2,1)S(1)} %maximum_add_fusion.1, bf16[1024,1152]{1,0:T(8,128)(2,1)S(1)} %copy-done.58), kind=kOutput, calls=%fused_computation.4 | convolution fusion | flops 5438472192 | bytes 12386304 | tf_op jit(solution)/shard_map/dot_general | solution.py:110
  465.4 4.3 all-to-all-start.6
  472.0 7.1 multiply_convert_fusion.1
  483.2 10.3 %convolution_convert_fusion.8 = bf16[512,2304]{1,0:T(8,128)(2,1)S(1)} fusion(bf16[512,2304]{1,0:T(8,128)(2,1)S(1)} %pad_maximum_fusion.3, bf16[2304,2304]{1,0:T(8,128)(2,1)} %all-gather.8.cloned.1.call-done), kind=kOutput, calls=%fused_computation.27 | convolution fusion | flops 5436997632 | bytes 15335424 | tf_op jit(solution)/shard_map/dot_general | solution.py:106
  501.7 10.6 %convolution_convert_fusion.1 = bf16[2304,1152]{1,0:T(8,128)(2,1)} fusion(bf16[1024,2304]{1,0:T(8,128)(2,1)} %copy-done.41, bf16[1024,2304]{1,0:T(8,128)(2,1)} %pad_maximum_fusion.1, bf16[]{:T(256)S(6)} %add.728), kind=kOutput, calls=%fused_computation.3 | convolution fusion | flops 5439651840 | bytes 12386306 | tf_op jit(solution)/shard_map/dot_general | solution.py:110
  519.3 4.5 all-to-all-start.7
  524.5 10.5 %convolution_convert_fusion = bf16[2304,1152]{1,0:T(8,128)(2,1)} fusion(bf16[1024,2304]{1,0:T(8,128)(2,1)} %copy-done.41, bf16[1024,2304]{1,0:T(8,128)(2,1)} %pad_maximum_fusion.1, bf16[]{:T(256)} %bitcast.63), kind=kOutput, calls=%fused_computation.2 | convolution fusion | flops 5439651840 | bytes 12386816 | tf_op jit(solution)/shard_map/dot_general | solution.py:110
  536.8 16.1 %all-to-all-done.7 = bf16[4,64,2304]{2,1,0:T(8,128)(2,1)} async-done(((bf16[4,64,2304]{2,1,0:T(8,128)(2,1)}), bf16[4,64,2304]{2,1,0:T(8,128)(2,1)}, u32[]{:S(2)}, u32[]{:S(2)}) %all-to-all-start.7) | async-done | bytes 1179680 | tf_op jit(solution)/shard_map/all_to_all | solution.py:381
  559.4 4.3 all-to-all-start.8
  569.4 6.5 collective-permute-done.14
  581.2 14.6 %all-to-all-done.8 = bf16[8,72,1152]{2,1,0:T(8,128)(2,1)} async-done(((bf16[8,72,1152]{2,1,0:T(8,128)(2,1)}), bf16[8,72,1152]{2,1,0:T(8,128)(2,1)}, u32[]{:S(2)}, u32[]{:S(2)}) %all-to-all-start.8) | async-done | bytes 1327136 | tf_op jit(solution)/shard_map/all_to_all | solution.py:394
  597.9 6.2 collective-permute-done.15
  608.9 4.9 all-to-all-start.9
  624.4 7.4 attend_back.1
  636.3 9.6 %all-to-all-done.9 = bf16[8,72,1152]{2,1,0:T(8,128)(2,1)} async-done(((bf16[8,72,1152]{2,1,0:T(8,128)(2,1)}), bf16[8,72,1152]{2,1,0:T(8,128)(2,1)}, u32[]{:S(2)}, u32[]{:S(2)}) %all-to-all-start.9) | async-done | bytes 1327136 | tf_op jit(solution)/shard_map/all_to_all | solution.py:394
  647.8 4.8 convolution_convert_fusion.10
  669.2 4.6 multiply_subtract_fusion.1
  684.1 5.1 all-to-all-start.12
  690.9 4.0 fusion.4
  698.8 5.8 collective-permute-done.21
  709.5 45.1 %all-to-all-done.12 = bf16[8,72,1152]{2,1,0:T(8,128)(2,1)S(1)} async-done(((bf16[8,72,1152]{2,1,0:T(8,128)(2,1)}), bf16[8,72,1152]{2,1,0:T(8,128)(2,1)S(1)}, u32[]{:S(2)}, u32[]{:S(2)}) %all-to-all-start.12) | async-done | bytes 1327136 | tf_op jit(solution)/shard_map/all_to_all | solution.py:394
  771.4 9.6 %multiply_subtract_fusion = (f32[72,18432]{1,0:T(8,128)}, f32[72,18432]{1,0:T(8,128)}, f32[72,18432]{1,0:T(8,128)}) fusion(f32[72,18432]{1,0:T(8,128)S(1)} %bitcast.264, f32[72,18432]{1,0:T(8,128)S(1)} %constant_dynamic-update-slice_fusion.3, f32[72,18432]{1,0:T(8,128)} %param.33, f32[72,18432]{1,0:T(8,128)} %param.28), kind=kLoop, calls=%fused_computation.13 | loop fusion | flops 19906560 | bytes 37158912 | tf_op jit(solution)/shard_map/sub | solution.py:94
  787.1 4.0 multiply_subtract_fusion.2
  (494 shorter events, 263.7 us)
Async XLA Ops:
  7.2 81.6 %all-gather.18.cloned.1.call-start = ((), (), s32[]{:S(2)}) async-start(), calls=%async_computation.27 | async-start | bytes 5308416 | tf_op jit(solution)/shard_map/all_gather | solution.py:264
  12.8 67.1 %all-to-all-start = ((bf16[8,72,2304]{2,1,0:T(8,128)(2,1)}), bf16[8,72,2304]{2,1,0:T(8,128)(2,1)}, u32[]{:S(2)}, u32[]{:S(2)}) async-start(bf16[8,72,2304]{2,1,0:T(8,128)(2,1)} %maximum_bitcast_fusion), calls=%async_computation | async-start | bytes 5308416 | tf_op jit(solution)/shard_map/all_to_all | solution.py:387
  83.9 62.5 %all-to-all-start.1 = ((bf16[32,80,512]{2,1,0:T(8,128)(2,1)}), bf16[32,80,512]{2,1,0:T(8,128)(2,1)}, u32[]{:S(2)}, u32[]{:S(2)}) async-start(bf16[32,80,512]{2,1,0:T(8,128)(2,1)} %bitcast.274), calls=%async_computation.1 | async-start | bytes 5242880 | tf_op jit(solution)/shard_map/all_to_all | solution.py:457
  87.5 158.9 %all-gather.8.cloned.1.call-start = ((), (), s32[]{:S(2)}) async-start(), calls=%async_computation.18 | async-start | bytes 13271040 | tf_op jit(solution)/shard_map/all_gather | solution.py:264
  151.0 32.7 %all-to-all-start.2 = ((bf16[32,72,256]{2,1,0:T(8,128)(2,1)}), bf16[32,72,256]{2,1,0:T(8,128)(2,1)}, u32[]{:S(2)}, u32[]{:S(2)}) async-start(bf16[32,72,256]{2,1,0:T(8,128)(2,1)} %bitcast.13), calls=%async_computation.2 | async-start | bytes 2359296 | tf_op jit(solution)/shard_map/all_to_all | solution.py:457
  163.3 4.3 collective-permute-start
  189.3 10.9 %collective-permute-start.1 = (bf16[4,128,2304]{2,1,0:T(8,128)(2,1)}, bf16[4,128,2304]{2,1,0:T(8,128)(2,1)}, u32[]{:S(2)}, u32[]{:S(2)}) collective-permute-start(bf16[4,128,2304]{2,1,0:T(8,128)(2,1)} %fusion.31), channel_id=1, source_target_pairs={{0,4},{4,0},{1,5},{5,1},{2,6},{6,2},{3,7},{7,3},{8,12},{12,8},{9,1... | collective-permute-start | bytes 7077896 | tf_op jit(solution)/shard_map/ppermute | solution.py:272
  195.9 36.4 %all-to-all-start.3 = ((bf16[8,72,1152]{2,1,0:T(8,128)(2,1)}), bf16[8,72,1152]{2,1,0:T(8,128)(2,1)}, u32[]{:S(2)}, u32[]{:S(2)}) async-start(bf16[8,72,1152]{2,1,0:T(8,128)(2,1)} %bitcast.260), calls=%async_computation.3 | async-start | bytes 2654208 | tf_op jit(solution)/shard_map/all_to_all | solution.py:387
  200.2 83.2 %all-gather.10.cloned.1.call-start = ((), (), s32[]{:S(2)}) async-start(), calls=%async_computation.19 | async-start | bytes 2654208 | tf_op jit(solution)/shard_map/all_gather | solution.py:264
  205.7 16.0 %collective-permute-start.2 = (bf16[64,2304]{1,0:T(8,128)(2,1)S(1)}, bf16[64,2304]{1,0:T(8,128)(2,1)S(1)}, u32[]{:S(2)}, u32[]{:S(2)}) collective-permute-start(bf16[64,2304]{1,0:T(8,128)(2,1)S(1)} %get-tuple-element.103), channel_id=1, source_target_pairs={{0,8},{8,0},{1,9},{9,1},{2,10},{10,2},{3,11},{11,3},{4,12},{12,4},... | collective-permute-start | bytes 884744 | tf_op jit(solution)/shard_map/ppermute | solution.py:272
  207.2 15.9 %collective-permute-start.4 = (bf16[64,2304]{1,0:T(8,128)(2,1)S(1)}, bf16[64,2304]{1,0:T(8,128)(2,1)S(1)}, u32[]{:S(2)}, u32[]{:S(2)}) collective-permute-start(bf16[64,2304]{1,0:T(8,128)(2,1)S(1)} %get-tuple-element.104), channel_id=1, source_target_pairs={{0,16},{16,0},{1,17},{17,1},{2,18},{18,2},{3,19},{19,3},{4,20},{20... | collective-permute-start | bytes 884744 | tf_op jit(solution)/shard_map/ppermute | solution.py:272
  225.1 18.7 %collective-permute-start.5 = (bf16[128,2304]{1,0:T(8,128)(2,1)}, bf16[128,2304]{1,0:T(8,128)(2,1)}, u32[]{:S(2)}, u32[]{:S(2)}) collective-permute-start(bf16[128,2304]{1,0:T(8,128)(2,1)} %pad_maximum_fusion.10), channel_id=1, source_target_pairs={{0,8},{8,0},{1,9},{9,1},{2,10},{10,2},{3,11},{11,3},{4,12},{12,4},... | collective-permute-start | bytes 1769480 | tf_op jit(solution)/shard_map/ppermute | solution.py:272
  226.5 17.3 %collective-permute-start.3 = (bf16[128,2304]{1,0:T(8,128)(2,1)}, bf16[128,2304]{1,0:T(8,128)(2,1)S(1)}, u32[]{:S(2)}, u32[]{:S(2)}) collective-permute-start(bf16[128,2304]{1,0:T(8,128)(2,1)} %pad_maximum_fusion.9), channel_id=1, source_target_pairs={{0,16},{16,0},{1,17},{17,1},{2,18},{18,2},{3,19},{19,3},{4,20},{20... | collective-permute-start | bytes 1769480 | tf_op jit(solution)/shard_map/ppermute | solution.py:272
  251.6 70.1 %all-gather.12.cloned.1.call-start = ((), (), s32[]{:S(2)}) async-start(), calls=%async_computation.20 | async-start | bytes 2654208 | tf_op jit(solution)/shard_map/all_gather | solution.py:264
  256.9 16.6 %collective-permute-start.6 = (bf16[288,1152]{1,0:T(8,128)(2,1)}, bf16[288,1152]{1,0:T(8,128)(2,1)S(1)}, u32[]{:S(2)}, u32[]{:S(2)}) collective-permute-start(bf16[288,1152]{1,0:T(8,128)(2,1)} %get-tuple-element.112), channel_id=1, source_target_pairs={{0,8},{8,0},{1,9},{9,1},{2,10},{10,2},{3,11},{11,3},{4,12},{12,4},... | collective-permute-start | bytes 1990664 | tf_op jit(solution)/shard_map/ppermute | solution.py:272
  258.2 19.3 %collective-permute-start.8 = (bf16[288,1152]{1,0:T(8,128)(2,1)}, bf16[288,1152]{1,0:T(8,128)(2,1)}, u32[]{:S(2)}, u32[]{:S(2)}) collective-permute-start(bf16[288,1152]{1,0:T(8,128)(2,1)} %get-tuple-element.111), channel_id=1, source_target_pairs={{0,16},{16,0},{1,17},{17,1},{2,18},{18,2},{3,19},{19,3},{4,20},{20... | collective-permute-start | bytes 1990664 | tf_op jit(solution)/shard_map/ppermute | solution.py:272
  276.1 30.1 %collective-permute-start.7 = (bf16[2,288,1152]{2,1,0:T(8,128)(2,1)}, bf16[2,288,1152]{2,1,0:T(8,128)(2,1)}, u32[]{:S(2)}, u32[]{:S(2)}) collective-permute-start(bf16[2,288,1152]{2,1,0:T(8,128)(2,1)} %maximum_select_fusion.4), channel_id=1, source_target_pairs={{0,16},{16,0},{1,17},{17,1},{2,18},{18,2},{3,19},{19,3},{4,20},{20... | collective-permute-start | bytes 3981320 | tf_op jit(solution)/shard_map/ppermute | solution.py:272
  280.2 29.8 %collective-permute-start.9 = (bf16[2,288,1152]{2,1,0:T(8,128)(2,1)}, bf16[2,288,1152]{2,1,0:T(8,128)(2,1)}, u32[]{:S(2)}, u32[]{:S(2)}) collective-permute-start(bf16[2,288,1152]{2,1,0:T(8,128)(2,1)} %maximum_select_fusion.6), channel_id=1, source_target_pairs={{0,8},{8,0},{1,9},{9,1},{2,10},{10,2},{3,11},{11,3},{4,12},{12,4},... | collective-permute-start | bytes 3981320 | tf_op jit(solution)/shard_map/ppermute | solution.py:272
  320.1 3.2 collective-permute-start.10
  327.0 33.5 %all-to-all-start.4 = ((bf16[4,64,2304]{2,1,0:T(8,128)(2,1)}), bf16[4,64,2304]{2,1,0:T(8,128)(2,1)}, u32[]{:S(2)}, u32[]{:S(2)}) async-start(bf16[4,64,2304]{2,1,0:T(8,128)(2,1)} %bitcast.292), calls=%async_computation.4 | async-start | bytes 2359296 | tf_op jit(solution)/shard_map/all_to_all | solution.py:381
  331.4 92.2 %all-gather.14.cloned.1.call-start = ((), (), s32[]{:S(2)}) async-start(), calls=%async_computation.21 | async-start | bytes 2654208 | tf_op jit(solution)/shard_map/all_gather | solution.py:264
  352.5 12.6 %collective-permute-start.11 = (bf16[256,2304]{1,0:T(8,128)(2,1)}, bf16[256,2304]{1,0:T(8,128)(2,1)}, u32[]{:S(2)}, u32[]{:S(2)}) collective-permute-start(bf16[256,2304]{1,0:T(8,128)(2,1)} %broadcast_select_fusion.2), channel_id=1, source_target_pairs={{0,4},{4,0},{1,5},{5,1},{2,6},{6,2},{3,7},{7,3},{8,12},{12,8},{9,1... | collective-permute-start | bytes 3538952 | tf_op jit(solution)/shard_map/ppermute | solution.py:272
  377.6 40.5 %all-to-all-start.5 = ((bf16[4,64,2304]{2,1,0:T(8,128)(2,1)}), bf16[4,64,2304]{2,1,0:T(8,128)(2,1)}, u32[]{:S(2)}, u32[]{:S(2)}) async-start(bf16[4,64,2304]{2,1,0:T(8,128)(2,1)} %bitcast.289), calls=%async_computation.5 | async-start | bytes 2359296 | tf_op jit(solution)/shard_map/all_to_all | solution.py:381
  381.9 72.0 %all-gather.16.cloned.1.call-start = ((), (), s32[]{:S(2)}) async-start(), calls=%async_computation.22 | async-start | bytes 2654208 | tf_op jit(solution)/shard_map/all_gather | solution.py:264
  423.3 133.5 %reduce-scatter.5.cloned.1.call-start = ((), (), s32[]{:S(2)}) async-start(), calls=%async_computation.23 | async-start | bytes 6635520 | tf_op jit(solution)/shard_map/reduce_scatter | solution.py:268
  465.4 33.6 %all-to-all-start.6 = ((bf16[4,64,2304]{2,1,0:T(8,128)(2,1)}), bf16[4,64,2304]{2,1,0:T(8,128)(2,1)}, u32[]{:S(2)}, u32[]{:S(2)}) async-start(bf16[4,64,2304]{2,1,0:T(8,128)(2,1)} %bitcast.290), calls=%async_computation.6 | async-start | bytes 2359296 | tf_op jit(solution)/shard_map/all_to_all | solution.py:381
  469.7 139.2 %reduce-scatter.7.cloned.1.call-start = ((), (), s32[]{:S(2)}) async-start(), calls=%async_computation.24 | async-start | bytes 6635520 | tf_op jit(solution)/shard_map/reduce_scatter | solution.py:268
  512.3 3.3 collective-permute-start.13
  519.3 33.6 %all-to-all-start.7 = ((bf16[4,64,2304]{2,1,0:T(8,128)(2,1)}), bf16[4,64,2304]{2,1,0:T(8,128)(2,1)}, u32[]{:S(2)}, u32[]{:S(2)}) async-start(bf16[4,64,2304]{2,1,0:T(8,128)(2,1)} %bitcast.291), calls=%async_computation.7 | async-start | bytes 2359296 | tf_op jit(solution)/shard_map/all_to_all | solution.py:381
  559.4 36.4 %all-to-all-start.8 = ((bf16[8,72,1152]{2,1,0:T(8,128)(2,1)}), bf16[8,72,1152]{2,1,0:T(8,128)(2,1)}, u32[]{:S(2)}, u32[]{:S(2)}) async-start(bf16[8,72,1152]{2,1,0:T(8,128)(2,1)} %bitcast.283), calls=%async_computation.9 | async-start | bytes 2654208 | tf_op jit(solution)/shard_map/all_to_all | solution.py:394
  563.7 117.8 %reduce-scatter.11.cloned.1.call-start = ((), (), s32[]{:S(2)}) async-start(), calls=%async_computation.26 | async-start | bytes 6635520 | tf_op jit(solution)/shard_map/reduce_scatter | solution.py:268
  566.3 9.7 %collective-permute-start.14 = (bf16[64,2304]{1,0:T(8,128)(2,1)}, bf16[64,2304]{1,0:T(8,128)(2,1)S(1)}, u32[]{:S(2)}, u32[]{:S(2)}) collective-permute-start(bf16[64,2304]{1,0:T(8,128)(2,1)} %get-tuple-element.133), channel_id=1, source_target_pairs={{0,8},{8,0},{1,9},{9,1},{2,10},{10,2},{3,11},{11,3},{4,12},{12,4},... | collective-permute-start | bytes 884744 | tf_op jit(solution)/shard_map/ppermute | solution.py:272
  567.8 11.4 %collective-permute-start.16 = (bf16[64,2304]{1,0:T(8,128)(2,1)}, bf16[64,2304]{1,0:T(8,128)(2,1)S(1)}, u32[]{:S(2)}, u32[]{:S(2)}) collective-permute-start(bf16[64,2304]{1,0:T(8,128)(2,1)} %get-tuple-element.132), channel_id=1, source_target_pairs={{0,16},{16,0},{1,17},{17,1},{2,18},{18,2},{3,19},{19,3},{4,20},{20... | collective-permute-start | bytes 884744 | tf_op jit(solution)/shard_map/ppermute | solution.py:272
  576.8 27.2 %collective-permute-start.15 = (bf16[2,64,2304]{2,1,0:T(8,128)(2,1)}, bf16[2,64,2304]{2,1,0:T(8,128)(2,1)}, u32[]{:S(2)}, u32[]{:S(2)}) collective-permute-start(bf16[2,64,2304]{2,1,0:T(8,128)(2,1)} %maximum_select_fusion.12), channel_id=1, source_target_pairs={{0,16},{16,0},{1,17},{17,1},{2,18},{18,2},{3,19},{19,3},{4,20},{20... | collective-permute-start | bytes 1769480 | tf_op jit(solution)/shard_map/ppermute | solution.py:272
  580.0 25.5 %collective-permute-start.17 = (bf16[2,64,2304]{2,1,0:T(8,128)(2,1)}, bf16[2,64,2304]{2,1,0:T(8,128)(2,1)}, u32[]{:S(2)}, u32[]{:S(2)}) collective-permute-start(bf16[2,64,2304]{2,1,0:T(8,128)(2,1)} %maximum_select_fusion.14), channel_id=1, source_target_pairs={{0,8},{8,0},{1,9},{9,1},{2,10},{10,2},{3,11},{11,3},{4,12},{12,4},... | collective-permute-start | bytes 1769480 | tf_op jit(solution)/shard_map/ppermute | solution.py:272
  608.8 7.6 collective-permute-start.18
  608.9 37.1 %all-to-all-start.9 = ((bf16[8,72,1152]{2,1,0:T(8,128)(2,1)}), bf16[8,72,1152]{2,1,0:T(8,128)(2,1)}, u32[]{:S(2)}, u32[]{:S(2)}) async-start(bf16[8,72,1152]{2,1,0:T(8,128)(2,1)} %bitcast.307), calls=%async_computation.11 | async-start | bytes 2654208 | tf_op jit(solution)/shard_map/all_to_all | solution.py:394
  632.6 23.8 %collective-permute-start.19 = (f32[1024,256]{1,0:T(8,128)}, f32[1024,256]{1,0:T(8,128)S(1)}, u32[]{:S(2)}, u32[]{:S(2)}) collective-permute-start(f32[1024,256]{1,0:T(8,128)} %get-tuple-element.50), channel_id=1, source_target_pairs={{0,4},{4,0},{1,5},{5,1},{2,6},{6,2},{3,7},{7,3},{8,12},{12,8},{9,1... | collective-permute-start | bytes 3145736 | tf_op jit(solution)/shard_map/ppermute | solution.py:272
  652.6 31.5 %all-to-all-start.11 = ((bf16[32,72,256]{2,1,0:T(8,128)(2,1)}), bf16[32,72,256]{2,1,0:T(8,128)(2,1)}, u32[]{:S(2)}, u32[]{:S(2)}) async-start(bf16[32,72,256]{2,1,0:T(8,128)(2,1)} %bitcast.309), calls=%async_computation.14 | async-start | bytes 2359296 | tf_op jit(solution)/shard_map/all_to_all | solution.py:620
  656.1 104.9 %reduce-scatter.9.cloned.1.call-start = ((), (), s32[]{:S(2)}) async-start(), calls=%async_computation.25 | async-start | bytes 2949120 | tf_op jit(solution)/shard_map/reduce_scatter | solution.py:268
  667.6 23.2 %collective-permute-start.20 = (bf16[4,128,2304]{2,1,0:T(8,128)(2,1)}, bf16[4,128,2304]{2,1,0:T(8,128)(2,1)}, u32[]{:S(2)}, u32[]{:S(2)}) collective-permute-start(bf16[4,128,2304]{2,1,0:T(8,128)(2,1)} %select_bitcast_fusion), channel_id=1, source_target_pairs={{0,4},{4,0},{1,5},{5,1},{2,6},{6,2},{3,7},{7,3},{8,12},{12,8},{9,1... | collective-permute-start | bytes 7077896 | tf_op jit(solution)/shard_map/ppermute | solution.py:272
  684.1 70.6 %all-to-all-start.12 = ((bf16[8,72,1152]{2,1,0:T(8,128)(2,1)}), bf16[8,72,1152]{2,1,0:T(8,128)(2,1)S(1)}, u32[]{:S(2)}, u32[]{:S(2)}) async-start(bf16[8,72,1152]{2,1,0:T(8,128)(2,1)} %bitcast.104), calls=%async_computation.16 | async-start | bytes 2654208 | tf_op jit(solution)/shard_map/all_to_all | solution.py:394
  695.0 9.5 %collective-permute-start.21 = (bf16[64,2304]{1,0:T(8,128)(2,1)S(1)}, bf16[64,2304]{1,0:T(8,128)(2,1)S(1)}, u32[]{:S(2)}, u32[]{:S(2)}) collective-permute-start(bf16[64,2304]{1,0:T(8,128)(2,1)S(1)} %get-tuple-element.93), channel_id=1, source_target_pairs={{0,8},{8,0},{1,9},{9,1},{2,10},{10,2},{3,11},{11,3},{4,12},{12,4},... | collective-permute-start | bytes 884744 | tf_op jit(solution)/shard_map/ppermute | solution.py:272
  695.8 9.1 %collective-permute-start.23 = (bf16[64,2304]{1,0:T(8,128)(2,1)S(1)}, bf16[64,2304]{1,0:T(8,128)(2,1)S(1)}, u32[]{:S(2)}, u32[]{:S(2)}) collective-permute-start(bf16[64,2304]{1,0:T(8,128)(2,1)S(1)} %get-tuple-element.94), channel_id=1, source_target_pairs={{0,16},{16,0},{1,17},{17,1},{2,18},{18,2},{3,19},{19,3},{4,20},{20... | collective-permute-start | bytes 884744 | tf_op jit(solution)/shard_map/ppermute | solution.py:272
  705.9 50.7 %collective-permute-start.24 = (bf16[128,2304]{1,0:T(8,128)(2,1)}, bf16[128,2304]{1,0:T(8,128)(2,1)S(1)}, u32[]{:S(2)}, u32[]{:S(2)}) collective-permute-start(bf16[128,2304]{1,0:T(8,128)(2,1)} %pad_maximum_fusion.12), channel_id=1, source_target_pairs={{0,8},{8,0},{1,9},{9,1},{2,10},{10,2},{3,11},{11,3},{4,12},{12,4},... | collective-permute-start | bytes 1769480 | tf_op jit(solution)/shard_map/ppermute | solution.py:272
  708.2 48.4 %collective-permute-start.22 = (bf16[128,2304]{1,0:T(8,128)(2,1)}, bf16[128,2304]{1,0:T(8,128)(2,1)S(1)}, u32[]{:S(2)}, u32[]{:S(2)}) collective-permute-start(bf16[128,2304]{1,0:T(8,128)(2,1)} %pad_maximum_fusion.11), channel_id=1, source_target_pairs={{0,16},{16,0},{1,17},{17,1},{2,18},{18,2},{3,19},{19,3},{4,20},{20... | collective-permute-start | bytes 1769480 | tf_op jit(solution)/shard_map/ppermute | solution.py:272
  762.8 18.2 %all-to-all-start.10 = ((bf16[8,72,512]{2,1,0:T(8,128)(2,1)}), bf16[8,72,512]{2,1,0:T(8,128)(2,1)S(1)}, u32[]{:S(2)}, u32[]{:S(2)}) async-start(bf16[8,72,512]{2,1,0:T(8,128)(2,1)} %bitcast.322), calls=%async_computation.13 | async-start | bytes 1179648 | tf_op jit(solution)/shard_map/all_to_all | solution.py:394
  783.7 10.8 %all-to-all-start.13 = ((f32[32,4,72]{2,1,0:T(4,128)}), f32[32,4,72]{2,1,0:T(4,128)S(1)}, u32[]{:S(2)}, u32[]{:S(2)}) async-start(f32[32,4,72]{2,1,0:T(4,128)} %fusion.95), calls=%async_computation.17 | async-start | bytes 131072 | tf_op jit(solution)/shard_map/all_to_all | solution.py:638
  (104 other events, 1023.6 us)
Sparse Core Ops, SparseCore 0:
  9.9 41.6 all-gather.17
  90.1 144.6 all-gather.7
  251.7 31.6 all-gather.9
  285.4 30.7 all-gather.11
  364.6 39.8 all-gather.13
  423.4 30.4 all-gather.15
  465.5 61.1 reduce-scatter.4
  530.3 74.3 reduce-scatter.6
  608.2 73.2 reduce-scatter.10
  683.7 72.9 reduce-scatter.8
